TPU v7x, 32 devices: a whole 2x2x4 slice. The times are simulated.
32 devices in a mesh: pipe: 2 (over core), dp: 4 (over z), tensor: 4 (over y, x).
Axes of the slice: x: 2, y: 2, z: 4, core: 2. Of those that a mesh axis runs over, the one named last changes fastest.
Arguments:
- boundary: bfloat16 [2, 8, 128, 512], P('pipe', 'dp', 'tensor'), may hold values from -10 to 10
- lengths: int32 [8], P('dp'), may hold values from 32 to 128, as said below
- batch_of: int32 [8], P('dp'), may hold values from 0 to 1, as said below
- mats: bfloat16 [2, 8, 512, 512], P('pipe', None, 'dp', 'tensor'), may hold values from -0.25 to 0.25
- ffw: bfloat16 [2, 4, 512, 2048], P('pipe', None, 'dp', 'tensor'), may hold values from -0.25 to 0.25
- vec_model: bfloat16 [2, 14, 512], P('pipe', None, ('dp', 'tensor')), may hold values from -1 to 1
- vec_inner: bfloat16 [2, 39, 512], P('pipe', None, ('tensor', 'dp')), may hold values from -1 to 1
- vec_ff: bfloat16 [2, 2, 2048], P('pipe', None, ('tensor', 'dp')), may hold values from -1 to 1
Outputs:
- boundary_out: bfloat16 [2, 8, 128, 512], P('pipe', 'dp', 'tensor')
- mats_grad: float32 [2, 8, 512, 512], P('pipe', None, 'dp', 'tensor')
- ffw_grad: float32 [2, 4, 512, 2048], P('pipe', None, 'dp', 'tensor')
- vec_model_grad: float32 [2, 14, 512], P('pipe', None, ('dp', 'tensor'))
- vec_inner_grad: float32 [2, 39, 512], P('pipe', None, ('tensor', 'dp'))
- vec_ff_grad: float32 [2, 2, 2048], P('pipe', None, ('tensor', 'dp'))
Inputs may be any that keep to these rules, and one draw needn't show every extreme that they name: `lengths`: some sequence has exactly 128 tokens and some exactly 32. `batch_of`: in each aligned block of 2 sequences (the sequences of one device) every micro-batch number stands exactly once.
All inputs are finite; a program needn't handle non-finite values.
Results may differ from a plain program's by a relative error of at most 0.03.
Values may be sent and summed in bfloat16 or wider, within the bound.
No kernel may reach another device: no remote copies, remote signals or barrier semaphores. Data moves between devices by JAX's collectives and lax.ppermute only.
A program may use at most 128 MiB of HBM per device.

v0:
```python
import jax
import jax.numpy as jnp
from jax import lax
from jax.sharding import PartitionSpec as P

HEAD_DIM = 64
MB = 2


EPSILON = 1e-05
HUGE_NEG = -1000000000.0


def passed_along(value, axis, steps):
    count = lax.axis_size(axis)
    initial, last = (max(0, -steps), min(count, count - steps))
    return lax.ppermute(value, axis, [(source, source + steps) for source in range(initial, last)])


def layer_norm(stream, gain, shift):
    centre = stream - jnp.mean(stream, axis=-1, keepdims=True)
    spread = jnp.mean(centre * centre, axis=-1, keepdims=True)
    return centre * lax.rsqrt(spread + EPSILON) * (1.0 + gain) + shift


def sinusoid(length, width):
    place = (length - 1 - jnp.arange(2 * length - 1)).astype(jnp.float32)
    index = jnp.arange(width // 2).astype(jnp.float32)
    rate = jnp.exp(index * (-2.0 * jnp.log(10000.0) / width))
    angle = place[:, None] * rate[None, :]
    return jnp.stack([jnp.sin(angle), jnp.cos(angle)], axis=-1).reshape(2 * length - 1, width)


def rel_shift(table):
    head_count, length, span = table.shape
    padded = jnp.pad(table, ((0, 0), (0, 0), (1, 0)))
    padded = padded.reshape(head_count, span + 1, length)[:, 1:]
    return padded.reshape(head_count, length, span)[:, :, :length]


def depthwise(mixed, taps):
    size = taps.shape[0]
    channels = mixed.shape[1]
    filtered = lax.conv_general_dilated(
        mixed[None],
        taps[:, None, :],
        (1,),
        [(size // 2, size // 2)],
        dimension_numbers=("NWC", "WIO", "NWC"),
        feature_group_count=channels,
        precision=lax.Precision.HIGHEST,
    )
    return filtered[0]


def gated_unit(first_half, second_half, key_mask):
    return first_half * jax.nn.sigmoid(second_half) * key_mask[:, None]


def contract(left_side, right_side, left_dim, right_dim):
    return lax.dot_general(
        left_side,
        right_side,
        (((left_dim,), (right_dim,)), ((), ())),
        preferred_element_type=jnp.float32,
    )


def rows_full(shard_rows):
    return lax.all_gather(shard_rows, "tensor", axis=0, tiled=True)


def rows_summed(partial_rows):
    return lax.psum_scatter(
        partial_rows.astype(jnp.bfloat16), "tensor", scatter_dimension=0, tiled=True
    ).astype(jnp.float32)


def grads_full(shard_rows):
    return lax.all_gather(shard_rows, "tensor", axis=0, tiled=True)


def grads_summed(partial_rows):
    return lax.psum_scatter(
        partial_rows.astype(jnp.bfloat16), "tensor", scatter_dimension=0, tiled=True
    ).astype(jnp.float32)


def fetch_weights(mats, ffw, vec_model, vec_inner, vec_ff):
    matrices, ff_mats, inner_vec, hidden_vec = (
        lax.all_gather(mats[0], "dp", axis=1, tiled=True),
        lax.all_gather(ffw[0], "dp", axis=1, tiled=True),
        lax.all_gather(vec_inner[0], "dp", axis=1, tiled=True),
        lax.all_gather(vec_ff[0], "dp", axis=1, tiled=True),
    )
    model_vec = lax.all_gather(vec_model[0], ("dp", "tensor"), axis=1, tiled=True)
    return (
        matrices,
        ff_mats,
        model_vec.astype(jnp.float32),
        inner_vec.astype(jnp.float32),
        hidden_vec.astype(jnp.float32),
    )


def spread_grads(grads):
    matrices, ff_mats, model_vec, inner_vec, hidden_vec = grads
    matrices, ff_mats, inner_vec, hidden_vec = (
        lax.psum_scatter(
            matrices.astype(jnp.bfloat16), "dp", scatter_dimension=1, tiled=True
        ).astype(jnp.float32),
        lax.psum_scatter(
            ff_mats.astype(jnp.bfloat16), "dp", scatter_dimension=1, tiled=True
        ).astype(jnp.float32),
        lax.psum_scatter(
            inner_vec.astype(jnp.bfloat16), "dp", scatter_dimension=1, tiled=True
        ).astype(jnp.float32),
        lax.psum_scatter(
            hidden_vec.astype(jnp.bfloat16), "dp", scatter_dimension=1, tiled=True
        ).astype(jnp.float32),
    )
    model_vec = lax.psum_scatter(model_vec, ("dp", "tensor"), scatter_dimension=1, tiled=True)
    return (matrices, ff_mats, model_vec, inner_vec, hidden_vec)


def scale_tree(tree, live_flag):
    return jax.tree.map(lambda grad_piece: live_flag * grad_piece, tree)


def add_trees(totals, addend):
    return jax.tree.map(lambda total_piece, grad_piece: total_piece + grad_piece, totals, addend)


def pos_weight(pos_table, d_pos):
    flat = d_pos.reshape(d_pos.shape[0], -1)
    upper = flat.astype(jnp.bfloat16)
    lower = (flat - upper.astype(jnp.float32)).astype(jnp.bfloat16)
    return contract(pos_table, upper, 0, 0) + contract(pos_table, lower, 0, 0)


def ff_forward(stream, weights, which, first_row):
    matrices, ff_mats, model_vec, inner_vec, hidden_vec = weights
    normed = rows_full(
        layer_norm(stream, model_vec[first_row], model_vec[first_row + 1]).astype(jnp.bfloat16)
    )
    before = (
        jnp.dot(normed, ff_mats[2 * which], preferred_element_type=jnp.float32) + hidden_vec[which]
    )
    active = jax.nn.silu(before).astype(jnp.bfloat16)
    branch = rows_summed(contract(active, ff_mats[2 * which + 1], 1, 1)) + model_vec[first_row + 2]
    return (stream + 0.5 * branch, (stream, normed, before, active))


def ff_backward(grad_rows, kept, weights, which, first_row):
    matrices, ff_mats, model_vec, inner_vec, hidden_vec = weights
    stream, normed, before, active = kept
    delta_rows = (0.5 * grad_rows).astype(jnp.bfloat16)
    bias_out = jnp.sum(delta_rows, axis=0, dtype=jnp.float32)
    delta_full = grads_full(delta_rows)
    weight_out = contract(delta_full, active, 0, 0)
    d_active = jnp.dot(delta_full, ff_mats[2 * which + 1], preferred_element_type=jnp.float32)
    unused_value, silu_back = jax.vjp(jax.nn.silu, before)
    d_before = silu_back(d_active)[0].astype(jnp.bfloat16)
    bias_in = jnp.sum(d_before, axis=0, dtype=jnp.float32)
    weight_in = contract(normed, d_before, 0, 0)
    d_normed = grads_summed(contract(d_before, ff_mats[2 * which], 1, 1))
    unused_norm, norm_back = jax.vjp(
        layer_norm, stream, model_vec[first_row], model_vec[first_row + 1]
    )
    d_stream, d_gain, d_shift = norm_back(d_normed)
    return (grad_rows + d_stream, (weight_in, weight_out, bias_in, (d_gain, d_shift, bias_out)))


def attn_scores(query_u, query_v, key_rows, rel_pos, key_mask):
    direct = jnp.einsum("ihd,jhd->hij", query_u, key_rows, preferred_element_type=jnp.float32)
    relative = rel_shift(
        jnp.einsum("ihd,rhd->hir", query_v, rel_pos, preferred_element_type=jnp.float32)
    )
    scores = (direct + relative) * HEAD_DIM ** (-0.5)
    return jnp.where(key_mask[None, None, :] > 0.5, scores, HUGE_NEG)


def attn_forward(stream, key_mask, weights, rel_pos):
    matrices, ff_mats, model_vec, inner_vec, hidden_vec = weights
    normed = rows_full(layer_norm(stream, model_vec[3], model_vec[4]).astype(jnp.bfloat16))
    length = normed.shape[0]
    head_count = matrices.shape[2] // HEAD_DIM
    split_shape = (length, head_count, HEAD_DIM)
    query_rows = jnp.dot(normed, matrices[0], preferred_element_type=jnp.float32) + inner_vec[0]
    query_u = (query_rows + inner_vec[2]).astype(jnp.bfloat16).reshape(split_shape)
    query_v = (query_rows + inner_vec[3]).astype(jnp.bfloat16).reshape(split_shape)
    key_rows = (
        jnp.dot(normed, matrices[1], preferred_element_type=jnp.float32)
        .astype(jnp.bfloat16)
        .reshape(split_shape)
    )
    value_rows = (
        (jnp.dot(normed, matrices[2], preferred_element_type=jnp.float32) + inner_vec[1])
        .astype(jnp.bfloat16)
        .reshape(split_shape)
    )
    scores = attn_scores(query_u, query_v, key_rows, rel_pos, key_mask)
    row_top = jnp.max(scores, axis=-1, keepdims=True)
    exp_terms = jnp.exp(scores - row_top)
    row_total = jnp.sum(exp_terms, axis=-1, keepdims=True)
    attn_probs = (exp_terms / row_total).astype(jnp.bfloat16)
    context = jnp.einsum("hij,jhd->ihd", attn_probs, value_rows, preferred_element_type=jnp.float32)
    context = context.reshape(length, head_count * HEAD_DIM).astype(jnp.bfloat16)
    branch = rows_summed(contract(context, matrices[3], 1, 1)) + model_vec[5]
    norm_log = row_top + jnp.log(row_total)
    return (
        stream + branch,
        (stream, normed, query_u, query_v, key_rows, value_rows, norm_log, context),
    )


def attn_backward(grad_rows, kept, key_mask, weights, rel_pos):
    matrices, ff_mats, model_vec, inner_vec, hidden_vec = weights
    stream, normed, query_u, query_v, key_rows, value_rows, norm_log, context = kept
    length, head_count = (query_u.shape[0], query_u.shape[1])
    delta_rows = grad_rows.astype(jnp.bfloat16)
    bias_out = jnp.sum(delta_rows, axis=0, dtype=jnp.float32)
    delta_full = grads_full(delta_rows)
    weight_out = contract(delta_full, context, 0, 0)
    d_context = jnp.dot(delta_full, matrices[3], preferred_element_type=jnp.float32).astype(
        jnp.bfloat16
    )
    d_context = d_context.reshape(length, head_count, HEAD_DIM)
    attn_probs = jnp.exp(attn_scores(query_u, query_v, key_rows, rel_pos, key_mask) - norm_log)
    d_values = jnp.einsum(
        "hij,ihd->jhd",
        attn_probs.astype(jnp.bfloat16),
        d_context,
        preferred_element_type=jnp.float32,
    )
    d_values = d_values.reshape(length, -1).astype(jnp.bfloat16)
    d_probs = jnp.einsum("ihd,jhd->hij", d_context, value_rows, preferred_element_type=jnp.float32)
    d_scores = attn_probs * (d_probs - jnp.sum(attn_probs * d_probs, axis=-1, keepdims=True))
    d_scores = d_scores.astype(jnp.bfloat16) * jnp.asarray(HEAD_DIM ** (-0.5), jnp.bfloat16)
    d_query_u = jnp.einsum("hij,jhd->ihd", d_scores, key_rows, preferred_element_type=jnp.float32)
    d_keys = jnp.einsum("hij,ihd->jhd", d_scores, query_u, preferred_element_type=jnp.float32)
    d_keys = d_keys.reshape(length, -1).astype(jnp.bfloat16)
    unused_shift, shift_back = jax.vjp(
        rel_shift, jnp.zeros((head_count, length, rel_pos.shape[0]), jnp.bfloat16)
    )
    d_relative = shift_back(d_scores)[0]
    d_query_v = jnp.einsum("hir,rhd->ihd", d_relative, rel_pos, preferred_element_type=jnp.float32)
    d_pos = jnp.einsum("hir,ihd->rhd", d_relative, query_v, preferred_element_type=jnp.float32)
    d_query = (d_query_u + d_query_v).reshape(length, -1).astype(jnp.bfloat16)
    bias_query = jnp.sum(d_query, axis=0, dtype=jnp.float32)
    bias_value = jnp.sum(d_values, axis=0, dtype=jnp.float32)
    bias_u = jnp.sum(d_query_u, axis=0).reshape(-1)
    bias_v = jnp.sum(d_query_v, axis=0).reshape(-1)
    weight_query = contract(normed, d_query, 0, 0)
    weight_key = contract(normed, d_keys, 0, 0)
    weight_value = contract(normed, d_values, 0, 0)
    d_normed = grads_summed(
        contract(d_query, matrices[0], 1, 1)
        + contract(d_keys, matrices[1], 1, 1)
        + contract(d_values, matrices[2], 1, 1)
    )
    unused_norm, norm_back = jax.vjp(layer_norm, stream, model_vec[3], model_vec[4])
    d_stream, d_gain, d_shift = norm_back(d_normed)
    parts = (
        (weight_query, weight_key, weight_value, weight_out),
        (bias_query, bias_value, bias_u, bias_v),
        (d_gain, d_shift, bias_out),
    )
    return (grad_rows + d_stream, parts, d_pos)


def conv_forward(stream, key_mask, weights):
    matrices, ff_mats, model_vec, inner_vec, hidden_vec = weights
    normed = rows_full(layer_norm(stream, model_vec[6], model_vec[7]).astype(jnp.bfloat16))
    gate_in = jnp.dot(normed, matrices[5], preferred_element_type=jnp.float32) + inner_vec[4]
    gate_sig = jnp.dot(normed, matrices[6], preferred_element_type=jnp.float32) + inner_vec[5]
    mixed = gated_unit(gate_in, gate_sig, key_mask)
    filtered = depthwise(mixed, inner_vec[8:])
    inside = key_mask[:, None]
    local_sum = jnp.sum(inside * filtered, axis=0)
    local_count = jnp.sum(key_mask)
    chan_total, token_count = lax.psum((local_sum, local_count), "dp")
    chan_mean = chan_total / token_count
    centre = filtered - chan_mean
    spread = lax.psum(jnp.sum(inside * centre * centre, axis=0), "dp") / token_count
    inv_spread = lax.rsqrt(spread + EPSILON)
    normal_in = (filtered - chan_mean) * inv_spread
    normal = normal_in * (1.0 + inner_vec[6]) + inner_vec[7]
    active = jax.nn.silu(normal).astype(jnp.bfloat16)
    branch = rows_summed(contract(active, matrices[7], 1, 1)) + model_vec[8]
    return (
        stream + branch,
        (
            stream,
            normed,
            gate_in,
            gate_sig,
            mixed,
            normal_in,
            inv_spread,
            token_count,
            normal,
            active,
        ),
    )


def conv_backward(grad_rows, kept, key_mask, weights):
    matrices, ff_mats, model_vec, inner_vec, hidden_vec = weights
    stream, normed, gate_in, gate_sig, mixed, normal_in, inv_spread, token_count, normal, active = (
        kept
    )
    delta_rows = grad_rows.astype(jnp.bfloat16)
    bias_out = jnp.sum(delta_rows, axis=0, dtype=jnp.float32)
    delta_full = grads_full(delta_rows)
    weight_out = contract(delta_full, active, 0, 0)
    d_active = jnp.dot(delta_full, matrices[7], preferred_element_type=jnp.float32)
    unused_value, silu_back = jax.vjp(jax.nn.silu, normal)
    d_normal = silu_back(d_active)[0]
    norm_gain = jnp.sum(d_normal * normal_in, axis=0)
    norm_shift = jnp.sum(d_normal, axis=0)
    d_hat = d_normal * (1.0 + inner_vec[6])
    plain_sum, tilted_sum = lax.psum(
        (jnp.sum(d_hat, axis=0), jnp.sum(d_hat * normal_in, axis=0)), "dp"
    )
    d_filtered = inv_spread * (
        d_hat - key_mask[:, None] / token_count * (plain_sum + normal_in * tilted_sum)
    )
    unused_conv, conv_back = jax.vjp(depthwise, mixed, inner_vec[8:])
    d_mixed, d_taps = conv_back(d_filtered)
    unused_gate, gate_back = jax.vjp(
        lambda first_half, second_half: gated_unit(first_half, second_half, key_mask),
        gate_in,
        gate_sig,
    )
    d_gate_in, d_gate_sig = gate_back(d_mixed)
    d_gate_in = d_gate_in.astype(jnp.bfloat16)
    d_gate_sig = d_gate_sig.astype(jnp.bfloat16)
    bias_in = jnp.sum(d_gate_in, axis=0, dtype=jnp.float32)
    bias_sig = jnp.sum(d_gate_sig, axis=0, dtype=jnp.float32)
    weight_in = contract(normed, d_gate_in, 0, 0)
    weight_sig = contract(normed, d_gate_sig, 0, 0)
    d_normed = grads_summed(
        contract(d_gate_in, matrices[5], 1, 1) + contract(d_gate_sig, matrices[6], 1, 1)
    )
    unused_norm, norm_back = jax.vjp(layer_norm, stream, model_vec[6], model_vec[7])
    d_stream, d_gain, d_shift = norm_back(d_normed)
    parts = (
        (weight_in, weight_sig, weight_out),
        (bias_in, bias_sig, norm_gain, norm_shift),
        d_taps,
        (d_gain, d_shift, bias_out),
    )
    return (grad_rows + d_stream, parts)


def layer_forward(stream, key_mask, weights, rel_pos):
    model_vec = weights[2]
    stream, ff_first = ff_forward(stream, weights, 0, 0)
    stream, attn_kept = attn_forward(stream, key_mask, weights, rel_pos)
    stream, conv_kept = conv_forward(stream, key_mask, weights)
    stream, ff_second = ff_forward(stream, weights, 1, 9)
    return (
        layer_norm(stream, model_vec[12], model_vec[13]),
        (ff_first, attn_kept, conv_kept, ff_second, stream),
    )


def layer_backward(grad_rows, kept, key_mask, weights, rel_pos):
    ff_first, attn_kept, conv_kept, ff_second, last_stream = kept
    model_vec = weights[2]
    unused_norm, final_back = jax.vjp(layer_norm, last_stream, model_vec[12], model_vec[13])
    grad_rows, last_gain, last_shift = final_back(grad_rows)
    grad_rows, second_parts = ff_backward(grad_rows, ff_second, weights, 1, 9)
    grad_rows, conv_parts = conv_backward(grad_rows, conv_kept, key_mask, weights)
    grad_rows, attn_parts, d_pos = attn_backward(grad_rows, attn_kept, key_mask, weights, rel_pos)
    grad_rows, first_parts = ff_backward(grad_rows, ff_first, weights, 0, 0)
    attn_mats, attn_inner, attn_model = attn_parts
    conv_mats, conv_inner, conv_taps, conv_model = conv_parts
    matrices_g = jnp.stack(
        [
            attn_mats[0],
            attn_mats[1],
            attn_mats[2],
            attn_mats[3],
            jnp.zeros_like(attn_mats[0]),
            conv_mats[0],
            conv_mats[1],
            conv_mats[2],
        ]
    )
    ff_g = jnp.stack([first_parts[0], first_parts[1], second_parts[0], second_parts[1]])
    model_g = jnp.stack(
        list(first_parts[3])
        + list(attn_model)
        + list(conv_model)
        + list(second_parts[3])
        + [last_gain, last_shift]
    )
    inner_g = jnp.concatenate([jnp.stack(list(attn_inner) + list(conv_inner)), conv_taps], axis=0)
    hidden_g = jnp.stack([first_parts[2], second_parts[2]])
    return (grad_rows, (matrices_g, ff_g, model_g, inner_g, hidden_g), d_pos)


def select_rows(ends, lengths, slot_of, micro_idx, full_length):
    seq_slot = lax.dynamic_index_in_dim(slot_of, micro_idx, 0, keepdims=False)
    own_rows = lax.dynamic_index_in_dim(ends, seq_slot, 0, keepdims=False)
    live_count = lax.dynamic_index_in_dim(lengths, seq_slot, 0, keepdims=False)
    return (own_rows, (jnp.arange(full_length) < live_count).astype(jnp.float32))


def per_device(boundary, lengths, batch_of, mats, ffw, vec_model, vec_inner, vec_ff):
    ends = boundary[0]
    rows_here = ends.shape[1]
    model_width = ends.shape[2]
    full_length = rows_here * lax.axis_size("tensor")
    section_idx = lax.axis_index("pipe")
    at_first = section_idx == 0
    slot_of = jnp.stack(
        [
            jnp.sum(jnp.arange(MB, dtype=jnp.int32) * (batch_of == micro_idx).astype(jnp.int32))
            for micro_idx in range(MB)
        ]
    )
    pos_table = sinusoid(full_length, model_width).astype(jnp.bfloat16)
    held = fetch_weights(mats, ffw, vec_model, vec_inner, vec_ff)
    incoming = jnp.zeros((rows_here, model_width), jnp.bfloat16)
    kept_steps = []
    made_rows = []
    rel_pos = None
    for fwd_step in range(MB + 1):
        weights = held
        if fwd_step == 0:
            matrices = weights[0]
            rel_pos = jnp.dot(pos_table, matrices[4], preferred_element_type=jnp.float32).astype(
                jnp.bfloat16
            )
            rel_pos = rel_pos.reshape(2 * full_length - 1, matrices.shape[2] // HEAD_DIM, HEAD_DIM)
        micro_idx = jnp.clip(fwd_step - section_idx, 0, MB - 1)
        own_rows, key_mask = select_rows(ends, lengths, slot_of, micro_idx, full_length)
        stream = jnp.where(at_first, own_rows, incoming).astype(jnp.float32)
        result, kept = layer_forward(stream, key_mask, weights, rel_pos)
        sent = result.astype(jnp.bfloat16)
        made_rows.append(sent)
        kept_steps.append((kept, key_mask))
        if fwd_step < MB:
            incoming = passed_along(sent, "pipe", 1)
    returning = jnp.zeros((rows_here, model_width), jnp.bfloat16)
    back_rows = []
    totals = None
    pos_total = None
    for bwd_step in range(MB + 1):
        fwd_step = MB - bwd_step
        weights = held
        micro_idx = jnp.clip(fwd_step - section_idx, 0, MB - 1)
        own_rows, unused_mask = select_rows(ends, lengths, slot_of, micro_idx, full_length)
        kept, key_mask = kept_steps[fwd_step]
        live_flag = ((fwd_step - section_idx >= 0) & (fwd_step - section_idx < MB)).astype(
            jnp.float32
        )
        stream_grad = jnp.where(at_first, returning, own_rows).astype(jnp.float32)
        d_stream, tick_grads, d_pos = layer_backward(stream_grad, kept, key_mask, weights, rel_pos)
        sent = d_stream.astype(jnp.bfloat16)
        back_rows.append(sent)
        scaled = scale_tree(tick_grads, live_flag)
        totals = scaled if totals is None else add_trees(totals, scaled)
        pos_total = live_flag * d_pos if pos_total is None else pos_total + live_flag * d_pos
        if bwd_step < MB:
            returning = passed_along(sent, "pipe", -1)
    shards = spread_grads(
        (totals[0].at[4].set(pos_weight(pos_table, pos_total)),) + tuple(totals[1:])
    )
    made_stack = jnp.stack(made_rows)
    back_stack = jnp.stack(back_rows)
    pieces = []
    for seq_slot in range(MB):
        micro_idx = batch_of[seq_slot]
        forward_out = lax.dynamic_index_in_dim(made_stack, micro_idx + 1, 0, keepdims=False)
        backward_out = lax.dynamic_index_in_dim(back_stack, MB - micro_idx, 0, keepdims=False)
        pieces.append(jnp.where(at_first, backward_out, forward_out))
    ends_out = jnp.stack(pieces)[None]
    return (ends_out,) + tuple((shard_piece[None] for shard_piece in shards))


def solution(mesh):
    return jax.shard_map(
        per_device,
        mesh=mesh,
        in_specs=(
            P("pipe", "dp", "tensor", None),
            P("dp"),
            P("dp"),
            P("pipe", None, "dp", "tensor"),
            P("pipe", None, "dp", "tensor"),
            P("pipe", None, ("dp", "tensor")),
            P("pipe", None, ("tensor", "dp")),
            P("pipe", None, ("tensor", "dp")),
        ),
        out_specs=(
            P("pipe", "dp", "tensor", None),
            P("pipe", None, "dp", "tensor"),
            P("pipe", None, "dp", "tensor"),
            P("pipe", None, ("dp", "tensor")),
            P("pipe", None, ("tensor", "dp")),
            P("pipe", None, ("tensor", "dp")),
        ),
        check_vma=False,
    )
```

profile of v0, /device:TPU:1, one launch (start us, length us, event | category | flops | bytes accessed | tf_op | source)
XLA Modules:
  0.0 1514.1 jit_solution(14603496412028425596)
XLA Ops:
  16.6 39.3 %all-gather = bf16[1,14,512]{1,0,2:T(2,128)(2,1)S(1)} all-gather(bf16[1,14,32]{1,0,2:T(2,128)(2,1)S(1)} %copy.196), channel_id=2, replica_groups=mesh['pipe'=2,'dp'=4,'tensor'=4] {'dp','tensor'}, dimensions={2}, use_global_device_ids=true | all-gather | bytes 15232 | tf_op jit(solution)/shard_map/all_gather | solution.py:96
  56.2 28.0 %fusion.91 = (f32[512]{0:T(512)S(1)}, f32[512]{0:T(512)}, f32[512]{0:T(512)}, f32[512]{0:T(512)S(1)}, f32[512]{0:T(512)}, /*index=5*/f32[512]{0:T(512)}, f32[512...) fusion(f32[1,14,512]{1,0,2:T(1,128)S(1)} %convert_element_type.979), kind=kLoop, calls=%fused_computation.249 | loop fusion | flops 2560 | bytes 57344 | tf_op jit(solution)/shard_map/jvp()/add | solution.py:23
  125.6 33.0 %reduce-scatter.36.cloned.1.call-done = bf16[32,512]{1,0:T(8,128)(2,1)} async-done(((bf16[128,512]{1,0:T(8,128)(2,1)}), bf16[32,512]{1,0:T(8,128)(2,1)}) %reduce-scatter.36.cloned.1.call-update) | async-done | bytes 32784 | tf_op jit(solution)/shard_map/reduce_scatter | solution.py:74
  177.2 22.8 %reduce-scatter.38.cloned.1.call-done = bf16[32,512]{1,0:T(8,128)(2,1)} async-done(((bf16[128,512]{1,0:T(8,128)(2,1)}), bf16[32,512]{1,0:T(8,128)(2,1)}) %reduce-scatter.38.cloned.1.call-update) | async-done | bytes 32784 | tf_op jit(solution)/shard_map/reduce_scatter | solution.py:74
  237.3 28.5 %reduce-scatter.40.cloned.1.call-done = bf16[32,512]{1,0:T(8,128)(2,1)} async-done(((bf16[128,512]{1,0:T(8,128)(2,1)}), bf16[32,512]{1,0:T(8,128)(2,1)}) %reduce-scatter.40.cloned.1.call-update) | async-done | bytes 32784 | tf_op jit(solution)/shard_map/reduce_scatter | solution.py:74
  277.9 26.1 %reduce-scatter.42.cloned.1.call-done = bf16[32,512]{1,0:T(8,128)(2,1)} async-done(((bf16[128,512]{1,0:T(8,128)(2,1)}), bf16[32,512]{1,0:T(8,128)(2,1)}) %reduce-scatter.42.cloned.1.call-update) | async-done | bytes 32784 | tf_op jit(solution)/shard_map/reduce_scatter | solution.py:74
  322.1 23.9 %reduce-scatter.44.cloned.1.call-done = bf16[32,512]{1,0:T(8,128)(2,1)} async-done(((bf16[128,512]{1,0:T(8,128)(2,1)}), bf16[32,512]{1,0:T(8,128)(2,1)}) %reduce-scatter.44.cloned.1.call-update) | async-done | bytes 32784 | tf_op jit(solution)/shard_map/reduce_scatter | solution.py:74
  373.4 25.0 %reduce-scatter.46.cloned.1.call-done = bf16[32,512]{1,0:T(8,128)(2,1)} async-done(((bf16[128,512]{1,0:T(8,128)(2,1)}), bf16[32,512]{1,0:T(8,128)(2,1)}) %reduce-scatter.46.cloned.1.call-update) | async-done | bytes 32784 | tf_op jit(solution)/shard_map/reduce_scatter | solution.py:74
  432.6 28.5 %reduce-scatter.48.cloned.1.call-done = bf16[32,512]{1,0:T(8,128)(2,1)} async-done(((bf16[128,512]{1,0:T(8,128)(2,1)}), bf16[32,512]{1,0:T(8,128)(2,1)}) %reduce-scatter.48.cloned.1.call-update) | async-done | bytes 32784 | tf_op jit(solution)/shard_map/reduce_scatter | solution.py:74
  473.9 26.1 %reduce-scatter.50.cloned.1.call-done = bf16[32,512]{1,0:T(8,128)(2,1)} async-done(((bf16[128,512]{1,0:T(8,128)(2,1)}), bf16[32,512]{1,0:T(8,128)(2,1)}) %reduce-scatter.50.cloned.1.call-update) | async-done | bytes 32784 | tf_op jit(solution)/shard_map/reduce_scatter | solution.py:74
  519.2 23.8 %reduce-scatter.52.cloned.1.call-done = bf16[32,512]{1,0:T(8,128)(2,1)} async-done(((bf16[128,512]{1,0:T(8,128)(2,1)}), bf16[32,512]{1,0:T(8,128)(2,1)}) %reduce-scatter.52.cloned.1.call-update) | async-done | bytes 32784 | tf_op jit(solution)/shard_map/reduce_scatter | solution.py:74
  576.0 21.8 %reduce-scatter.54.cloned.1.call-done = bf16[32,512]{1,0:T(8,128)(2,1)} async-done(((bf16[128,512]{1,0:T(8,128)(2,1)}), bf16[32,512]{1,0:T(8,128)(2,1)}) %reduce-scatter.54.cloned.1.call-update) | async-done | bytes 32784 | tf_op jit(solution)/shard_map/reduce_scatter | solution.py:74
  640.1 25.4 %reduce-scatter.56.cloned.1.call-done = bf16[32,512]{1,0:T(8,128)(2,1)} async-done(((bf16[128,512]{1,0:T(8,128)(2,1)}), bf16[32,512]{1,0:T(8,128)(2,1)}) %reduce-scatter.56.cloned.1.call-update) | async-done | bytes 32784 | tf_op jit(solution)/shard_map/reduce_scatter | solution.py:74
  681.2 23.1 %reduce-scatter.58.cloned.1.call-done = bf16[32,512]{1,0:T(8,128)(2,1)} async-done(((bf16[128,512]{1,0:T(8,128)(2,1)}), bf16[32,512]{1,0:T(8,128)(2,1)}) %reduce-scatter.58.cloned.1.call-update) | async-done | bytes 32784 | tf_op jit(solution)/shard_map/reduce_scatter | solution.py:74
  722.9 22.6 %reduce-scatter.60.cloned.1.call-done = bf16[32,512]{1,0:T(8,128)(2,1)} async-done(((bf16[128,512]{1,0:T(8,128)(2,1)}), bf16[32,512]{1,0:T(8,128)(2,1)}) %reduce-scatter.60.cloned.1.call-update) | async-done | bytes 32784 | tf_op jit(solution)/shard_map/reduce_scatter | solution.py:84
  779.3 22.3 %reduce-scatter.62.cloned.1.call-done = bf16[32,512]{1,0:T(8,128)(2,1)} async-done(((bf16[128,512]{1,0:T(8,128)(2,1)}), bf16[32,512]{1,0:T(8,128)(2,1)}) %reduce-scatter.62.cloned.1.call-update) | async-done | bytes 32784 | tf_op jit(solution)/shard_map/reduce_scatter | solution.py:84
  843.5 22.5 %reduce-scatter.64.cloned.1.call-done = bf16[32,512]{1,0:T(8,128)(2,1)} async-done(((bf16[128,512]{1,0:T(8,128)(2,1)}), bf16[32,512]{1,0:T(8,128)(2,1)}) %reduce-scatter.64.cloned.1.call-update) | async-done | bytes 32784 | tf_op jit(solution)/shard_map/reduce_scatter | solution.py:84
  884.3 23.5 %reduce-scatter.66.cloned.1.call-done = bf16[32,512]{1,0:T(8,128)(2,1)} async-done(((bf16[128,512]{1,0:T(8,128)(2,1)}), bf16[32,512]{1,0:T(8,128)(2,1)}) %reduce-scatter.66.cloned.1.call-update) | async-done | bytes 32784 | tf_op jit(solution)/shard_map/reduce_scatter | solution.py:84
  990.0 22.1 %reduce-scatter.70.cloned.1.call-done = bf16[32,512]{1,0:T(8,128)(2,1)} async-done(((bf16[128,512]{1,0:T(8,128)(2,1)}), bf16[32,512]{1,0:T(8,128)(2,1)}) %reduce-scatter.70.cloned.1.call-update) | async-done | bytes 32784 | tf_op jit(solution)/shard_map/reduce_scatter | solution.py:84
  1094.2 23.6 %reduce-scatter.74.cloned.1.call-done = bf16[32,512]{1,0:T(8,128)(2,1)} async-done(((bf16[128,512]{1,0:T(8,128)(2,1)}), bf16[32,512]{1,0:T(8,128)(2,1)}) %reduce-scatter.74.cloned.1.call-update) | async-done | bytes 32784 | tf_op jit(solution)/shard_map/reduce_scatter | solution.py:84
  1197.5 22.3 %reduce-scatter.78.cloned.1.call-done = bf16[32,512]{1,0:T(8,128)(2,1)} async-done(((bf16[128,512]{1,0:T(8,128)(2,1)}), bf16[32,512]{1,0:T(8,128)(2,1)}) %reduce-scatter.78.cloned.1.call-update) | async-done | bytes 32784 | tf_op jit(solution)/shard_map/reduce_scatter | solution.py:84
  1356.6 65.2 %reduce-scatter.88.cloned.1.call-done = f32[32,14]{1,0:T(8,128)} async-done(((f32[512,14]{1,0:T(8,128)}), f32[32,14]{1,0:T(8,128)}) %reduce-scatter.88.cloned.1.call-update) | async-done | bytes 1808
  1423.2 36.6 %reduce-scatter.84.cloned.1.call-done = bf16[8,128,128]{2,1,0:T(8,128)(2,1)} async-done(((bf16[8,512,128]{2,1,0:T(8,128)(2,1)}), bf16[8,128,128]{2,1,0:T(8,128)(2,1)}) %reduce-scatter.84.cloned.1.call-update) | async-done | bytes 262160 | tf_op jit(solution)/shard_map/reduce_scatter | solution.py:109
  1461.6 43.1 %reduce-scatter.86.cloned.1.call-done = bf16[4,128,512]{2,1,0:T(8,128)(2,1)} async-done(((bf16[4,512,512]{2,1,0:T(8,128)(2,1)}), bf16[4,128,512]{2,1,0:T(8,128)(2,1)}) %reduce-scatter.86.cloned.1.call-update) | async-done | bytes 524304 | tf_op jit(solution)/shard_map/reduce_scatter | solution.py:112
  (1048 shorter events, 803.9 us)
Async XLA Ops:
  7.2 112.8 %all-gather.8.cloned.1.call-start = ((), (), s32[]{:S(2)}) async-start(), calls=%async_computation.55 | async-start | bytes 2621440 | tf_op jit(solution)/shard_map/all_gather | solution.py:92
  7.9 116.4 %all-gather.10.cloned.1.call-start = ((), (), s32[]{:S(2)}) async-start(), calls=%async_computation.56 | async-start | bytes 1310720 | tf_op jit(solution)/shard_map/all_gather | solution.py:91
  8.6 150.0 %reduce-scatter.36.cloned.1.call-start = ((), (), s32[]{:S(2)}) async-start(), calls=%async_computation.29 | async-start | bytes 163840 | tf_op jit(solution)/shard_map/reduce_scatter | solution.py:74
  123.4 76.7 %reduce-scatter.38.cloned.1.call-start = ((), (), s32[]{:S(2)}) async-start(), calls=%async_computation.30 | async-start | bytes 163840 | tf_op jit(solution)/shard_map/reduce_scatter | solution.py:74
  173.9 91.9 %reduce-scatter.40.cloned.1.call-start = ((), (), s32[]{:S(2)}) async-start(), calls=%async_computation.31 | async-start | bytes 163840 | tf_op jit(solution)/shard_map/reduce_scatter | solution.py:74
  277.9 68.1 %reduce-scatter.44.cloned.1.call-start = ((), (), s32[]{:S(2)}) async-start(), calls=%async_computation.33 | async-start | bytes 163840 | tf_op jit(solution)/shard_map/reduce_scatter | solution.py:74
  321.0 77.4 %reduce-scatter.46.cloned.1.call-start = ((), (), s32[]{:S(2)}) async-start(), calls=%async_computation.34 | async-start | bytes 163840 | tf_op jit(solution)/shard_map/reduce_scatter | solution.py:74
  372.2 88.9 %reduce-scatter.48.cloned.1.call-start = ((), (), s32[]{:S(2)}) async-start(), calls=%async_computation.35 | async-start | bytes 163840 | tf_op jit(solution)/shard_map/reduce_scatter | solution.py:74
  473.8 69.2 %reduce-scatter.52.cloned.1.call-start = ((), (), s32[]{:S(2)}) async-start(), calls=%async_computation.37 | async-start | bytes 163840 | tf_op jit(solution)/shard_map/reduce_scatter | solution.py:74
  518.0 79.8 %reduce-scatter.54.cloned.1.call-start = ((), (), s32[]{:S(2)}) async-start(), calls=%async_computation.38 | async-start | bytes 163840 | tf_op jit(solution)/shard_map/reduce_scatter | solution.py:74
  571.7 93.8 %reduce-scatter.56.cloned.1.call-start = ((), (), s32[]{:S(2)}) async-start(), calls=%async_computation.39 | async-start | bytes 163840 | tf_op jit(solution)/shard_map/reduce_scatter | solution.py:74
  719.4 82.2 %reduce-scatter.62.cloned.1.call-start = ((), (), s32[]{:S(2)}) async-start(), calls=%async_computation.42 | async-start | bytes 163840 | tf_op jit(solution)/shard_map/reduce_scatter | solution.py:84
  776.2 89.8 %reduce-scatter.64.cloned.1.call-start = ((), (), s32[]{:S(2)}) async-start(), calls=%async_computation.43 | async-start | bytes 163840 | tf_op jit(solution)/shard_map/reduce_scatter | solution.py:84
  839.9 68.0 %reduce-scatter.66.cloned.1.call-start = ((), (), s32[]{:S(2)}) async-start(), calls=%async_computation.44 | async-start | bytes 163840 | tf_op jit(solution)/shard_map/reduce_scatter | solution.py:84
  881.7 75.0 %reduce-scatter.68.cloned.1.call-start = ((), (), s32[]{:S(2)}) async-start(), calls=%async_computation.45 | async-start | bytes 163840 | tf_op jit(solution)/shard_map/reduce_scatter | solution.py:84
  932.6 79.5 %reduce-scatter.70.cloned.1.call-start = ((), (), s32[]{:S(2)}) async-start(), calls=%async_computation.46 | async-start | bytes 163840 | tf_op jit(solution)/shard_map/reduce_scatter | solution.py:84
  986.7 89.0 %reduce-scatter.72.cloned.1.call-start = ((), (), s32[]{:S(2)}) async-start(), calls=%async_computation.47 | async-start | bytes 163840 | tf_op jit(solution)/shard_map/reduce_scatter | solution.py:84
  1049.6 68.2 %reduce-scatter.74.cloned.1.call-start = ((), (), s32[]{:S(2)}) async-start(), calls=%async_computation.48 | async-start | bytes 163840 | tf_op jit(solution)/shard_map/reduce_scatter | solution.py:84
  1091.6 73.1 %reduce-scatter.76.cloned.1.call-start = ((), (), s32[]{:S(2)}) async-start(), calls=%async_computation.49 | async-start | bytes 163840 | tf_op jit(solution)/shard_map/reduce_scatter | solution.py:84
  1140.7 79.1 %reduce-scatter.78.cloned.1.call-start = ((), (), s32[]{:S(2)}) async-start(), calls=%async_computation.50 | async-start | bytes 163840 | tf_op jit(solution)/shard_map/reduce_scatter | solution.py:84
  1194.4 84.0 %reduce-scatter.80.cloned.1.call-start = ((), (), s32[]{:S(2)}) async-start(), calls=%async_computation.51 | async-start | bytes 163840 | tf_op jit(solution)/shard_map/reduce_scatter | solution.py:84
  1294.9 127.0 %reduce-scatter.88.cloned.1.call-start = ((), (), s32[]{:S(2)}) async-start(), calls=%async_computation.57 | async-start | bytes 278528
  1319.0 140.8 %reduce-scatter.84.cloned.1.call-start = ((), (), s32[]{:S(2)}) async-start(), calls=%async_computation.53 | async-start | bytes 1310720 | tf_op jit(solution)/shard_map/reduce_scatter | solution.py:109
  1320.3 184.3 %reduce-scatter.86.cloned.1.call-start = ((), (), s32[]{:S(2)}) async-start(), calls=%async_computation.54 | async-start | bytes 2621440 | tf_op jit(solution)/shard_map/reduce_scatter | solution.py:112
  (267 other events, 3859.3 us)
Sparse Core Ops, SparseCore 0:
  9.6 50.4 all-gather.7
  61.6 26.6 all-gather.9
  123.5 35.0 reduce-scatter.35
  174.1 25.9 reduce-scatter.37
  237.4 28.4 reduce-scatter.39
  278.0 25.9 reduce-scatter.41
  372.3 26.0 reduce-scatter.45
  432.7 28.4 reduce-scatter.47
  473.9 25.9 reduce-scatter.49
  571.8 26.0 reduce-scatter.53
  637.1 28.4 reduce-scatter.55
  678.3 25.9 reduce-scatter.57
  719.5 25.9 reduce-scatter.59
  776.4 25.2 reduce-scatter.61
  840.0 25.9 reduce-scatter.63
  881.8 25.9 reduce-scatter.65
  1049.7 25.9 reduce-scatter.71
  1091.7 26.0 reduce-scatter.73
  1194.5 25.2 reduce-scatter.77
  1252.4 26.0 reduce-scatter.79
  1289.4 25.9 reduce-scatter.81
  1357.2 64.5 reduce-scatter.87
  1424.7 35.1 reduce-scatter.83
  1462.1 42.4 reduce-scatter.85
  (7 shorter events, 156.8 us)
where the time goes:
time: 1530 us; the launch traced here: 1510 us
  waiting for transfers between devices  707 us (46%)
  blocking collectives  291 us (19%)
  other arithmetic  181 us (12%)
  matrix products  171 us (11%)
  local copies, waits for them, and re-layouts  122 us (8%)
  between operations  31.2 us (2%)
    reduce_scatter x12, waiting for transfers between devices, rows_summed(): lax.psum_scatter(partial_rows.astype(jnp.bfloat16), 'tensor', scatter_dim...  308 us
    reduce_scatter x12, waiting for transfers between devices, grads_summed(): lax.psum_scatter(partial_rows.astype(jnp.bfloat16), 'tensor', scatter_dim...  231 us
    unnamed x34, waiting for transfers between devices  84.6 us
    all_gather x12, blocking collectives, grads_full(): return lax.all_gather(shard_rows, 'tensor', axis=0, tiled=True)  77.2 us
    all_gather x12, blocking collectives, rows_full(): return lax.all_gather(shard_rows, 'tensor', axis=0, tiled=True)  76.7 us
    dot_general x68, matrix products, contract(): lax.dot_general(left_side, right_side, (((left_dim,), (right_dim,)), ((),...  76 us
    unnamed x534, local copies, waits for them, and re-layouts  60.7 us
    reduce_scatter x1, waiting for transfers between devices, spread_grads(): lax.psum_scatter(ff_mats.astype(jnp.bfloat16), 'dp', scatter_dimension=1,...  43.1 us
  transfers between devices with their start and end apart: 35, of which 30 were waited for; matrix products, arithmetic and copies ran while one was open for 11% of the time, Pallas kernels for 0%

commit v1 on v0

v1 whole, which is shorter than its diff:
```python
import functools

import jax
import jax.numpy as jnp
from jax import lax
from jax.experimental import pallas as pl
from jax.experimental.pallas import tpu as pltpu
from jax.sharding import PartitionSpec as P

HEAD_DIM = 64
MB = 2
EPSILON = 1e-05
HUGE_NEG = -1000000000.0
F32 = jnp.float32
BF16 = jnp.bfloat16
LANES = 128
VMEM_LIMIT = 56 * 1024 * 1024

ORDER_A = 0
ORDER_B = 1
ORDER_C = 2


def sinusoid(length, width):
    place = (length - 1 - jnp.arange(2 * length - 1)).astype(F32)
    index = jnp.arange(width // 2).astype(F32)
    rate = jnp.exp(index * (-2.0 * jnp.log(10000.0) / width))
    angle = place[:, None] * rate[None, :]
    return jnp.stack([jnp.sin(angle), jnp.cos(angle)], axis=-1).reshape(2 * length - 1, width)


def nn(a, b):
    return lax.dot_general(a, b, (((1,), (0,)), ((), ())), preferred_element_type=F32)


def nt(a, b):
    return lax.dot_general(a, b, (((1,), (1,)), ((), ())), preferred_element_type=F32)


def tn(a, b):
    return lax.dot_general(a, b, (((0,), (0,)), ((), ())), preferred_element_type=F32)


def ln_parts(v):
    centre = v - jnp.mean(v, axis=-1, keepdims=True)
    rstd = lax.rsqrt(jnp.mean(centre * centre, axis=-1, keepdims=True) + EPSILON)
    return centre * rstd, rstd


def ln(v, gain, shift):
    xhat, _ = ln_parts(v)
    return xhat * (1.0 + gain) + shift


def ln_back(v, gain, dy):
    xhat, rstd = ln_parts(v)
    g = dy * (1.0 + gain)
    dx = rstd * (
        g - jnp.mean(g, axis=-1, keepdims=True) - xhat * jnp.mean(g * xhat, axis=-1, keepdims=True)
    )
    return dx, rows_sum(dy * xhat), rows_sum(dy)


def rows_sum(v):
    return jnp.sum(v, axis=0, keepdims=True)


def sigmoid(v):
    return 1.0 / (1.0 + jnp.exp(-v))


def silu_slope(v):
    s = sigmoid(v)
    return s * (1.0 + v * (1.0 - s))


def bit_order(order, count):
    return [(order + k) % count for k in range(count)]


def slot_mask(slot, bits):
    out = 0
    for k, b in enumerate(bits):
        out |= ((slot >> k) & 1) << b
    return out


def start_weights(meta, own, oth, dst, sem, order, slots, tensor, half, which=None):
    bits = bit_order(order, slots.bit_length() - 1)
    me, core = meta[0], meta[1]
    rows, cols = own.shape[-2], own.shape[-1]
    for slot in range(slots):
        f = me ^ slot_mask(slot, bits)
        plane, t = f // tensor, lax.rem(f, tensor)
        col = pl.ds(pl.multiple_of(t * cols, cols), cols)
        for src, c in ((own, core), (oth, 1 - core)):
            row = pl.ds(pl.multiple_of((c * half + plane) * rows, rows), rows)
            s = src.at[slot] if which is None else src.at[slot, pl.ds(which[0], which[1])]
            pltpu.make_async_copy(s, dst.at[:, row, col], sem).start()


def wait_weights(dst, sem):
    pltpu.make_async_copy(dst, dst, sem).wait()


def head_mask(h):
    lane = lax.broadcasted_iota(jnp.int32, (1, LANES), 1)
    return (lane // HEAD_DIM) == h


def blk(i):
    return slice(i * LANES, (i + 1) * LANES)


def f1_kernel(dims, meta, x_ref, vm_ref, vi_ref, vf_ref, pos_ref, a_own, a_oth, b_own, b_oth,
              s2_ref, filt_ref, stat_ref, s1_ref, before_ref, qu_ref, qv_ref, k_ref, v_ref,
              rel_ref, probs_ref, ctx_ref, gi_ref, gs_ref,
              wa, wb, pad, sems):
    slots, tensor, half = dims
    start_weights(meta, a_own, a_oth, wa, sems.at[0], ORDER_A, slots, tensor, half)
    start_weights(meta, b_own, b_oth, wb, sems.at[1], ORDER_B, slots, tensor, half)
    length = meta[2]
    n_tok = x_ref.shape[0]
    vm = lambda r: vm_ref[r:r + 1, :]
    vi = lambda r: vi_ref[r:r + 1, :]
    x = x_ref[...].astype(F32)
    wait_weights(wa, sems.at[0])
    n0 = ln(x, vm(0), vm(1)).astype(BF16)
    before = nn(n0, wa[0]) + vf_ref[0:1, :]
    before_ref[...] = before
    active = (before * sigmoid(before)).astype(BF16)
    s1 = x + 0.5 * (nt(active, wa[1]) + vm(2))
    s1_ref[...] = s1
    wait_weights(wb, sems.at[1])
    rel_ref[...] = nn(pos_ref[...], wb[4]).astype(BF16)
    n1 = ln(s1, vm(3), vm(4)).astype(BF16)
    q = nn(n1, wb[0]) + vi(0)
    qu_ref[...] = (q + vi(2)).astype(BF16)
    qv_ref[...] = (q + vi(3)).astype(BF16)
    k_ref[...] = nn(n1, wb[1]).astype(BF16)
    v_ref[...] = (nn(n1, wb[2]) + vi(1)).astype(BF16)
    keep = lax.broadcasted_iota(jnp.int32, (1, n_tok), 1) < length
    for i in range(qu_ref.shape[1] // LANES):
        qub, qvb, kb, vb = (r[:, blk(i)] for r in (qu_ref, qv_ref, k_ref, v_ref))
        rb = rel_ref[:, blk(i)]
        halves = []
        for h in range(2):
            mask = head_mask(h)
            direct = nt(jnp.where(mask, qub, 0), kb)
            table = nt(jnp.where(mask, qvb, 0), rb)
            shifted = pltpu.roll(table, n_tok + 1, 1, stride=1, stride_axis=0)[:, :n_tok]
            scores = jnp.where(keep, (direct + shifted) * HEAD_DIM ** (-0.5), HUGE_NEG)
            e = jnp.exp(scores - jnp.max(scores, axis=-1, keepdims=True))
            probs = e / jnp.sum(e, axis=-1, keepdims=True)
            probs_ref[2 * i + h] = probs
            halves.append(nn(probs.astype(BF16), vb))
        ctx_ref[:, blk(i)] = jnp.where(head_mask(0), halves[0], halves[1]).astype(BF16)
    s2 = s1 + nt(ctx_ref[...], wb[3]) + vm(5)
    s2_ref[...] = s2
    n2 = ln(s2, vm(6), vm(7)).astype(BF16)
    gi = nn(n2, wb[5]) + vi(4)
    gs = nn(n2, wb[6]) + vi(5)
    gi_ref[...] = gi
    gs_ref[...] = gs
    inside = (lax.broadcasted_iota(jnp.int32, (n_tok, 1), 0) < length).astype(F32)
    mixed = gi * sigmoid(gs) * inside
    taps = vi_ref.shape[0] - 9
    pad_store(pad, mixed)
    run_taps(pad, vi_ref, [8 + k for k in range(taps)], filt_ref)
    f = filt_ref[...]
    count = length.astype(F32)
    total = rows_sum(inside * f)
    centre = (f - total / count) * inside
    stat_ref[0:1, :] = total
    stat_ref[1:2, :] = rows_sum(centre * centre)
    stat_ref[2:3, :] = jnp.full_like(total, 1.0) * count
    stat_ref[3:8, :] = jnp.zeros((5, total.shape[1]), F32)


def pad_store(pad, value):
    rows = value.shape[0]
    pad[0:16, :] = jnp.zeros((16, value.shape[1]), F32)
    pad[16:16 + rows, :] = value
    pad[16 + rows:32 + rows, :] = jnp.zeros((16, value.shape[1]), F32)


def run_taps(pad, vi_ref, rows, out_ref):
    n_tok = out_ref.shape[0]
    wide = n_tok + 8
    for i in range(out_ref.shape[1] // LANES):
        total = None
        for s in range(8):
            part = None
            for q in range(4):
                e = 8 * q + s - 1
                if 0 <= e < len(rows):
                    term = vi_ref[rows[e]:rows[e] + 1, blk(i)] * pad[8 * q:8 * q + wide, blk(i)]
                    part = term if part is None else part + term
            moved = part[s:s + n_tok]
            total = moved if total is None else total + moved
        out_ref[:, blk(i)] = total


def bn_combine(stats_ref):
    groups = stats_ref.shape[0]
    total = sum(stats_ref[g, 0:1, :] for g in range(groups))
    count = sum(stats_ref[g, 2:3, :] for g in range(groups))
    mean = total / count
    m2 = 0.0
    for g in range(groups):
        n_g = stats_ref[g, 2:3, :]
        off = stats_ref[g, 0:1, :] / n_g - mean
        m2 = m2 + stats_ref[g, 1:2, :] + n_g * off * off
    return mean, lax.rsqrt(m2 / count + EPSILON), count


def f2_kernel(dims, meta, s2_ref, filt_ref, stats_ref, vm_ref, vi_ref, vf_ref, b_own, b_oth,
              c_own, c_oth, out_ref, s3_ref, before_ref, s4_ref, bn_ref, wct, wc, sems):
    slots, tensor, half = dims
    start_weights(meta, b_own, b_oth, wct, sems.at[0], ORDER_B, slots, tensor, half, (7, 1))
    start_weights(meta, c_own, c_oth, wc, sems.at[1], ORDER_C, slots, tensor, half)
    vm = lambda r: vm_ref[r:r + 1, :]
    vi = lambda r: vi_ref[r:r + 1, :]
    mean, inv, count = bn_combine(stats_ref)
    bn_ref[0:1, :] = mean
    bn_ref[1:2, :] = inv
    bn_ref[2:3, :] = count
    bn_ref[3:8, :] = jnp.zeros((5, mean.shape[1]), F32)
    normal = (filt_ref[...] - mean) * inv * (1.0 + vi(6)) + vi(7)
    active = (normal * sigmoid(normal)).astype(BF16)
    wait_weights(wct, sems.at[0])
    s3 = s2_ref[...] + nt(active, wct[0]) + vm(8)
    s3_ref[...] = s3
    n3 = ln(s3, vm(9), vm(10)).astype(BF16)
    wait_weights(wc, sems.at[1])
    before = nn(n3, wc[0]) + vf_ref[1:2, :]
    before_ref[...] = before
    act = (before * sigmoid(before)).astype(BF16)
    s4 = s3 + 0.5 * (nt(act, wc[1]) + vm(11))
    s4_ref[...] = s4
    out_ref[...] = ln(s4, vm(12), vm(13)).astype(BF16)


def b1_kernel(dims, meta, g_ref, s4_ref, s3_ref, before_ref, filt_ref, bn_ref, vm_ref, vi_ref,
              b_own, b_oth, c_own, c_oth,
              ds3_ref, dnorm_ref, sum_ref, n3_ref, db_ref, dl_ref, a_ref, dlc_ref, ac_ref,
              gm_ref, gi_ref, gf_ref, wct, wc, sems):
    slots, tensor, half = dims
    start_weights(meta, c_own, c_oth, wc, sems.at[1], ORDER_C, slots, tensor, half)
    start_weights(meta, b_own, b_oth, wct, sems.at[0], ORDER_B, slots, tensor, half, (7, 1))
    vm = lambda r: vm_ref[r:r + 1, :]
    vi = lambda r: vi_ref[r:r + 1, :]
    ds4, gain4, shift4 = ln_back(s4_ref[...], vm(12), g_ref[...].astype(F32))
    delta = (0.5 * ds4).astype(BF16)
    dl_ref[...] = delta
    s3 = s3_ref[...]
    n3_ref[...] = ln(s3, vm(9), vm(10)).astype(BF16)
    before = before_ref[...]
    a_ref[...] = (before * sigmoid(before)).astype(BF16)
    wait_weights(wc, sems.at[1])
    db = (nn(delta, wc[1]) * silu_slope(before)).astype(BF16)
    db_ref[...] = db
    dn = nt(db, wc[0])
    dx, gain3, shift3 = ln_back(s3, vm(9), dn)
    ds3 = ds4 + dx
    ds3_ref[...] = ds3
    dlc = ds3.astype(BF16)
    dlc_ref[...] = dlc
    xhat = (filt_ref[...] - bn_ref[0:1, :]) * bn_ref[1:2, :]
    normal = xhat * (1.0 + vi(6)) + vi(7)
    ac_ref[...] = (normal * sigmoid(normal)).astype(BF16)
    wait_weights(wct, sems.at[0])
    dnorm = nn(dlc, wct[0]) * silu_slope(normal)
    dnorm_ref[...] = dnorm
    u6 = rows_sum(dnorm * xhat)
    u7 = rows_sum(dnorm)
    sum_ref[0:1, :] = u7 * (1.0 + vi(6))
    sum_ref[1:2, :] = u6 * (1.0 + vi(6))
    sum_ref[2:8, :] = jnp.zeros((6, u6.shape[1]), F32)
    gm_ref[0:1, :] = rows_sum(dlc.astype(F32))
    gm_ref[1:2, :] = gain3
    gm_ref[2:3, :] = shift3
    gm_ref[3:4, :] = rows_sum(delta.astype(F32))
    gm_ref[4:5, :] = gain4
    gm_ref[5:6, :] = shift4
    gm_ref[6:8, :] = jnp.zeros((2, u6.shape[1]), F32)
    gi_ref[0:1, :] = u6
    gi_ref[1:2, :] = u7
    gi_ref[2:8, :] = jnp.zeros((6, u6.shape[1]), F32)
    gf_ref[...] = rows_sum(db.astype(F32))


def b2_kernel(dims, meta, ds3_ref, dnorm_ref, sums_ref, filt_ref, bn_ref, gin_ref, gsig_ref,
              s2_ref, s1_ref, x_ref, before_ref, qu_ref, qv_ref, k_ref, v_ref, rel_ref,
              probs_ref, vm_ref, vi_ref, a_own, a_oth, b_own, b_oth,
              dx_ref, n2_ref, dgi_ref, dgs_ref, dla_ref, n1_ref, dq_ref, dk_ref, dv_ref,
              drel_ref, n0_ref, db_ref, dl_ref, a_ref, gm_ref, gi_ref, gf_ref,
              wa, wb, pad_m, pad_d, dmix, sems):
    slots, tensor, half = dims
    start_weights(meta, b_own, b_oth, wb, sems.at[1], ORDER_B, slots, tensor, half)
    start_weights(meta, a_own, a_oth, wa, sems.at[0], ORDER_A, slots, tensor, half)
    length = meta[2]
    n_tok, width = ds3_ref.shape
    vm = lambda r: vm_ref[r:r + 1, :]
    vi = lambda r: vi_ref[r:r + 1, :]
    groups = sums_ref.shape[0]
    plain = sum(sums_ref[g, 0:1, :] for g in range(groups))
    tilted = sum(sums_ref[g, 1:2, :] for g in range(groups))
    inv = bn_ref[1:2, :]
    xhat = (filt_ref[...] - bn_ref[0:1, :]) * inv
    inside = (lax.broadcasted_iota(jnp.int32, (n_tok, 1), 0) < length).astype(F32)
    dfilt = inv * (
        dnorm_ref[...] * (1.0 + vi(6)) - inside / bn_ref[2:3, :] * (plain + xhat * tilted)
    )
    gin = gin_ref[...]
    sig = sigmoid(gsig_ref[...])
    taps = vi_ref.shape[0] - 9
    pad_store(pad_m, gin * sig * inside)
    pad_store(pad_d, dfilt)
    run_taps(pad_d, vi_ref, [8 + taps - 1 - e for e in range(taps)], dmix)
    wide = n_tok + 8
    for i in range(width // LANES):
        for s in range(8):
            moved = pad_d[16 - s:16 - s + wide, blk(i)]
            for q in range(4):
                e = 8 * q + s - 1
                if 0 <= e < taps:
                    gi_ref[6 + e:7 + e, blk(i)] = rows_sum(
                        moved * pad_m[8 * q:8 * q + wide, blk(i)]
                    )
    dm = dmix[...] * inside
    dgi = (dm * sig).astype(BF16)
    dgs = (dm * gin * sig * (1.0 - sig)).astype(BF16)
    dgi_ref[...] = dgi
    dgs_ref[...] = dgs
    wait_weights(wb, sems.at[1])
    s2 = s2_ref[...]
    n2_ref[...] = ln(s2, vm(6), vm(7)).astype(BF16)
    dx, gain, shift = ln_back(s2, vm(6), nt(dgi, wb[5]) + nt(dgs, wb[6]))
    gm_ref[6:7, :] = gain
    gm_ref[7:8, :] = shift
    ds2 = ds3_ref[...] + dx
    dla = ds2.astype(BF16)
    dla_ref[...] = dla
    dctx = nn(dla, wb[3]).astype(BF16)
    row = lax.broadcasted_iota(jnp.int32, (n_tok, n_tok), 0)
    col = lax.broadcasted_iota(jnp.int32, (n_tok, n_tok), 1)
    flip = (row + col == n_tok - 1).astype(F32).astype(BF16)
    for i in range(width // LANES):
        qub, qvb, kb, vb = (r[:, blk(i)] for r in (qu_ref, qv_ref, k_ref, v_ref))
        rb = rel_ref[:, blk(i)]
        dcb = dctx[:, blk(i)]
        got = []
        for h in range(2):
            mask = head_mask(h)
            probs = probs_ref[2 * i + h]
            dprobs = nt(jnp.where(mask, dcb, 0), vb)
            dvh = tn(probs.astype(BF16), dcb)
            ds = probs * (dprobs - jnp.sum(probs * dprobs, axis=-1, keepdims=True))
            ds = (ds.astype(BF16).astype(F32) * HEAD_DIM ** (-0.5)).astype(BF16)
            turned = jnp.concatenate([nn(flip, ds), jnp.zeros((n_tok, n_tok), F32)], axis=1)
            turned = pltpu.roll(turned, 0, 1, stride=1, stride_axis=0).astype(BF16)
            dr = nn(flip, turned).astype(BF16)
            got.append((nn(ds, kb), nn(dr, rb), tn(ds, qub), dvh, tn(dr, qvb)))
        first = head_mask(0)
        dqu, dqv, dk, dv, drel = (jnp.where(first, a, b) for a, b in zip(*got))
        dq = (dqu + dqv).astype(BF16)
        dvb = dv.astype(BF16)
        dq_ref[:, blk(i)] = dq
        dk_ref[:, blk(i)] = dk.astype(BF16)
        dv_ref[:, blk(i)] = dvb
        drel_ref[:, blk(i)] = drel.astype(BF16)
        gi_ref[0:1, blk(i)] = rows_sum(dq.astype(F32))
        gi_ref[1:2, blk(i)] = rows_sum(dvb.astype(F32))
        gi_ref[2:3, blk(i)] = rows_sum(dqu)
        gi_ref[3:4, blk(i)] = rows_sum(dqv)
    gi_ref[4:5, :] = rows_sum(dgi.astype(F32))
    gi_ref[5:6, :] = rows_sum(dgs.astype(F32))
    gi_ref[6 + taps:40, :] = jnp.zeros((40 - 6 - taps, width), F32)
    s1 = s1_ref[...]
    n1_ref[...] = ln(s1, vm(3), vm(4)).astype(BF16)
    dn = nt(dq_ref[...], wb[0]) + nt(dk_ref[...], wb[1]) + nt(dv_ref[...], wb[2])
    dx, gain, shift = ln_back(s1, vm(3), dn)
    gm_ref[3:4, :] = gain
    gm_ref[4:5, :] = shift
    gm_ref[5:6, :] = rows_sum(dla.astype(F32))
    ds1 = ds2 + dx
    delta = (0.5 * ds1).astype(BF16)
    dl_ref[...] = delta
    before = before_ref[...]
    a_ref[...] = (before * sigmoid(before)).astype(BF16)
    wait_weights(wa, sems.at[0])
    db = (nn(delta, wa[1]) * silu_slope(before)).astype(BF16)
    db_ref[...] = db
    x = x_ref[...].astype(F32)
    n0_ref[...] = ln(x, vm(0), vm(1)).astype(BF16)
    dx, gain, shift = ln_back(x, vm(0), nt(db, wa[0]))
    gm_ref[0:1, :] = gain
    gm_ref[1:2, :] = shift
    gm_ref[2:3, :] = rows_sum(delta.astype(F32))
    gf_ref[...] = rows_sum(db.astype(F32))
    dx_ref[...] = (ds1 + dx).astype(BF16)


def w_kernel(dims, order, count, meta, *refs):
    slots, tensor, half = dims
    pairs, out = refs[:2 * count], refs[2 * count]
    bits = bit_order(order, slots.bit_length() - 1)
    me, core = meta[0], meta[1]
    rows, cols = out.shape[-2], out.shape[-1]
    mine = half * rows
    for i in range(count):
        left, right = pairs[2 * i], pairs[2 * i + 1]
        part = left[:, pl.ds(pl.multiple_of(core * mine, mine), mine)]
        grad = tn(part, right[...])
        for f in range(slots):
            rel = me ^ f
            slot = sum((lax.shift_right_logical(rel, b) & 1) << k for k, b in enumerate(bits))
            plane, t = f // tensor, f % tensor
            out[slot, i] = grad[plane * rows:(plane + 1) * rows, t * cols:(t + 1) * cols].astype(BF16)


def vmem(*shape):
    return pl.BlockSpec(memory_space=pltpu.VMEM)


def call(kernel, ins, outs, scratch=(), any_from=None, flops=0, name=None):
    specs = [pl.BlockSpec(memory_space=pltpu.SMEM)]
    for i in range(1, len(ins)):
        away = any_from is not None and i >= any_from
        specs.append(pl.BlockSpec(memory_space=pl.ANY if away else pltpu.VMEM))
    nbytes = sum(a.size * a.dtype.itemsize for a in ins)
    return pl.pallas_call(
        kernel,
        out_shape=[jax.ShapeDtypeStruct(s, d) for s, d in outs],
        in_specs=specs,
        out_specs=[pl.BlockSpec(memory_space=pltpu.VMEM) for _ in outs],
        scratch_shapes=list(scratch),
        compiler_params=pltpu.CompilerParams(vmem_limit_bytes=VMEM_LIMIT),
        cost_estimate=pl.CostEstimate(flops=flops, bytes_accessed=nbytes, transcendentals=0),
        name=name,
    )(*ins)


def permute(value, pairs):
    return lax.ppermute(value, ("pipe", "dp", "tensor"), pairs)


def per_device(n, tensor, boundary, lengths, batch_of, mats, ffw, vec_model, vec_inner, vec_ff):
    half = n // 2
    slots = half * tensor
    nbits = slots.bit_length() - 1
    dims = (slots, tensor, half)
    core = lax.axis_index("pipe")
    d = lax.axis_index("dp")
    t = lax.axis_index("tensor")
    upper = d // half
    plane = lax.rem(d, half)
    me = plane * tensor + t
    is_upper = upper == 1

    def flat(c, dd, tt):
        return (c * n + dd) * tensor + tt

    everyone = [(c, dd, tt) for c in range(2) for dd in range(n) for tt in range(tensor)]

    def home(c, dd, tt):
        u = dd // half
        return (c, dd, tt) if c == u else (1 - c, dd + half if u == 0 else dd - half, tt)

    swap_pairs = [(flat(*e), flat(*home(*e))) for e in everyone]
    core_pairs = [(flat(c, dd, tt), flat(1 - c, dd, tt)) for c, dd, tt in everyone]

    def bit_pairs(b):
        out = []
        for c, dd, tt in everyone:
            f = ((dd % half) * tensor + tt) ^ (1 << b)
            out.append((flat(c, dd, tt), flat(c, dd // half * half + f // tensor, f % tensor)))
        return out

    def gather(block, order):
        held = permute(block, swap_pairs)[None]
        for b in bit_order(order, nbits):
            held = jnp.concatenate([held, permute(held, bit_pairs(b))], axis=0)
        return held, permute(held, core_pairs)

    def natural(value, lead):
        shape = value.shape
        value = value.reshape((2,) * nbits + shape[1:])
        for b in range(nbits):
            on = lax.shift_right_logical(me, b) & 1
            value = jnp.where(on == 1, jnp.flip(value, nbits - 1 - b), value)
        return value.reshape(shape)

    def by_core(own, oth):
        return jnp.where(core == 0, jnp.stack([own, oth]), jnp.stack([oth, own]))

    ends = boundary[0]
    rows_here, width = ends.shape[1], ends.shape[2]
    length_all = rows_here * tensor
    per_vec = [vec_model.shape[1] * vec_model.shape[2], vec_inner.shape[1] * vec_inner.shape[2],
               vec_ff.shape[1] * vec_ff.shape[2]]
    rows_vec = -(-(sum(per_vec) + MB) // width)
    rows_vec = -(-rows_vec // 16) * 16
    first_is = batch_of[0] == 0
    ordered = jnp.where(first_is, ends, ends[::-1]).reshape(MB * rows_here, width)
    len_ordered = jnp.where(first_is, lengths, lengths[::-1]).astype(BF16)
    vec = jnp.concatenate([vec_model[0].reshape(-1), vec_inner[0].reshape(-1),
                           vec_ff[0].reshape(-1), len_ordered])
    vec = jnp.pad(vec, (0, rows_vec * width - vec.size)).reshape(rows_vec, width)
    v_own, v_oth = gather(jnp.concatenate([ordered, vec], axis=0), 0)
    a_own, a_oth = gather(ffw[0, 0:2], ORDER_A)
    b_own, b_oth = gather(mats[0], ORDER_B)
    c_own, c_oth = gather(ffw[0, 2:4], ORDER_C)

    everything = by_core(natural(v_own, 0), natural(v_oth, 0))
    everything = everything.reshape(n, tensor, MB * rows_here + rows_vec, width)
    vecs = everything[:, :, MB * rows_here:].reshape(n, tensor, rows_vec * width)
    cut = [0, per_vec[0], per_vec[0] + per_vec[1], sum(per_vec)]
    vm = vecs[:, :, cut[0]:cut[1]].reshape(n, tensor, vec_model.shape[1], -1)
    vm = vm.transpose(2, 0, 1, 3).reshape(vec_model.shape[1], width).astype(F32)
    vi = vecs[:, :, cut[1]:cut[2]].reshape(n, tensor, vec_inner.shape[1], -1)
    vi = vi.transpose(2, 1, 0, 3).reshape(vec_inner.shape[1], width).astype(F32)
    vi = jnp.pad(vi, ((0, 1), (0, 0)))
    vf = vecs[:, :, cut[2]:cut[3]].reshape(n, tensor, vec_ff.shape[1], -1)
    vf = vf.transpose(2, 1, 0, 3).reshape(vec_ff.shape[1], -1).astype(F32)
    side, micro = lax.rem(t, 2), t // 2
    source = side * half + plane
    mine = lax.dynamic_index_in_dim(everything, source, 0, keepdims=False)
    tokens = mine[:, :MB * rows_here].reshape(tensor, MB, rows_here, width)
    x0 = lax.dynamic_index_in_dim(tokens, micro, 1, keepdims=False).reshape(length_all, width)
    my_lengths = vecs[:, 0, cut[3]:cut[3] + MB]
    my_length = lax.dynamic_index_in_dim(my_lengths, source, 0, keepdims=False)
    my_length = lax.dynamic_index_in_dim(my_length, micro, 0, keepdims=False).astype(jnp.int32)
    meta = jnp.stack([me, core, my_length, upper]).astype(jnp.int32)
    pos = jnp.pad(sinusoid(length_all, width), ((0, 1), (0, 0))).astype(BF16)

    hidden = vf.shape[1]
    rows, fcols, mcols = ffw.shape[2], ffw.shape[3], mats.shape[3]
    heads = width // HEAD_DIM
    L, D, H = length_all, width, hidden
    wa_s = pltpu.VMEM((2, D, H), BF16)
    wb_s = pltpu.VMEM((8, D, D), BF16)
    wct_s = pltpu.VMEM((1, D, D), BF16)
    sems = pltpu.SemaphoreType.DMA((2,))
    pad_s = pltpu.VMEM((L + 32, D), F32)
    mat_flops = 2 * L * D * D

    def f1(x):
        return call(
            functools.partial(f1_kernel, dims),
            [meta, x, vm, vi, vf, pos, a_own, a_oth, b_own, b_oth],
            [((L, D), F32), ((L, D), F32), ((8, D), F32), ((L, D), F32), ((L, H), F32)]
            + [((L, D), BF16)] * 4
            + [((2 * L, D), BF16), ((heads, L, L), F32), ((L, D), BF16), ((L, D), F32), ((L, D), F32)],
            [wa_s, wb_s, pad_s, sems], 6, 15 * mat_flops, "layer_front",
        )

    def f2(s2, filt, stats):
        return call(
            functools.partial(f2_kernel, dims),
            [meta, s2, filt, stats, vm, vi, vf, b_own, b_oth, c_own, c_oth],
            [((L, D), BF16), ((L, D), F32), ((L, H), F32), ((L, D), F32), ((8, D), F32)],
            [wct_s, wa_s, sems], 7, 9 * mat_flops, "layer_rear",
        )

    def b1(g, s4, s3, before, filt, bn):
        return call(
            functools.partial(b1_kernel, dims),
            [meta, g, s4, s3, before, filt, bn, vm, vi, b_own, b_oth, c_own, c_oth],
            [((L, D), F32), ((L, D), F32), ((8, D), F32), ((L, D), BF16), ((L, H), BF16),
             ((L, D), BF16), ((L, H), BF16), ((L, D), BF16), ((L, D), BF16),
             ((8, D), F32), ((8, D), F32), ((1, H), F32)],
            [wct_s, wa_s, sems], 9, 9 * mat_flops, "back_rear",
        )

    def b2(ds3, dnorm, sums, filt, bn, gin, gsig, s2, s1, x, before, qu, qv, k, v, rel, probs):
        return call(
            functools.partial(b2_kernel, dims),
            [meta, ds3, dnorm, sums, filt, bn, gin, gsig, s2, s1, x, before, qu, qv, k, v, rel,
             probs, vm, vi, a_own, a_oth, b_own, b_oth],
            [((L, D), BF16)] * 9 + [((2 * L, D), BF16), ((L, D), BF16), ((L, H), BF16),
             ((L, D), BF16), ((L, H), BF16), ((8, D), F32), ((40, D), F32), ((1, H), F32)],
            [wa_s, wb_s, pad_s, pad_s, pltpu.VMEM((L, D), F32), sems], 20, 20 * mat_flops,
            "back_front",
        )

    def w(order, pairs, cols):
        flat_pairs = [a for pair in pairs for a in pair]
        return call(
            functools.partial(w_kernel, dims, order, len(pairs)),
            [meta] + flat_pairs,
            [((slots, len(pairs), rows, cols), BF16)],
            (), None, 4 * mat_flops, "weight_grads",
        )[0]

    norm_bits = [0] + list(range(tensor.bit_length() - 1, nbits))

    def norm_group(value):
        held = value[None]
        for b in norm_bits:
            held = jnp.concatenate([held, permute(held, bit_pairs(b))], axis=0)
        return held

    up_pairs = [(flat(c, dd, tt), flat(c, dd + half, tt)) for c, dd, tt in everyone if dd < half]
    down_pairs = [(b, a) for a, b in up_pairs]

    def forward(x):
        front = f1(x)
        stats = norm_group(front[2])
        rear = f2(front[0], front[1], stats)
        return front, rear

    front, rear = forward(x0)
    middle = permute(rear[0], up_pairs)
    x1 = jnp.where(is_upper, middle, x0)
    front, rear = forward(x1)
    (s2, filt, _, s1, before0, qu, qv, k, v, rel, probs, ctx, gin, gsig) = front
    made, s3, before1, s4, bn = rear

    def backward(g):
        part1 = b1(g, s4, s3, before1, filt, bn)
        sums = norm_group(part1[2])
        part2 = b2(part1[0], part1[1], sums, filt, bn, gin, gsig, s2, s1, x1, before0, qu, qv, k,
                   v, rel, probs)
        return part1, part2

    _, part2 = backward(x0)
    d_middle = permute(part2[0], down_pairs)
    part1, part2 = backward(jnp.where(is_upper, x0, d_middle))
    (_, _, _, n3, db1, dl3, a1, dlc, ac, gm1, gi1, gf1) = part1
    (dx, n2, dgi, dgs, dla, n1, dq, dk, dv, drel, n0, db0, dl0, a0, gm2, gi2, gf2) = part2

    def scatter(value, order):
        bits = bit_order(order, nbits)
        for b in reversed(bits):
            keep = value.shape[0] // 2
            got = permute(value[keep:], bit_pairs(b))
            value = (value[:keep].astype(F32) + got.astype(F32)).astype(value.dtype)
        return permute(value[0], swap_pairs)

    grad_c = scatter(w(ORDER_C, [(n3, db1), (dl3, a1)], fcols), ORDER_C)
    pos_pair = jnp.pad(pos, ((0, 0), (0, 0)))
    grad_b = scatter(
        w(ORDER_B, [(n1, dq), (n1, dk), (n1, dv), (dla, ctx), (pos_pair, drel), (n2, dgi),
                    (n2, dgs), (dlc, ac)], mcols), ORDER_B)
    grad_a = scatter(w(ORDER_A, [(n0, db0), (dl0, a0)], fcols), ORDER_A)

    gm = jnp.concatenate([gm2[0:8], gm1[0:6]], axis=0)
    gi = jnp.concatenate([gi2[0:6], gi1[0:2], gi2[6:6 + vec_inner.shape[1] - 8]], axis=0)
    gf = jnp.concatenate([gf2, gf1], axis=0)
    gm = gm.reshape(gm.shape[0], n, tensor, -1).transpose(1, 2, 0, 3).reshape(n, tensor, -1)
    gi = gi.reshape(gi.shape[0], tensor, n, -1).transpose(2, 1, 0, 3).reshape(n, tensor, -1)
    gf = gf.reshape(gf.shape[0], tensor, n, -1).transpose(2, 1, 0, 3).reshape(n, tensor, -1)
    gv = jnp.concatenate([gm, gi, gf], axis=2)
    gv = jnp.pad(gv, ((0, 0), (0, 0), (0, rows_vec * width - gv.shape[2])))
    gv = lax.dynamic_slice_in_dim(gv, core * half, half, 0).reshape(slots, rows_vec, width)
    gv = scatter(natural(gv, 0), 0).reshape(-1)

    stream = jnp.where(is_upper, made, dx).reshape(tensor, rows_here, width)
    got = [None] * MB
    for j in range(tensor):
        sent = lax.dynamic_index_in_dim(stream, t ^ j, 0, keepdims=False)
        if j:
            pairs = [(flat(tt & 1, dd, tt), flat(tt & 1, dd, tt ^ j))
                     for c, dd, tt in everyone if c == 0]
            sent = permute(sent, pairs)
        got[j >> 1] = sent if got[j >> 1] is None else jnp.where(
            lax.rem(t ^ j, 2) == core, sent, got[j >> 1])
    pair = jnp.stack(got)
    pair = jnp.where(micro == 0, pair, pair[::-1])
    pair = permute(pair, swap_pairs)
    ends_out = jnp.where(first_is, pair, pair[::-1])[None]

    return (
        ends_out,
        grad_b.astype(F32)[None],
        jnp.concatenate([grad_a, grad_c], axis=0).astype(F32)[None],
        gv[cut[0]:cut[1]].reshape(vec_model.shape),
        gv[cut[1]:cut[2]].reshape(vec_inner.shape),
        gv[cut[2]:cut[3]].reshape(vec_ff.shape),
    )


def solution(mesh):
    return jax.shard_map(
        functools.partial(per_device, mesh.shape["dp"], mesh.shape["tensor"]),
        mesh=mesh,
        in_specs=(
            P("pipe", "dp", "tensor", None),
            P("dp"),
            P("dp"),
            P("pipe", None, "dp", "tensor"),
            P("pipe", None, "dp", "tensor"),
            P("pipe", None, ("dp", "tensor")),
            P("pipe", None, ("tensor", "dp")),
            P("pipe", None, ("tensor", "dp")),
        ),
        out_specs=(
            P("pipe", "dp", "tensor", None),
            P("pipe", None, "dp", "tensor"),
            P("pipe", None, "dp", "tensor"),
            P("pipe", None, ("dp", "tensor")),
            P("pipe", None, ("tensor", "dp")),
            P("pipe", None, ("tensor", "dp")),
        ),
        check_vma=False,
    )
```

time: 1530 us -> 352 us (0.23)
  waiting for transfers between devices: 707 us -> 102 us
  blocking collectives: 291 us -> 0 us
  matrix products: 171 us -> 0 us
  other arithmetic: 181 us -> 43.4 us
  local copies, waits for them, and re-layouts: 122 us -> 25.8 us
  Pallas kernels: 0 us -> 93.3 us
  starting transfers between devices: 10.6 us -> 78.7 us
  between operations: 31.2 us -> 3.1 us
    reduce_scatter x26 -> x0, waiting for transfers between devices: 619 us -> none  [the longest x12 308 us: rows_summed(): lax.psum_scatter(partial_rows.astype(jnp.bfloat16), 'tensor', scatter_dim...]
    all_gather x27 -> x0, blocking collectives: 209 us -> none  [the longest x12 77.2 us: grads_full(): return lax.all_gather(shard_rows, 'tensor', axis=0, tiled=True)]
    dot_general x129 -> x0, matrix products: 153 us -> none  [the longest x68 76 us: contract(): lax.dot_general(left_side, right_side, (((left_dim,), (right_dim,)), ((),...]
    ppermute x4 -> x50, waiting for transfers between devices: 3.65 us -> 102 us  [permute(): return lax.ppermute(value, ('pipe', 'dp', 'tensor'), pairs)]
    pallas_call x0 -> x11, Pallas kernels: none -> 93.3 us  [call(): pl.pallas_call(kernel, out_shape=[jax.ShapeDtypeStruct(s, d) for s, d in...]
    reduce_sum x87 -> x0, other arithmetic: 88.3 us -> none  [the longest x22 30.7 us: layer_norm(): return centre * lax.rsqrt(spread + EPSILON) * (1.0 + gain) + shift]
    unnamed x34 -> x0, waiting for transfers between devices: 84.6 us -> none
    psum x9 -> x0, blocking collectives: 82.3 us -> none  [the longest x3 30.9 us: conv_forward(): chan_total, token_count = lax.psum((local_sum, local_count), 'dp')]
  transfers between devices with their start and end apart: 35 -> 50, of which waited for: 30 -> 25; matrix products, arithmetic and copies ran while one was open for 11% -> 18% of each run, Pallas kernels for 0% -> 10%
where the time goes in v1:
time: 352 us; the launch traced here: 346 us
  waiting for transfers between devices  102 us (29%)
  Pallas kernels  93.3 us (27%)
  starting transfers between devices  78.7 us (22%)
  other arithmetic  43.4 us (12%)
  local copies, waits for them, and re-layouts  25.8 us (7%)
    ppermute x50, waiting for transfers between devices, permute(): return lax.ppermute(value, ('pipe', 'dp', 'tensor'), pairs)  102 us
    pallas_call x11, Pallas kernels, call(): pl.pallas_call(kernel, out_shape=[jax.ShapeDtypeStruct(s, d) for s, d in...  93.3 us
    ppermute x50, starting transfers between devices, permute(): return lax.ppermute(value, ('pipe', 'dp', 'tensor'), pairs)  78.7 us
    concatenate x12, other arithmetic, gather(): held = jnp.concatenate([held, permute(held, bit_pairs(b))], axis=0)  10.6 us
    another operation x1, other arithmetic  8.14 us
    concatenate x8, other arithmetic, norm_group(): held = jnp.concatenate([held, permute(held, bit_pairs(b))], axis=0)  7.57 us
    slice x11, local copies, waits for them, and re-layouts, scatter(): got = permute(value[keep:], bit_pairs(b))  7.3 us
  transfers between devices with their start and end apart: 50, of which 25 were waited for; matrix products, arithmetic and copies ran while one was open for 18% of the time, Pallas kernels for 10%

profile of v1, /device:TPU:1, one launch (start us, length us, event | category | flops | bytes accessed | tf_op | source)
XLA Modules:
  0.0 346.1 jit_solution(9229962740952214291)
XLA Ops:
  1.7 5.6 %collective-permute-start.5 = (bf16[2,128,512]{2,1,0:T(8,128)(2,1)S(1)}, bf16[2,128,512]{2,1,0:T(8,128)(2,1)S(1)}, u32[]{:S(2)}, u32[]{:S(2)}) collective-permute-start(bf16[2,128,512]{2,1,0:T(8,128)(2,1)S(1)} %get-tuple-element.125), channel_id=1, source_target_pairs={{0,0},{1,1},{2,2},{3,3},{4,4},{5,5},{6,6},{7,7},{8,16},{9,17},{10,... | collective-permute-start | bytes 786440 | tf_op jit(solution)/shard_map/ppermute | solution.py:446
  9.2 4.5 %collective-permute-start.17 = (bf16[2,128,512]{2,1,0:T(8,128)(2,1)S(1)}, bf16[2,128,512]{2,1,0:T(8,128)(2,1)S(1)}, u32[]{:S(2)}, u32[]{:S(2)}) collective-permute-start(bf16[2,128,512]{2,1,0:T(8,128)(2,1)S(1)} %get-tuple-element.124), channel_id=1, source_target_pairs={{0,0},{1,1},{2,2},{3,3},{4,4},{5,5},{6,6},{7,7},{8,16},{9,17},{10,... | collective-permute-start | bytes 786440 | tf_op jit(solution)/shard_map/ppermute | solution.py:446
  26.3 4.3 %collective-permute-done = bf16[80,512]{1,0:T(8,128)(2,1)S(1)} collective-permute-done((bf16[80,512]{1,0:T(8,128)(2,1)S(1)}, bf16[80,512]{1,0:T(8,128)(2,1)S(1)}, u32[]{:S(2)}, u32[]{:S(2)}) %collective-permute-start) | collective-permute-done | bytes 81952 | tf_op jit(solution)/shard_map/ppermute | solution.py:446
  35.4 5.0 %collective-permute-done.18 = bf16[1,2,128,512]{3,2,1,0:T(8,128)(2,1)S(1)} collective-permute-done((bf16[1,2,128,512]{3,2,1,0:T(8,128)(2,1)S(1)}, bf16[1,2,128,512]{3,2,1,0:T(8,128)(2,1)S(1)}, u32[]{:S(2)}, u32[]{:S(2)}) %collective-permute-start.18) | collective-permute-done | bytes 262176 | tf_op jit(solution)/shard_map/ppermute | solution.py:446
  43.5 8.1 %collective-permute-done.12 = bf16[2,8,128,128]{3,2,1,0:T(8,128)(2,1)S(1)} collective-permute-done((bf16[2,8,128,128]{3,2,1,0:T(8,128)(2,1)S(1)}, bf16[2,8,128,128]{3,2,1,0:T(8,128)(2,1)S(1)}, u32[]{:S(2)}, u32[]{:S(2)}) %collective-permute-start.12) | collective-permute-done | bytes 524320 | tf_op jit(solution)/shard_map/ppermute | solution.py:446
  53.1 8.1 %fusion = (bf16[255,256,1]{0,2,1:T(2,128)(2,1)S(1)}, bf16[255,256,1]{0,2,1:T(2,128)(2,1)S(1)}) fusion(f32[255]{0:T(256)S(1)} %subtract_convert_fusion, f32[256]{0:T(256)S(1)} %multiply_exponential_fusion), kind=kLoop, calls=%fused_computation.35 | loop fusion | flops 195840 | bytes 263164 | tf_op jit(solution)/shard_map/convert.16
  62.7 10.0 %collective-permute-done.3 = bf16[4,80,512]{2,1,0:T(8,128)(2,1)S(1)} collective-permute-done((bf16[4,80,512]{2,1,0:T(8,128)(2,1)S(1)}, bf16[4,80,512]{2,1,0:T(8,128)(2,1)S(1)}, u32[]{:S(2)}, u32[]{:S(2)}) %collective-permute-start.3) | collective-permute-done | bytes 327712 | tf_op jit(solution)/shard_map/ppermute | solution.py:446
  96.3 10.2 %layer_front.2 = (f32[128,512]{1,0:T(8,128)}, f32[128,512]{1,0:T(8,128)}, f32[8,512]{1,0:T(8,128)}, f32[128,512]{1,0:T(8,128)}, f32[128,2048]{1,0:T(8,128)}, /*i...) custom-call(s32[4]{0:T(128)} %pad_add_fusion.meta, ...), custom_call_target="tpu_custom_call" | custom-call | flops 1006632960 | bytes 8908816 | tf_op jit(solution)/shard_map/layer_front/pallas_call | solution.py:433
  114.2 5.6 %layer_rear.2 = (bf16[128,512]{1,0:T(8,128)(2,1)}, f32[128,512]{1,0:T(8,128)}, f32[128,2048]{1,0:T(8,128)}, f32[128,512]{1,0:T(8,128)}, f32[8,512]{1,0:T(8,128)}) custom-call(s32[4]{0:T(128)} %pad_add_fusion.meta, f32[128,512]{1,0:T(8,128)} %get-tuple-element.62.s2_ref, f32[128,512]{1,0:T(8,128)} %get-tuple-element.63.filt_ref, ...), custom_call_target="tpu_custom_call" | custom-call | flops 603979776 | bytes 9105424 | tf_op jit(solution)/shard_map/layer_rear/pallas_call | solution.py:433
  119.9 4.6 %collective-permute-start.22 = (bf16[128,512]{1,0:T(8,128)(2,1)}, bf16[128,512]{1,0:T(8,128)(2,1)S(1)}, u32[]{:S(2)}, u32[]{:S(2)}) collective-permute-start(bf16[128,512]{1,0:T(8,128)(2,1)} %get-tuple-element.65), channel_id=1, source_target_pairs={{0,8},{1,9},{2,10},{3,11},{4,12},{5,13},{6,14},{7,15},{16,24},{17,... | collective-permute-start | bytes 393224 | tf_op jit(solution)/shard_map/ppermute | solution.py:446
  127.1 10.2 %layer_front.3 = (f32[128,512]{1,0:T(8,128)}, f32[128,512]{1,0:T(8,128)}, f32[8,512]{1,0:T(8,128)}, f32[128,512]{1,0:T(8,128)}, f32[128,2048]{1,0:T(8,128)}, /*i...) custom-call(s32[4]{0:T(128)} %pad_add_fusion.meta, ...), custom_call_target="tpu_custom_call" | custom-call | flops 1006632960 | bytes 8908816 | tf_op jit(solution)/shard_map/layer_front/pallas_call | solution.py:433
  146.1 5.6 %layer_rear.3 = (bf16[128,512]{1,0:T(8,128)(2,1)}, f32[128,512]{1,0:T(8,128)}, f32[128,2048]{1,0:T(8,128)}, f32[128,512]{1,0:T(8,128)}, f32[8,512]{1,0:T(8,128)}) custom-call(s32[4]{0:T(128)} %pad_add_fusion.meta, f32[128,512]{1,0:T(8,128)} %get-tuple-element.66.s2_ref, f32[128,512]{1,0:T(8,128)} %get-tuple-element.67.filt_ref, ...), custom_call_target="tpu_custom_call" | custom-call | flops 603979776 | bytes 9105424 | tf_op jit(solution)/shard_map/layer_rear/pallas_call | solution.py:433
  151.7 6.4 %back_rear.2 = (f32[128,512]{1,0:T(8,128)}, f32[128,512]{1,0:T(8,128)}, f32[8,512]{1,0:T(8,128)}, bf16[128,512]{1,0:T(8,128)(2,1)}, bf16[128,2048]{1,0:T(8,128)(...) custom-call(s32[4]{0:T(128)} %pad_add_fusion.meta, ...), custom_call_target="tpu_custom_call" | custom-call | flops 603979776 | bytes 10481680 | tf_op jit(solution)/shard_map/back_rear/pallas_call | solution.py:433
  166.2 24.6 %back_front.2 = (bf16[128,512]{1,0:T(8,128)(2,1)}, bf16[128,512]{1,0:T(8,128)(2,1)}, bf16[128,512]{1,0:T(8,128)(2,1)}, bf16[128,512]{1,0:T(8,128)(2,1)}, bf16[12...) custom-call(s32[4]{0:T(128)} %pad_add_fusion.meta, ...), custom_call_target="tpu_custom_call" | custom-call | flops 1342177280 | bytes 12906512 | tf_op jit(solution)/shard_map/back_front/pallas_call | solution.py:433
  192.1 8.1 %collective-permute-done.27 = bf16[128,512]{1,0:T(8,128)(2,1)S(1)} collective-permute-done((bf16[128,512]{1,0:T(8,128)(2,1)}, bf16[128,512]{1,0:T(8,128)(2,1)S(1)}, u32[]{:S(2)}, u32[]{:S(2)}) %collective-permute-start.27) | collective-permute-done | bytes 131104 | tf_op jit(solution)/shard_map/ppermute | solution.py:446
  200.9 6.4 %back_rear.3 = (f32[128,512]{1,0:T(8,128)}, f32[128,512]{1,0:T(8,128)}, f32[8,512]{1,0:T(8,128)}, bf16[128,512]{1,0:T(8,128)(2,1)}, bf16[128,2048]{1,0:T(8,128)(...) custom-call(s32[4]{0:T(128)} %pad_add_fusion.meta, ...), custom_call_target="tpu_custom_call" | custom-call | flops 603979776 | bytes 10481680 | tf_op jit(solution)/shard_map/back_rear/pallas_call | solution.py:433
  219.3 13.8 %back_front.3 = (bf16[128,512]{1,0:T(8,128)(2,1)}, bf16[128,512]{1,0:T(8,128)(2,1)}, bf16[128,512]{1,0:T(8,128)(2,1)}, bf16[128,512]{1,0:T(8,128)(2,1)}, bf16[12...) custom-call(s32[4]{0:T(128)} %pad_add_fusion.meta, ...), custom_call_target="tpu_custom_call" | custom-call | flops 1342177280 | bytes 12906512 | tf_op jit(solution)/shard_map/back_front/pallas_call | solution.py:433
  245.3 4.5 %collective-permute-start.34 = (bf16[4,8,128,128]{3,2,1,0:T(8,128)(2,1)}, bf16[4,8,128,128]{3,2,1,0:T(8,128)(2,1)}, u32[]{:S(2)}, u32[]{:S(2)}) collective-permute-start(bf16[4,8,128,128]{3,2,1,0:T(8,128)(2,1)} %slice.175), channel_id=1, source_target_pairs={{0,1},{1,0},{2,3},{3,2},{4,5},{5,4},{6,7},{7,6},{8,9},{9,8},{10,11... | collective-permute-start | bytes 3145736 | tf_op jit(solution)/shard_map/ppermute | solution.py:446
  258.6 17.5 %collective-permute-done.46 = f32[4,16,512]{2,1,0:T(8,128)S(1)} collective-permute-done((f32[4,16,512]{2,1,0:T(8,128)S(1)}, f32[4,16,512]{2,1,0:T(8,128)S(1)}, u32[]{:S(2)}, u32[]{:S(2)}) %collective-permute-start.46) | collective-permute-done | bytes 131104 | tf_op jit(solution)/shard_map/ppermute | solution.py:446
  279.8 11.1 %collective-permute-start.33 = (bf16[2,32,512]{2,1,0:T(8,128)(2,1)S(1)}, bf16[2,32,512]{2,1,0:T(8,128)(2,1)S(1)}, u32[]{:S(2)}, u32[]{:S(2)}) collective-permute-start(bf16[2,32,512]{2,1,0:T(8,128)(2,1)S(1)} %reverse_select_fusion.10), channel_id=1, source_target_pairs={{0,0},{1,1},{2,2},{3,3},{4,4},{5,5},{6,6},{7,7},{8,16},{9,17},{10,... | collective-permute-start | bytes 196616 | tf_op jit(solution)/shard_map/ppermute | solution.py:446
  291.0 4.0 %collective-permute-start.49 = (f32[16,512]{1,0:T(8,128)S(1)}, f32[16,512]{1,0:T(8,128)S(1)}, u32[]{:S(2)}, u32[]{:S(2)}) collective-permute-start(f32[16,512]{1,0:T(8,128)S(1)} %fusion.6), channel_id=1, source_target_pairs={{0,0},{1,1},{2,2},{3,3},{4,4},{5,5},{6,6},{7,7},{8,16},{9,17},{10,... | collective-permute-start | bytes 98312 | tf_op jit(solution)/shard_map/ppermute | solution.py:446
  304.5 7.2 %collective-permute-done.43 = bf16[2,2,128,512]{3,2,1,0:T(8,128)(2,1)S(1)} collective-permute-done((bf16[2,2,128,512]{3,2,1,0:T(8,128)(2,1)S(1)}, bf16[2,2,128,512]{3,2,1,0:T(8,128)(2,1)S(1)}, u32[]{:S(2)}, u32[]{:S(2)}) %collective-permute-start.43) | collective-permute-done | bytes 524320 | tf_op jit(solution)/shard_map/ppermute | solution.py:446
  324.5 4.5 %collective-permute-start.41 = (bf16[2,128,512]{2,1,0:T(8,128)(2,1)S(1)}, bf16[2,128,512]{2,1,0:T(8,128)(2,1)S(1)}, u32[]{:S(2)}, u32[]{:S(2)}) collective-permute-start(bf16[2,128,512]{2,1,0:T(8,128)(2,1)S(1)} %fusion.3), channel_id=1, source_target_pairs={{0,0},{1,1},{2,2},{3,3},{4,4},{5,5},{6,6},{7,7},{8,16},{9,17},{10,... | collective-permute-start | bytes 786440 | tf_op jit(solution)/shard_map/ppermute | solution.py:446
  331.7 7.8 %collective-permute-done.45 = bf16[2,128,512]{2,1,0:T(8,128)(2,1)S(1)} collective-permute-done((bf16[2,128,512]{2,1,0:T(8,128)(2,1)S(1)}, bf16[2,128,512]{2,1,0:T(8,128)(2,1)S(1)}, u32[]{:S(2)}, u32[]{:S(2)}) %collective-permute-start.45) | collective-permute-done | bytes 262176 | tf_op jit(solution)/shard_map/ppermute | solution.py:446
  (249 shorter events, 145.2 us)
Async XLA Ops:
  1.7 16.6 %collective-permute-start.5 = (bf16[2,128,512]{2,1,0:T(8,128)(2,1)S(1)}, bf16[2,128,512]{2,1,0:T(8,128)(2,1)S(1)}, u32[]{:S(2)}, u32[]{:S(2)}) collective-permute-start(bf16[2,128,512]{2,1,0:T(8,128)(2,1)S(1)} %get-tuple-element.125), channel_id=1, source_target_pairs={{0,0},{1,1},{2,2},{3,3},{4,4},{5,5},{6,6},{7,7},{8,16},{9,17},{10,... | collective-permute-start | bytes 786440 | tf_op jit(solution)/shard_map/ppermute | solution.py:446
  7.3 15.3 %collective-permute-start.10 = (bf16[8,128,128]{2,1,0:T(8,128)(2,1)}, bf16[8,128,128]{2,1,0:T(8,128)(2,1)S(1)}, u32[]{:S(2)}, u32[]{:S(2)}) collective-permute-start(bf16[8,128,128]{2,1,0:T(8,128)(2,1)} %bitcast.148), channel_id=1, source_target_pairs={{0,0},{1,1},{2,2},{3,3},{4,4},{5,5},{6,6},{7,7},{8,16},{9,17},{10,... | collective-permute-start | bytes 786440 | tf_op jit(solution)/shard_map/ppermute | solution.py:446
  9.2 22.7 %collective-permute-start.17 = (bf16[2,128,512]{2,1,0:T(8,128)(2,1)S(1)}, bf16[2,128,512]{2,1,0:T(8,128)(2,1)S(1)}, u32[]{:S(2)}, u32[]{:S(2)}) collective-permute-start(bf16[2,128,512]{2,1,0:T(8,128)(2,1)S(1)} %get-tuple-element.124), channel_id=1, source_target_pairs={{0,0},{1,1},{2,2},{3,3},{4,4},{5,5},{6,6},{7,7},{8,16},{9,17},{10,... | collective-permute-start | bytes 786440 | tf_op jit(solution)/shard_map/ppermute | solution.py:446
  26.0 14.8 %collective-permute-start.7 = (bf16[2,2,128,512]{3,2,1,0:T(8,128)(2,1)S(1)}, bf16[2,2,128,512]{3,2,1,0:T(8,128)(2,1)S(1)}, u32[]{:S(2)}, u32[]{:S(2)}) collective-permute-start(bf16[2,2,128,512]{3,2,1,0:T(8,128)(2,1)S(1)} %pad_maximum_fusion.7), channel_id=1, source_target_pairs={{0,2},{1,3},{2,0},{3,1},{4,6},{5,7},{6,4},{7,5},{8,10},{9,11},{10,... | collective-permute-start | bytes 1572872 | tf_op jit(solution)/shard_map/ppermute | solution.py:446
  33.3 18.3 %collective-permute-start.12 = (bf16[2,8,128,128]{3,2,1,0:T(8,128)(2,1)S(1)}, bf16[2,8,128,128]{3,2,1,0:T(8,128)(2,1)S(1)}, u32[]{:S(2)}, u32[]{:S(2)}) collective-permute-start(bf16[2,8,128,128]{3,2,1,0:T(8,128)(2,1)S(1)} %pad_maximum_fusion.8), channel_id=1, source_target_pairs={{0,4},{1,5},{2,6},{3,7},{4,0},{5,1},{6,2},{7,3},{8,12},{9,13},{10,... | collective-permute-start | bytes 1572872 | tf_op jit(solution)/shard_map/ppermute | solution.py:446
  40.5 20.8 %collective-permute-start.19 = (bf16[2,2,128,512]{3,2,1,0:T(8,128)(2,1)S(1)}, bf16[2,2,128,512]{3,2,1,0:T(8,128)(2,1)S(1)}, u32[]{:S(2)}, u32[]{:S(2)}) collective-permute-start(bf16[2,2,128,512]{3,2,1,0:T(8,128)(2,1)S(1)} %pad_maximum_fusion.9), channel_id=1, source_target_pairs={{0,1},{1,0},{2,3},{3,2},{4,5},{5,4},{6,7},{7,6},{8,9},{9,8},{10,11... | collective-permute-start | bytes 1572872 | tf_op jit(solution)/shard_map/ppermute | solution.py:446
  41.9 32.8 %collective-permute-start.8 = (bf16[4,2,128,512]{3,2,1,0:T(8,128)(2,1)}, bf16[4,2,128,512]{3,2,1,0:T(8,128)(2,1)}, u32[]{:S(2)}, u32[]{:S(2)}) collective-permute-start(bf16[4,2,128,512]{3,2,1,0:T(8,128)(2,1)} %pad_maximum_fusion.3), channel_id=1, source_target_pairs={{0,4},{1,5},{2,6},{3,7},{4,0},{5,1},{6,2},{7,3},{8,12},{9,13},{10,... | collective-permute-start | bytes 3145736 | tf_op jit(solution)/shard_map/ppermute | solution.py:446
  43.4 29.2 %collective-permute-start.3 = (bf16[4,80,512]{2,1,0:T(8,128)(2,1)S(1)}, bf16[4,80,512]{2,1,0:T(8,128)(2,1)S(1)}, u32[]{:S(2)}, u32[]{:S(2)}) collective-permute-start(bf16[4,80,512]{2,1,0:T(8,128)(2,1)S(1)} %pad_maximum_fusion.10), channel_id=1, source_target_pairs={{0,4},{1,5},{2,6},{3,7},{4,0},{5,1},{6,2},{7,3},{8,12},{9,13},{10,... | collective-permute-start | bytes 983048 | tf_op jit(solution)/shard_map/ppermute | solution.py:446
  52.8 25.3 %collective-permute-start.13 = (bf16[4,8,128,128]{3,2,1,0:T(8,128)(2,1)}, bf16[4,8,128,128]{3,2,1,0:T(8,128)(2,1)}, u32[]{:S(2)}, u32[]{:S(2)}) collective-permute-start(bf16[4,8,128,128]{3,2,1,0:T(8,128)(2,1)} %pad_maximum_fusion.4), channel_id=1, source_target_pairs={{0,1},{1,0},{2,3},{3,2},{4,5},{5,4},{6,7},{7,6},{8,9},{9,8},{10,11... | collective-permute-start | bytes 3145736 | tf_op jit(solution)/shard_map/ppermute | solution.py:446
  62.4 19.3 %collective-permute-start.20 = (bf16[4,2,128,512]{3,2,1,0:T(8,128)(2,1)}, bf16[4,2,128,512]{3,2,1,0:T(8,128)(2,1)}, u32[]{:S(2)}, u32[]{:S(2)}) collective-permute-start(bf16[4,2,128,512]{3,2,1,0:T(8,128)(2,1)} %pad_maximum_fusion.5), channel_id=1, source_target_pairs={{0,2},{1,3},{2,0},{3,1},{4,6},{5,7},{6,4},{7,5},{8,10},{9,11},{10,... | collective-permute-start | bytes 3145736 | tf_op jit(solution)/shard_map/ppermute | solution.py:446
  77.6 18.7 %collective-permute-start.9 = (bf16[8,2,128,512]{3,2,1,0:T(8,128)(2,1)}, bf16[8,2,128,512]{3,2,1,0:T(8,128)(2,1)}, u32[]{:S(2)}, u32[]{:S(2)}) collective-permute-start(bf16[8,2,128,512]{3,2,1,0:T(8,128)(2,1)} %pad_maximum_fusion.a_own), channel_id=1, source_target_pairs={{0,16},{1,17},{2,18},{3,19},{4,20},{5,21},{6,22},{7,23},{8,24},{9,... | collective-permute-start | bytes 6291464 | tf_op jit(solution)/shard_map/ppermute | solution.py:446
  79.5 16.8 %collective-permute-start.14 = (bf16[8,8,128,128]{3,2,1,0:T(8,128)(2,1)S(1)}, bf16[8,8,128,128]{3,2,1,0:T(8,128)(2,1)}, u32[]{:S(2)}, u32[]{:S(2)}) collective-permute-start(bf16[8,8,128,128]{3,2,1,0:T(8,128)(2,1)S(1)} %pad_maximum_fusion.1.b_own), channel_id=1, source_target_pairs={{0,16},{1,17},{2,18},{3,19},{4,20},{5,21},{6,22},{7,23},{8,24},{9,... | collective-permute-start | bytes 6291464 | tf_op jit(solution)/shard_map/ppermute | solution.py:446
  84.5 29.7 %collective-permute-start.21 = (bf16[8,2,128,512]{3,2,1,0:T(8,128)(2,1)}, bf16[8,2,128,512]{3,2,1,0:T(8,128)(2,1)}, u32[]{:S(2)}, u32[]{:S(2)}) collective-permute-start(bf16[8,2,128,512]{3,2,1,0:T(8,128)(2,1)} %pad_maximum_fusion.2.c_own), channel_id=1, source_target_pairs={{0,16},{1,17},{2,18},{3,19},{4,20},{5,21},{6,22},{7,23},{8,24},{9,... | collective-permute-start | bytes 6291464 | tf_op jit(solution)/shard_map/ppermute | solution.py:446
  216.7 82.2 %collective-permute-start.42 = (bf16[4,2,128,512]{3,2,1,0:T(8,128)(2,1)}, bf16[4,2,128,512]{3,2,1,0:T(8,128)(2,1)S(1)}, u32[]{:S(2)}, u32[]{:S(2)}) collective-permute-start(bf16[4,2,128,512]{3,2,1,0:T(8,128)(2,1)} %slice.187), channel_id=1, source_target_pairs={{0,2},{1,3},{2,0},{3,1},{4,6},{5,7},{6,4},{7,5},{8,10},{9,11},{10,... | collective-permute-start | bytes 3145736 | tf_op jit(solution)/shard_map/ppermute | solution.py:446
  235.7 21.4 %collective-permute-start.31 = (bf16[32,512]{1,0:T(8,128)(2,1)S(1)}, bf16[32,512]{1,0:T(8,128)(2,1)S(1)}, u32[]{:S(2)}, u32[]{:S(2)}) collective-permute-start(bf16[32,512]{1,0:T(8,128)(2,1)S(1)} %get-tuple-element.130), channel_id=1, source_target_pairs={{0,3},{17,18},{2,1},{19,16},{4,7},{21,22},{6,5},{23,20},{8,11},{25... | collective-permute-start | bytes 98312 | tf_op jit(solution)/shard_map/ppermute | solution.py:446
  237.0 21.4 %collective-permute-start.32 = (bf16[32,512]{1,0:T(8,128)(2,1)S(1)}, bf16[32,512]{1,0:T(8,128)(2,1)S(1)}, u32[]{:S(2)}, u32[]{:S(2)}) collective-permute-start(bf16[32,512]{1,0:T(8,128)(2,1)S(1)} %get-tuple-element.129), channel_id=1, source_target_pairs={{0,2},{17,19},{2,0},{19,17},{4,6},{21,23},{6,4},{23,21},{8,10},{25... | collective-permute-start | bytes 98312 | tf_op jit(solution)/shard_map/ppermute | solution.py:446
  237.6 20.9 %collective-permute-start.30 = (bf16[32,512]{1,0:T(8,128)(2,1)S(1)}, bf16[32,512]{1,0:T(8,128)(2,1)S(1)}, u32[]{:S(2)}, u32[]{:S(2)}) collective-permute-start(bf16[32,512]{1,0:T(8,128)(2,1)S(1)} %get-tuple-element.128), channel_id=1, source_target_pairs={{0,1},{17,16},{2,3},{19,18},{4,5},{21,20},{6,7},{23,22},{8,9},{25,... | collective-permute-start | bytes 98312 | tf_op jit(solution)/shard_map/ppermute | solution.py:446
  245.3 57.4 %collective-permute-start.34 = (bf16[4,8,128,128]{3,2,1,0:T(8,128)(2,1)}, bf16[4,8,128,128]{3,2,1,0:T(8,128)(2,1)}, u32[]{:S(2)}, u32[]{:S(2)}) collective-permute-start(bf16[4,8,128,128]{3,2,1,0:T(8,128)(2,1)} %slice.175), channel_id=1, source_target_pairs={{0,1},{1,0},{2,3},{3,2},{4,5},{5,4},{6,7},{7,6},{8,9},{9,8},{10,11... | collective-permute-start | bytes 3145736 | tf_op jit(solution)/shard_map/ppermute | solution.py:446
  257.1 43.7 %collective-permute-start.38 = (bf16[4,2,128,512]{3,2,1,0:T(8,128)(2,1)}, bf16[4,2,128,512]{3,2,1,0:T(8,128)(2,1)}, u32[]{:S(2)}, u32[]{:S(2)}) collective-permute-start(bf16[4,2,128,512]{3,2,1,0:T(8,128)(2,1)} %slice.181), channel_id=1, source_target_pairs={{0,4},{1,5},{2,6},{3,7},{4,0},{5,1},{6,2},{7,3},{8,12},{9,13},{10,... | collective-permute-start | bytes 3145736 | tf_op jit(solution)/shard_map/ppermute | solution.py:446
  258.4 17.7 %collective-permute-start.46 = (f32[4,16,512]{2,1,0:T(8,128)S(1)}, f32[4,16,512]{2,1,0:T(8,128)S(1)}, u32[]{:S(2)}, u32[]{:S(2)}) collective-permute-start(f32[4,16,512]{2,1,0:T(8,128)S(1)} %bitcast.127), channel_id=1, source_target_pairs={{0,4},{1,5},{2,6},{3,7},{4,0},{5,1},{6,2},{7,3},{8,12},{9,13},{10,... | collective-permute-start | bytes 393224 | tf_op jit(solution)/shard_map/ppermute | solution.py:446
  279.8 15.2 %collective-permute-start.33 = (bf16[2,32,512]{2,1,0:T(8,128)(2,1)S(1)}, bf16[2,32,512]{2,1,0:T(8,128)(2,1)S(1)}, u32[]{:S(2)}, u32[]{:S(2)}) collective-permute-start(bf16[2,32,512]{2,1,0:T(8,128)(2,1)S(1)} %reverse_select_fusion.10), channel_id=1, source_target_pairs={{0,0},{1,1},{2,2},{3,3},{4,4},{5,5},{6,6},{7,7},{8,16},{9,17},{10,... | collective-permute-start | bytes 196616 | tf_op jit(solution)/shard_map/ppermute | solution.py:446
  322.4 17.0 %collective-permute-start.45 = (bf16[2,128,512]{2,1,0:T(8,128)(2,1)S(1)}, bf16[2,128,512]{2,1,0:T(8,128)(2,1)S(1)}, u32[]{:S(2)}, u32[]{:S(2)}) collective-permute-start(bf16[2,128,512]{2,1,0:T(8,128)(2,1)S(1)} %fusion.4), channel_id=1, source_target_pairs={{0,0},{1,1},{2,2},{3,3},{4,4},{5,5},{6,6},{7,7},{8,16},{9,17},{10,... | collective-permute-start | bytes 786440 | tf_op jit(solution)/shard_map/ppermute | solution.py:446
  324.5 17.8 %collective-permute-start.41 = (bf16[2,128,512]{2,1,0:T(8,128)(2,1)S(1)}, bf16[2,128,512]{2,1,0:T(8,128)(2,1)S(1)}, u32[]{:S(2)}, u32[]{:S(2)}) collective-permute-start(bf16[2,128,512]{2,1,0:T(8,128)(2,1)S(1)} %fusion.3), channel_id=1, source_target_pairs={{0,0},{1,1},{2,2},{3,3},{4,4},{5,5},{6,6},{7,7},{8,16},{9,17},{10,... | collective-permute-start | bytes 786440 | tf_op jit(solution)/shard_map/ppermute | solution.py:446
  329.1 16.0 %collective-permute-start.37 = (bf16[8,128,128]{2,1,0:T(8,128)(2,1)S(1)}, bf16[8,128,128]{2,1,0:T(8,128)(2,1)S(1)}, u32[]{:S(2)}, u32[]{:S(2)}) collective-permute-start(bf16[8,128,128]{2,1,0:T(8,128)(2,1)S(1)} %fusion.2), channel_id=1, source_target_pairs={{0,0},{1,1},{2,2},{3,3},{4,4},{5,5},{6,6},{7,7},{8,16},{9,17},{10,... | collective-permute-start | bytes 786440 | tf_op jit(solution)/shard_map/ppermute | solution.py:446
  (44 other events, 397.2 us)

commit v2 on v1

v2 whole, which is shorter than its diff:
```python
import functools

import jax
import jax.numpy as jnp
import numpy as np
from jax import lax
from jax.experimental import pallas as pl
from jax.experimental.pallas import tpu as pltpu
from jax.sharding import PartitionSpec as P

HEAD_DIM = 64
MB = 2
EPSILON = 1e-05
HUGE_NEG = -1000000000.0
F32 = jnp.float32
BF16 = jnp.bfloat16
LANES = 128
VMEM_LIMIT = 56 * 1024 * 1024

ORDER_A = 0
ORDER_B = 1
ORDER_C = 2


def sinusoid(length, width):
    place = (length - 1 - np.arange(2 * length - 1)).astype(np.float32)
    index = np.arange(width // 2).astype(np.float32)
    rate = np.exp(index * np.float32(-2.0 * np.log(10000.0) / width)).astype(np.float32)
    angle = (place[:, None] * rate[None, :]).astype(np.float64)
    table = np.stack([np.sin(angle), np.cos(angle)], axis=-1).reshape(2 * length - 1, width)
    return np.pad(table, ((0, 1), (0, 0))).astype(np.float32)


def nn(a, b):
    return lax.dot_general(a, b, (((1,), (0,)), ((), ())), preferred_element_type=F32)


def nt(a, b):
    return lax.dot_general(a, b, (((1,), (1,)), ((), ())), preferred_element_type=F32)


def tn(a, b):
    return lax.dot_general(a, b, (((0,), (0,)), ((), ())), preferred_element_type=F32)


def ln_parts(v):
    centre = v - jnp.mean(v, axis=-1, keepdims=True)
    rstd = lax.rsqrt(jnp.mean(centre * centre, axis=-1, keepdims=True) + EPSILON)
    return centre * rstd, rstd


def ln(v, gain, shift):
    xhat, _ = ln_parts(v)
    return xhat * (1.0 + gain) + shift


def ln_back(v, gain, dy):
    xhat, rstd = ln_parts(v)
    g = dy * (1.0 + gain)
    dx = rstd * (
        g - jnp.mean(g, axis=-1, keepdims=True) - xhat * jnp.mean(g * xhat, axis=-1, keepdims=True)
    )
    return dx, rows_sum(dy * xhat), rows_sum(dy)


def rows_sum(v):
    return jnp.sum(v, axis=0, keepdims=True)


def sigmoid(v):
    return 1.0 / (1.0 + jnp.exp(-v))


def silu_slope(v):
    s = sigmoid(v)
    return s * (1.0 + v * (1.0 - s))


def bit_order(order, count):
    return [(order + k) % count for k in range(count)]


def slot_mask(slot, bits):
    out = 0
    for k, b in enumerate(bits):
        out |= ((slot >> k) & 1) << b
    return out


def owners(meta, order, dims):
    slots, tensor, half = dims
    bits = bit_order(order, slots.bit_length() - 1)
    me, core = meta[0], meta[1]
    out = []
    for slot in range(slots):
        f = me ^ slot_mask(slot, bits)
        plane, t = f // tensor, lax.rem(f, tensor)
        hi, at = divmod(slot, slots // 2)
        out.append((hi, at, core * half + plane, t))
        out.append((2 + hi, at, (1 - core) * half + plane, t))
    return out


def start_a(meta, srcs, dst, sem, order, dims):
    cols = srcs[0].shape[-1]
    rows = dst.shape[1] // (2 * dims[2])
    for which, at, d, t in owners(meta, order, dims):
        col = pl.ds(pl.multiple_of(t * cols, cols), cols)
        row = pl.ds(pl.multiple_of(d * rows, rows), rows)
        for k in range(2):
            pltpu.make_async_copy(
                srcs[which].at[at, pl.ds(k * rows, rows)], dst.at[k, row, col], sem).start()


def start_b(meta, srcs, dst, sem, order, dims, which_mats):
    rows, cols = srcs[0].shape[-2:]
    for which, at, d, t in owners(meta, order, dims):
        col = pl.ds(pl.multiple_of(t * cols, cols), cols)
        row = pl.ds(pl.multiple_of(d * rows, rows), rows)
        pltpu.make_async_copy(
            srcs[which].at[at, pl.ds(*which_mats)], dst.at[:, row, col], sem).start()


def wait_weights(dst, sem):
    pltpu.make_async_copy(dst, dst, sem).wait()


def head_mask(h):
    lane = lax.broadcasted_iota(jnp.int32, (1, LANES), 1)
    return (lane // HEAD_DIM) == h


def blk(i):
    return slice(i * LANES, (i + 1) * LANES)


VEC_MODEL, VEC_INNER, VEC_FF, VEC_ROWS = 0, 16, 56, 64


def lane_offsets(d, t, dims, width, hidden):
    slots, tensor, half = dims
    n = 2 * half
    w_small, w_ff = width // (n * tensor), hidden // (n * tensor)
    return (d * tensor + t) * w_small, (t * n + d) * w_small, (t * n + d) * w_ff


def prep_kernel(dims, rows, meta, *refs):
    srcs, (vm_ref, vi_ref, vf_ref, held, sem) = refs[:4], refs[4:]
    where = owners(meta, ORDER_A, dims)
    for i, (which, at, d, t) in enumerate(where):
        pltpu.make_async_copy(srcs[which].at[at, pl.ds(2 * rows, 16)], held.at[i], sem).start()
    wait_weights(held, sem)
    width, hidden = vm_ref.shape[1], vf_ref.shape[1]
    totals = None
    for i, (which, at, d, t) in enumerate(where):
        got = held[i].astype(F32)
        pieces = [got[:, blk(k)] for k in range(4)]
        model, inner, ff = pieces[0], jnp.concatenate(pieces[1:3] + [pieces[3][0:8]], axis=0), pieces[3][8:16]
        offs = lane_offsets(d, t, dims, width, hidden)
        placed = []
        for value, off, full in ((model, offs[0], width), (inner, offs[1], width), (ff, offs[2], hidden)):
            value = jnp.concatenate([value, jnp.zeros((value.shape[0], full - LANES), F32)], axis=1)
            placed.append(pltpu.roll(value, off, 1))
        totals = placed if totals is None else [a + b for a, b in zip(totals, placed)]
    vm_ref[...], vi_ref[...], vf_ref[...] = totals


def f1_kernel(dims, meta, xa_ref, xb_ref, vm_ref, vi_ref, vf_ref, pos_ref, a0, a1, a2, a3,
              b0, b1, b2, b3, s2_ref, filt_ref, stat_ref, s1_ref, before_ref, qu_ref, qv_ref, k_ref, v_ref,
              rel_ref, probs_ref, ctx_ref, gi_ref, gs_ref,
              wa, wb, pad, sems):
    start_a(meta, (a0, a1, a2, a3), wa, sems.at[0], ORDER_A, dims)
    start_b(meta, (b0, b1, b2, b3), wb, sems.at[1], ORDER_B, dims, (0, 8))
    length = meta[2]
    n_tok = xa_ref.shape[0]
    vm = lambda r: vm_ref[r:r + 1, :]
    vi = lambda r: vi_ref[r:r + 1, :]
    x = jnp.where(meta[3] == 1, xb_ref[...].astype(F32), xa_ref[...].astype(F32))
    wait_weights(wa, sems.at[0])
    n0 = ln(x, vm(0), vm(1)).astype(BF16)
    before = nn(n0, wa[0]) + vf_ref[0:1, :]
    before_ref[...] = before
    active = (before * sigmoid(before)).astype(BF16)
    s1 = x + 0.5 * (nt(active, wa[1]) + vm(2))
    s1_ref[...] = s1
    wait_weights(wb, sems.at[1])
    rel_ref[...] = nn(pos_ref[...], wb[4]).astype(BF16)
    n1 = ln(s1, vm(3), vm(4)).astype(BF16)
    q = nn(n1, wb[0]) + vi(0)
    qu_ref[...] = (q + vi(2)).astype(BF16)
    qv_ref[...] = (q + vi(3)).astype(BF16)
    k_ref[...] = nn(n1, wb[1]).astype(BF16)
    v_ref[...] = (nn(n1, wb[2]) + vi(1)).astype(BF16)
    keep = lax.broadcasted_iota(jnp.int32, (1, n_tok), 1) < length
    for i in range(qu_ref.shape[1] // LANES):
        qub, qvb, kb, vb = (r[:, blk(i)] for r in (qu_ref, qv_ref, k_ref, v_ref))
        rb = rel_ref[:, blk(i)]
        halves = []
        for h in range(2):
            mask = head_mask(h)
            direct = nt(jnp.where(mask, qub, 0), kb)
            table = nt(jnp.where(mask, qvb, 0), rb)
            shifted = pltpu.roll(table, n_tok + 1, 1, stride=1, stride_axis=0)[:, :n_tok]
            scores = jnp.where(keep, (direct + shifted) * HEAD_DIM ** (-0.5), HUGE_NEG)
            e = jnp.exp(scores - jnp.max(scores, axis=-1, keepdims=True))
            probs = e / jnp.sum(e, axis=-1, keepdims=True)
            probs_ref[2 * i + h] = probs
            halves.append(nn(probs.astype(BF16), vb))
        ctx_ref[:, blk(i)] = jnp.where(head_mask(0), halves[0], halves[1]).astype(BF16)
    s2 = s1 + nt(ctx_ref[...], wb[3]) + vm(5)
    s2_ref[...] = s2
    n2 = ln(s2, vm(6), vm(7)).astype(BF16)
    gi = nn(n2, wb[5]) + vi(4)
    gs = nn(n2, wb[6]) + vi(5)
    gi_ref[...] = gi
    gs_ref[...] = gs
    inside = (lax.broadcasted_iota(jnp.int32, (n_tok, 1), 0) < length).astype(F32)
    mixed = gi * sigmoid(gs) * inside
    taps = vi_ref.shape[0] - 9
    pad_store(pad, mixed)
    run_taps(pad, vi_ref, [8 + k for k in range(taps)], filt_ref)
    f = filt_ref[...]
    count = length.astype(F32)
    total = rows_sum(inside * f)
    centre = (f - total / count) * inside
    stat_ref[0:1, :] = total
    stat_ref[1:2, :] = rows_sum(centre * centre)
    stat_ref[2:3, :] = jnp.full_like(total, 1.0) * count
    stat_ref[3:8, :] = jnp.zeros((5, total.shape[1]), F32)


def pad_store(pad, value):
    rows = value.shape[0]
    pad[0:16, :] = jnp.zeros((16, value.shape[1]), F32)
    pad[16:16 + rows, :] = value
    pad[16 + rows:32 + rows, :] = jnp.zeros((16, value.shape[1]), F32)


def run_taps(pad, vi_ref, rows, out_ref):
    n_tok = out_ref.shape[0]
    wide = n_tok + 8
    for i in range(out_ref.shape[1] // LANES):
        total = None
        for s in range(8):
            part = None
            for q in range(4):
                e = 8 * q + s - 1
                if 0 <= e < len(rows):
                    term = vi_ref[rows[e]:rows[e] + 1, blk(i)] * pad[8 * q:8 * q + wide, blk(i)]
                    part = term if part is None else part + term
            moved = part[s:s + n_tok]
            total = moved if total is None else total + moved
        out_ref[:, blk(i)] = total


def each_group(refs):
    return [(r, g) for r in refs for g in range(r.shape[0])]


def bn_combine(refs):
    groups = each_group(refs)
    total = sum(r[g, 0:1, :] for r, g in groups)
    count = sum(r[g, 2:3, :] for r, g in groups)
    mean = total / count
    m2 = 0.0
    for r, g in groups:
        n_g = r[g, 2:3, :]
        off = r[g, 0:1, :] / n_g - mean
        m2 = m2 + r[g, 1:2, :] + n_g * off * off
    return mean, lax.rsqrt(m2 / count + EPSILON), count


def f2_kernel(dims, groups, meta, s2_ref, filt_ref, *refs):
    stats, refs = refs[:groups], refs[groups:]
    vm_ref, vi_ref, vf_ref, b0, b1, b2, b3, c0, c1, c2, c3 = refs[:11]
    out_ref, s3_ref, before_ref, s4_ref, bn_ref, wct, wc, sems = refs[11:]
    start_b(meta, (b0, b1, b2, b3), wct, sems.at[0], ORDER_B, dims, (7, 1))
    start_a(meta, (c0, c1, c2, c3), wc, sems.at[1], ORDER_C, dims)
    vm = lambda r: vm_ref[r:r + 1, :]
    vi = lambda r: vi_ref[r:r + 1, :]
    mean, inv, count = bn_combine(stats)
    bn_ref[0:1, :] = mean
    bn_ref[1:2, :] = inv
    bn_ref[2:3, :] = count
    bn_ref[3:8, :] = jnp.zeros((5, mean.shape[1]), F32)
    normal = (filt_ref[...] - mean) * inv * (1.0 + vi(6)) + vi(7)
    active = (normal * sigmoid(normal)).astype(BF16)
    wait_weights(wct, sems.at[0])
    s3 = s2_ref[...] + nt(active, wct[0]) + vm(8)
    s3_ref[...] = s3
    n3 = ln(s3, vm(9), vm(10)).astype(BF16)
    wait_weights(wc, sems.at[1])
    before = nn(n3, wc[0]) + vf_ref[1:2, :]
    before_ref[...] = before
    act = (before * sigmoid(before)).astype(BF16)
    s4 = s3 + 0.5 * (nt(act, wc[1]) + vm(11))
    s4_ref[...] = s4
    out_ref[...] = ln(s4, vm(12), vm(13)).astype(BF16)


def b1_kernel(dims, meta, ga_ref, gb_ref, s4_ref, s3_ref, before_ref, filt_ref, bn_ref, vm_ref,
              vi_ref, b0, b1, b2, b3, c0, c1, c2, c3,
              ds3_ref, dnorm_ref, sum_ref, n3_ref, db_ref, dl_ref, a_ref, dlc_ref, ac_ref,
              gm_ref, gi_ref, gf_ref, wct, wc, sems):
    start_a(meta, (c0, c1, c2, c3), wc, sems.at[1], ORDER_C, dims)
    start_b(meta, (b0, b1, b2, b3), wct, sems.at[0], ORDER_B, dims, (7, 1))
    vm = lambda r: vm_ref[r:r + 1, :]
    vi = lambda r: vi_ref[r:r + 1, :]
    g = jnp.where(meta[3] == 1, ga_ref[...].astype(F32), gb_ref[...].astype(F32))
    ds4, gain4, shift4 = ln_back(s4_ref[...], vm(12), g)
    delta = (0.5 * ds4).astype(BF16)
    dl_ref[...] = delta
    s3 = s3_ref[...]
    n3_ref[...] = ln(s3, vm(9), vm(10)).astype(BF16)
    before = before_ref[...]
    a_ref[...] = (before * sigmoid(before)).astype(BF16)
    wait_weights(wc, sems.at[1])
    db = (nn(delta, wc[1]) * silu_slope(before)).astype(BF16)
    db_ref[...] = db
    dn = nt(db, wc[0])
    dx, gain3, shift3 = ln_back(s3, vm(9), dn)
    ds3 = ds4 + dx
    ds3_ref[...] = ds3
    dlc = ds3.astype(BF16)
    dlc_ref[...] = dlc
    xhat = (filt_ref[...] - bn_ref[0:1, :]) * bn_ref[1:2, :]
    normal = xhat * (1.0 + vi(6)) + vi(7)
    ac_ref[...] = (normal * sigmoid(normal)).astype(BF16)
    wait_weights(wct, sems.at[0])
    dnorm = nn(dlc, wct[0]) * silu_slope(normal)
    dnorm_ref[...] = dnorm
    u6 = rows_sum(dnorm * xhat)
    u7 = rows_sum(dnorm)
    sum_ref[0:1, :] = u7 * (1.0 + vi(6))
    sum_ref[1:2, :] = u6 * (1.0 + vi(6))
    sum_ref[2:8, :] = jnp.zeros((6, u6.shape[1]), F32)
    gm_ref[0:1, :] = rows_sum(dlc.astype(F32))
    gm_ref[1:2, :] = gain3
    gm_ref[2:3, :] = shift3
    gm_ref[3:4, :] = rows_sum(delta.astype(F32))
    gm_ref[4:5, :] = gain4
    gm_ref[5:6, :] = shift4
    gm_ref[6:8, :] = jnp.zeros((2, u6.shape[1]), F32)
    gi_ref[0:1, :] = u6
    gi_ref[1:2, :] = u7
    gi_ref[2:8, :] = jnp.zeros((6, u6.shape[1]), F32)
    gf_ref[...] = rows_sum(db.astype(F32))


def b2_kernel(dims, groups, meta, ds3_ref, dnorm_ref, *refs):
    sums, refs = refs[:groups], refs[groups:]
    (filt_ref, bn_ref, gin_ref, gsig_ref, s2_ref, s1_ref, qu_ref, qv_ref, k_ref, v_ref, rel_ref,
     probs_ref, gm1_ref, gi1_ref, vm_ref, vi_ref, b0, b1, b2, b3) = refs[:20]
    (ds1_ref, n2_ref, dgi_ref, dgs_ref, dla_ref, n1_ref, dq_ref, dk_ref, dv_ref, drel_ref,
     gm_ref, gi_ref, wb, pad_m, pad_d, dmix, sem) = refs[20:]
    start_b(meta, (b0, b1, b2, b3), wb, sem, ORDER_B, dims, (0, 8))
    length = meta[2]
    n_tok, width = ds3_ref.shape
    vm = lambda r: vm_ref[r:r + 1, :]
    vi = lambda r: vi_ref[r:r + 1, :]
    plain = sum(r[g, 0:1, :] for r, g in each_group(sums))
    tilted = sum(r[g, 1:2, :] for r, g in each_group(sums))
    inv = bn_ref[1:2, :]
    xhat = (filt_ref[...] - bn_ref[0:1, :]) * inv
    inside = (lax.broadcasted_iota(jnp.int32, (n_tok, 1), 0) < length).astype(F32)
    dfilt = inv * (
        dnorm_ref[...] * (1.0 + vi(6)) - inside / bn_ref[2:3, :] * (plain + xhat * tilted)
    )
    gin = gin_ref[...]
    sig = sigmoid(gsig_ref[...])
    taps = vi_ref.shape[0] - 9
    pad_store(pad_m, gin * sig * inside)
    pad_store(pad_d, dfilt)
    run_taps(pad_d, vi_ref, [8 + taps - 1 - e for e in range(taps)], dmix)
    wide = n_tok + 8
    for i in range(width // LANES):
        for s in range(8):
            moved = pad_d[16 - s:16 - s + wide, blk(i)]
            for q in range(4):
                e = 8 * q + s - 1
                if 0 <= e < taps:
                    gi_ref[8 + e:9 + e, blk(i)] = rows_sum(
                        moved * pad_m[8 * q:8 * q + wide, blk(i)]
                    )
    dm = dmix[...] * inside
    dgi = (dm * sig).astype(BF16)
    dgs = (dm * gin * sig * (1.0 - sig)).astype(BF16)
    dgi_ref[...] = dgi
    dgs_ref[...] = dgs
    wait_weights(wb, sem)
    s2 = s2_ref[...]
    n2_ref[...] = ln(s2, vm(6), vm(7)).astype(BF16)
    dx, gain, shift = ln_back(s2, vm(6), nt(dgi, wb[5]) + nt(dgs, wb[6]))
    gm_ref[6:7, :] = gain
    gm_ref[7:8, :] = shift
    ds2 = ds3_ref[...] + dx
    dla = ds2.astype(BF16)
    dla_ref[...] = dla
    dctx = nn(dla, wb[3]).astype(BF16)
    row = lax.broadcasted_iota(jnp.int32, (n_tok, n_tok), 0)
    col = lax.broadcasted_iota(jnp.int32, (n_tok, n_tok), 1)
    flip = (row + col == n_tok - 1).astype(F32).astype(BF16)
    for i in range(width // LANES):
        qub, qvb, kb, vb = (r[:, blk(i)] for r in (qu_ref, qv_ref, k_ref, v_ref))
        rb = rel_ref[:, blk(i)]
        dcb = dctx[:, blk(i)]
        got = []
        for h in range(2):
            mask = head_mask(h)
            probs = probs_ref[2 * i + h]
            dprobs = nt(jnp.where(mask, dcb, 0), vb)
            dvh = tn(probs.astype(BF16), dcb)
            ds = probs * (dprobs - jnp.sum(probs * dprobs, axis=-1, keepdims=True))
            ds = (ds.astype(BF16).astype(F32) * HEAD_DIM ** (-0.5)).astype(BF16)
            turned = jnp.concatenate([nn(flip, ds), jnp.zeros((n_tok, n_tok), F32)], axis=1)
            turned = pltpu.roll(turned, 0, 1, stride=1, stride_axis=0).astype(BF16)
            dr = nn(flip, turned).astype(BF16)
            got.append((nn(ds, kb), nn(dr, rb), tn(ds, qub), dvh, tn(dr, qvb)))
        first = head_mask(0)
        dqu, dqv, dk, dv, drel = (jnp.where(first, a, b) for a, b in zip(*got))
        dq = (dqu + dqv).astype(BF16)
        dvb = dv.astype(BF16)
        dq_ref[:, blk(i)] = dq
        dk_ref[:, blk(i)] = dk.astype(BF16)
        dv_ref[:, blk(i)] = dvb
        drel_ref[:, blk(i)] = drel.astype(BF16)
        gi_ref[0:1, blk(i)] = rows_sum(dq.astype(F32))
        gi_ref[1:2, blk(i)] = rows_sum(dvb.astype(F32))
        gi_ref[2:3, blk(i)] = rows_sum(dqu)
        gi_ref[3:4, blk(i)] = rows_sum(dqv)
    gi_ref[4:5, :] = rows_sum(dgi.astype(F32))
    gi_ref[5:6, :] = rows_sum(dgs.astype(F32))
    gi_ref[6:8, :] = gi1_ref[0:2, :]
    gi_ref[8 + taps:40, :] = jnp.zeros((40 - 8 - taps, width), F32)
    gm_ref[0:3, :] = jnp.zeros((3, width), F32)
    gm_ref[8:16, :] = gm1_ref[...]
    s1 = s1_ref[...]
    n1_ref[...] = ln(s1, vm(3), vm(4)).astype(BF16)
    dn = nt(dq_ref[...], wb[0]) + nt(dk_ref[...], wb[1]) + nt(dv_ref[...], wb[2])
    dx, gain, shift = ln_back(s1, vm(3), dn)
    gm_ref[3:4, :] = gain
    gm_ref[4:5, :] = shift
    gm_ref[5:6, :] = rows_sum(dla.astype(F32))
    ds1_ref[...] = ds2 + dx


def b3_kernel(dims, meta, ds1_ref, xa_ref, xb_ref, before_ref, vm_ref, a0, a1, a2, a3,
              dx_ref, n0_ref, db_ref, dl_ref, a_ref, gm_ref, gf_ref, wa, sem):
    start_a(meta, (a0, a1, a2, a3), wa, sem, ORDER_A, dims)
    vm = lambda r: vm_ref[r:r + 1, :]
    ds1 = ds1_ref[...]
    delta = (0.5 * ds1).astype(BF16)
    dl_ref[...] = delta
    before = before_ref[...]
    a_ref[...] = (before * sigmoid(before)).astype(BF16)
    slope = silu_slope(before)
    x = jnp.where(meta[3] == 1, xb_ref[...].astype(F32), xa_ref[...].astype(F32))
    n0_ref[...] = ln(x, vm(0), vm(1)).astype(BF16)
    wait_weights(wa, sem)
    db = (nn(delta, wa[1]) * slope).astype(BF16)
    db_ref[...] = db
    dx, gain, shift = ln_back(x, vm(0), nt(db, wa[0]))
    gm_ref[0:1, :] = gain
    gm_ref[1:2, :] = shift
    gm_ref[2:3, :] = rows_sum(delta.astype(F32))
    gm_ref[3:8, :] = jnp.zeros((5, gain.shape[1]), F32)
    gf_ref[...] = rows_sum(db.astype(F32))
    dx_ref[...] = (ds1 + dx).astype(BF16)


def pieces_of(slots):
    out, top = [], slots
    while top > 1:
        out.append(range(top // 2, top))
        top //= 2
    return out + [range(0, 1)]


def w_kernel(dims, order, count, vectors, meta, *refs):
    slots, tensor, half = dims
    ins, refs = refs[:2 * count], refs[2 * count:]
    vecs, refs = refs[:vectors], refs[vectors:]
    outs, grad = refs[:-1], refs[-1]
    bits = bit_order(order, slots.bit_length() - 1)
    me, core = meta[0], meta[1]
    flat_rows = len(outs[0].shape) == 3
    cols = outs[0].shape[-1]
    rows = ins[0].shape[1] // (2 * half)
    mine = half * rows
    for i in range(count):
        part = ins[2 * i][:, pl.ds(pl.multiple_of(core * mine, mine), mine)]
        grad[i] = tn(part, ins[2 * i + 1][...])
    for out, piece in zip(outs, pieces_of(slots)):
        for at, slot in enumerate(piece):
            f = me ^ slot_mask(slot, bits)
            plane, t = f // tensor, lax.rem(f, tensor)
            row = pl.ds(pl.multiple_of(plane * rows, rows), rows)
            col = pl.ds(pl.multiple_of(t * cols, cols), cols)
            for i in range(count):
                block = grad[i, row, col].astype(BF16)
                if flat_rows:
                    out[at, i * rows:(i + 1) * rows, :] = block
                else:
                    out[at, i] = block
            if vectors:
                gm2_ref, gm0_ref, gi_ref, gf0_ref, gf1_ref = vecs
                width, hidden = gm2_ref.shape[1], gf0_ref.shape[1]
                offs = lane_offsets(core * half + plane, t, dims, width, hidden)
                model = gm2_ref[...] + jnp.concatenate(
                    [gm0_ref[...], jnp.zeros((8, width), F32)], axis=0)
                ff = jnp.concatenate(
                    [gf0_ref[...], gf1_ref[...], jnp.zeros((6, hidden), F32)], axis=0)
                moved = [
                    pltpu.roll(v, v.shape[1] - off, 1)[:, :LANES]
                    for v, off in ((model, offs[0]), (gi_ref[...], offs[1]), (ff, offs[2]))
                ]
                tail = jnp.concatenate([moved[1][32:40], moved[2]], axis=0)
                out[at, count * rows:count * rows + 16, :] = jnp.concatenate(
                    [moved[0], moved[1][0:16], moved[1][16:32], tail], axis=1).astype(BF16)


def vmem(*shape):
    return pl.BlockSpec(memory_space=pltpu.VMEM)


def call(kernel, ins, outs, scratch=(), any_from=None, flops=0, name=None):
    specs = [pl.BlockSpec(memory_space=pltpu.SMEM)]
    for i in range(1, len(ins)):
        away = any_from is not None and i >= any_from
        specs.append(pl.BlockSpec(memory_space=pl.ANY if away else pltpu.VMEM))
    nbytes = sum(a.size * a.dtype.itemsize for a in ins)
    return pl.pallas_call(
        kernel,
        out_shape=[jax.ShapeDtypeStruct(s, d) for s, d in outs],
        in_specs=specs,
        out_specs=[pl.BlockSpec(memory_space=pltpu.VMEM) for _ in outs],
        scratch_shapes=list(scratch),
        compiler_params=pltpu.CompilerParams(vmem_limit_bytes=VMEM_LIMIT),
        cost_estimate=pl.CostEstimate(flops=flops, bytes_accessed=nbytes, transcendentals=0),
        name=name,
    )(*ins)


def permute(value, pairs):
    return lax.ppermute(value, ("pipe", "dp", "tensor"), pairs)


def per_device(n, tensor, boundary, lengths, batch_of, mats, ffw, vec_model, vec_inner, vec_ff):
    half = n // 2
    slots = half * tensor
    nbits = slots.bit_length() - 1
    dims = (slots, tensor, half)
    core = lax.axis_index("pipe")
    d = lax.axis_index("dp")
    t = lax.axis_index("tensor")
    upper = d // half
    plane = lax.rem(d, half)
    me = plane * tensor + t
    is_upper = upper == 1

    def flat(c, dd, tt):
        return (c * n + dd) * tensor + tt

    everyone = [(c, dd, tt) for c in range(2) for dd in range(n) for tt in range(tensor)]

    def home(c, dd, tt):
        u = dd // half
        return (c, dd, tt) if c == u else (1 - c, dd + half if u == 0 else dd - half, tt)

    swap_pairs = [(flat(*e), flat(*home(*e))) for e in everyone]
    core_pairs = [(flat(c, dd, tt), flat(1 - c, dd, tt)) for c, dd, tt in everyone]

    def bit_pairs(b):
        out = []
        for c, dd, tt in everyone:
            f = ((dd % half) * tensor + tt) ^ (1 << b)
            out.append((flat(c, dd, tt), flat(c, dd // half * half + f // tensor, f % tensor)))
        return out

    def gather(block, order):
        held = permute(block, swap_pairs)[None]
        order = bit_order(order, nbits)
        for b in order[:-1]:
            held = jnp.concatenate([held, permute(held, bit_pairs(b))], axis=0)
        far = permute(held, bit_pairs(order[-1]))
        return [held, far, permute(held, core_pairs), permute(far, core_pairs)]

    ends = boundary[0]
    rows_here, width = ends.shape[1], ends.shape[2]
    length_all = rows_here * tensor
    side, micro = lax.rem(t, 2), t // 2
    first_is = batch_of[0] == 0

    there, back = [], []
    for k in range(2):
        pairs = []
        for h in range(2):
            for dd in range(n):
                for tt in range(tensor):
                    s = dd // half
                    j = (s ^ (tt & 1)) + 2 * k
                    pairs.append((flat(h, dd, tt), flat(j & 1, h * half + dd % half, tt ^ j)))
        there.append(pairs)
        back.append([(b, a) for a, b in pairs])

    ordered = jnp.where(first_is, ends, ends[::-1])
    len_ordered = jnp.where(first_is, lengths, lengths[::-1]).astype(BF16)
    parcels = jnp.concatenate(
        [ordered, jnp.broadcast_to(len_ordered[:, None, None], (MB, 16, width))], axis=1)
    sends = jnp.where(micro == 0, parcels, parcels[::-1])
    arrived = jnp.stack([permute(sends[k], there[k]) for k in range(2)])
    others = permute(arrived, core_pairs)
    both = jnp.where(core == 0, jnp.stack([arrived, others], 1), jnp.stack([others, arrived], 1))
    both = jnp.where(lax.rem(t, 2) == 0, both, both[:, ::-1])
    both = jnp.where(micro == 0, both, both[::-1])
    x0 = both[:, :, :rows_here].reshape(length_all, width)
    my_length = both[0, 0, rows_here, 0].astype(jnp.int32)
    meta = jnp.stack([me, core, my_length, upper]).astype(jnp.int32)
    pos = jnp.asarray(sinusoid(length_all, width)).astype(BF16)

    def lanes(v):
        return jnp.pad(v[0], ((0, 0), (0, LANES - v.shape[2])))

    vec = jnp.concatenate([
        jnp.pad(lanes(vec_model), ((0, VEC_INNER - vec_model.shape[1]), (0, 0))),
        jnp.pad(lanes(vec_inner), ((0, VEC_FF - VEC_INNER - vec_inner.shape[1]), (0, 0))),
        jnp.pad(lanes(vec_ff), ((0, VEC_ROWS - VEC_FF - vec_ff.shape[1]), (0, 0)))], axis=0)
    vec = vec.reshape(4, 16, LANES).transpose(1, 0, 2).reshape(16, 4 * LANES)
    rows, fcols, mcols = ffw.shape[2], ffw.shape[3], mats.shape[3]
    a_all = gather(jnp.concatenate([ffw[0, 0:2].reshape(2 * rows, fcols), vec], axis=0), ORDER_A)
    b_all = gather(mats[0], ORDER_B)
    c_all = gather(ffw[0, 2:4].reshape(2 * rows, fcols), ORDER_C)

    hidden = fcols * tensor
    heads = width // HEAD_DIM
    L, D, H = length_all, width, hidden
    wa_s = pltpu.VMEM((2, D, H), BF16)
    wb_s = pltpu.VMEM((8, D, D), BF16)
    wct_s = pltpu.VMEM((1, D, D), BF16)
    sem_s = pltpu.SemaphoreType.DMA
    sems = pltpu.SemaphoreType.DMA((2,))
    pad_s = pltpu.VMEM((L + 32, D), F32)
    mat_flops = 2 * L * D * D

    vm, vi, vf = call(
        functools.partial(prep_kernel, dims, rows), [meta] + a_all,
        [((16, D), F32), ((40, D), F32), ((8, H), F32)],
        [pltpu.VMEM((2 * slots, 16, 4 * LANES), BF16), sem_s], 1, 0, "vectors",
    )

    def f1(xa, xb):
        return call(
            functools.partial(f1_kernel, dims),
            [meta, xa, xb, vm, vi, vf, pos] + a_all + b_all,
            [((L, D), F32), ((L, D), F32), ((8, D), F32), ((L, D), F32), ((L, H), F32)]
            + [((L, D), BF16)] * 4
            + [((2 * L, D), BF16), ((heads, L, L), F32), ((L, D), BF16), ((L, D), F32), ((L, D), F32)],
            [wa_s, wb_s, pad_s, sems], 7, 15 * mat_flops, "layer_front",
        )

    def f2(s2, filt, stats):
        return call(
            functools.partial(f2_kernel, dims, len(stats)),
            [meta, s2, filt] + stats + [vm, vi, vf] + b_all + c_all,
            [((L, D), BF16), ((L, D), F32), ((L, H), F32), ((L, D), F32), ((8, D), F32)],
            [wct_s, wa_s, sems], 6 + len(stats), 9 * mat_flops, "layer_rear",
        )

    def b1(ga, gb, s4, s3, before, filt, bn):
        return call(
            functools.partial(b1_kernel, dims),
            [meta, ga, gb, s4, s3, before, filt, bn, vm, vi] + b_all + c_all,
            [((L, D), F32), ((L, D), F32), ((8, D), F32), ((L, D), BF16), ((L, H), BF16),
             ((L, D), BF16), ((L, H), BF16), ((L, D), BF16), ((L, D), BF16),
             ((8, D), F32), ((8, D), F32), ((1, H), F32)],
            [wct_s, wa_s, sems], 10, 9 * mat_flops, "back_rear",
        )

    def b2(ds3, dnorm, sums, *rest):
        ins = [meta, ds3, dnorm] + sums + list(rest) + [vm, vi]
        return call(
            functools.partial(b2_kernel, dims, len(sums)), ins + b_all,
            [((L, D), F32)] + [((L, D), BF16)] * 8
            + [((2 * L, D), BF16), ((16, D), F32), ((40, D), F32)],
            [wb_s, pad_s, pad_s, pltpu.VMEM((L, D), F32), sem_s], len(ins), 16 * mat_flops,
            "back_front",
        )

    def b3(ds1, xa, xb, before):
        return call(
            functools.partial(b3_kernel, dims), [meta, ds1, xa, xb, before, vm] + a_all,
            [((L, D), BF16), ((L, D), BF16), ((L, H), BF16), ((L, D), BF16), ((L, H), BF16),
             ((8, D), F32), ((1, H), F32)],
            [wa_s, sem_s], 6, 8 * mat_flops, "back_first",
        )

    def w(order, pairs, cols, is_ff, vecs=()):
        count = len(pairs)
        if is_ff:
            shape = (count * rows + (16 if vecs else 0), cols)
        else:
            shape = (count, rows, cols)
        return call(
            functools.partial(w_kernel, dims, order, count, len(vecs)),
            [meta] + [a for pair in pairs for a in pair] + list(vecs),
            [((len(p),) + shape, BF16) for p in pieces_of(slots)],
            [pltpu.VMEM((count, half * rows, cols * tensor), F32)], None, 4 * mat_flops,
            "weight_grads",
        )

    norm_bits = [0] + list(range(tensor.bit_length() - 1, nbits))

    def mask_pairs(mask):
        out = []
        for c, dd, tt in everyone:
            f = ((dd % half) * tensor + tt) ^ mask
            out.append((flat(c, dd, tt), flat(c, dd // half * half + f // tensor, f % tensor)))
        return out

    def norm_group(value):
        held = value[None]
        for first in range(0, len(norm_bits), 2):
            masks = [0]
            for b in norm_bits[first:first + 2]:
                masks = masks + [m ^ (1 << b) for m in masks]
            parts = [held] + [permute(held, mask_pairs(m)) for m in masks[1:]]
            if first + 2 < len(norm_bits):
                held = jnp.concatenate(parts, axis=0)
        return parts

    up_pairs = [(flat(c, dd, tt), flat(c, dd + half, tt)) for c, dd, tt in everyone if dd < half]
    down_pairs = [(b, a) for a, b in up_pairs]

    def forward(xa, xb):
        front = f1(xa, xb)
        stats = norm_group(front[2])
        return front, f2(front[0], front[1], stats)

    front, rear = forward(x0, x0)
    middle = permute(rear[0], up_pairs)
    front, rear = forward(x0, middle)
    (s2, filt, _, s1, before0, qu, qv, k, v, rel, probs, ctx, gin, gsig) = front
    made, s3, before1, s4, bn = rear

    def backward(gb):
        part1 = b1(x0, gb, s4, s3, before1, filt, bn)
        sums = norm_group(part1[2])
        part2 = b2(part1[0], part1[1], sums, filt, bn, gin, gsig, s2, s1, qu, qv, k, v, rel, probs,
                   part1[9], part1[10])
        return part1, part2

    part1, part2 = backward(x0)
    d_middle = permute(b3(part2[0], x0, middle, before0)[0], down_pairs)
    part1, part2 = backward(d_middle)
    (_, _, _, n3, db1, dl3, a1, dlc, ac, _, _, gf1) = part1
    (ds1, n2, dgi, dgs, dla, n1, dq, dk, dv, drel, gm2, gi2) = part2

    def scatter(sent, order):
        got = []
        for piece, b in zip(sent[:-1], reversed(bit_order(order, nbits))):
            size = piece.shape[0]
            for g in got:
                piece = piece.astype(F32) + g[size:2 * size].astype(F32)
            got.append(permute(piece.astype(BF16), bit_pairs(b)))
        total = sent[-1][0].astype(F32)
        for g in got:
            total = total + g[0].astype(F32)
        return permute(total.astype(BF16), swap_pairs)

    grad_c = scatter(w(ORDER_C, [(n3, db1), (dl3, a1)], fcols, True), ORDER_C)
    pieces_b = list(w(ORDER_B, [(n1, dq), (n1, dk), (n1, dv), (dla, ctx), (pos, drel), (n2, dgi),
                                (n2, dgs), (dlc, ac)], mcols, False))
    ds1, pieces_b[0] = lax.optimization_barrier((ds1, pieces_b[0]))
    dx, n0, db0, dl0, a0, gm0, gf0 = b3(ds1, x0, middle, before0)
    grad_b = scatter(pieces_b, ORDER_B)
    grad_a = scatter(w(ORDER_A, [(n0, db0), (dl0, a0)], fcols, True, (gm2, gm0, gi2, gf0, gf1)),
                     ORDER_A)

    stream = jnp.where(is_upper, made, dx).reshape(tensor, rows_here, width)
    pair = jnp.stack([
        permute(lax.dynamic_index_in_dim(stream, t ^ (core + 2 * k), 0, keepdims=False), back[k])
        for k in range(2)])
    pair = jnp.where(micro == 0, pair, pair[::-1])
    ends_out = jnp.where(first_is, pair, pair[::-1])[None]

    grad_a = grad_a.astype(F32)
    gv = grad_a[2 * rows:]
    small = vec_model.shape[2]
    gvi = jnp.concatenate([gv[:, LANES:LANES + small], gv[:, 2 * LANES:2 * LANES + small],
                           gv[:8, 3 * LANES:3 * LANES + small]], axis=0)
    grad_f = jnp.concatenate([grad_a[:2 * rows].reshape(2, rows, fcols),
                              grad_c.astype(F32).reshape(2, rows, fcols)], axis=0)
    return (
        ends_out,
        grad_b.astype(F32)[None],
        grad_f[None],
        gv[:vec_model.shape[1], :small][None],
        gvi[:vec_inner.shape[1]][None],
        gv[8:8 + vec_ff.shape[1], 3 * LANES:3 * LANES + vec_ff.shape[2]][None],
    )


def solution(mesh):
    return jax.shard_map(
        functools.partial(per_device, mesh.shape["dp"], mesh.shape["tensor"]),
        mesh=mesh,
        in_specs=(
            P("pipe", "dp", "tensor", None),
            P("dp"),
            P("dp"),
            P("pipe", None, "dp", "tensor"),
            P("pipe", None, "dp", "tensor"),
            P("pipe", None, ("dp", "tensor")),
            P("pipe", None, ("tensor", "dp")),
            P("pipe", None, ("tensor", "dp")),
        ),
        out_specs=(
            P("pipe", "dp", "tensor", None),
            P("pipe", None, "dp", "tensor"),
            P("pipe", None, "dp", "tensor"),
            P("pipe", None, ("dp", "tensor")),
            P("pipe", None, ("tensor", "dp")),
            P("pipe", None, ("tensor", "dp")),
        ),
        check_vma=False,
    )
```

time: 352 us -> 298 us (0.85)
  waiting for transfers between devices: 102 us -> 60.5 us
  other arithmetic: 43.4 us -> 13.6 us
  starting transfers between devices: 78.7 us -> 104 us
  local copies, waits for them, and re-layouts: 25.8 us -> 9.97 us
  Pallas kernels: 93.3 us -> 105 us
    ppermute x50 -> x49, waiting for transfers between devices: 102 us -> 60.5 us  [permute(): return lax.ppermute(value, ('pipe', 'dp', 'tensor'), pairs)]
    ppermute x50 -> x49, starting transfers between devices: 78.7 us -> 104 us  [permute(): return lax.ppermute(value, ('pipe', 'dp', 'tensor'), pairs)]
    pallas_call x11 -> x14, Pallas kernels: 93.3 us -> 105 us  [call(): pl.pallas_call(kernel, out_shape=[jax.ShapeDtypeStruct(s, d) for s, d in...]
    slice x21 -> x7, local copies, waits for them, and re-layouts: 12.1 us -> 2.31 us  [the longest x1 1.07 us: per_device(): c_all = gather(ffw[0, 2:4].reshape(2 * rows, fcols), ORDER_C)]
    another operation x5 -> x2, other arithmetic: 8.81 us -> 0.02 us  [the longest x1 0.01 us: per_device(): jnp.stack([arrived, others], 1)]
    concatenate x12 -> x3, other arithmetic: 7.61 us -> 0.75 us  [the longest x1 0.72 us: per_device(): jnp.concatenate([jnp.pad(lanes(vec_model), ((0, VEC_INNER - vec_model.sha...]
    unnamed x39 -> x65, local copies, waits for them, and re-layouts: 1.56 us -> 6.89 us
    select_n x12 -> x5, other arithmetic: 5.3 us -> 0.13 us  [the longest x1 0.04 us: per_device(): both = jnp.where(lax.rem(t, 2) == 0, both, both[:, ::-1])]
  transfers between devices with their start and end apart: 50 -> 49, of which waited for: 25 -> 26; matrix products, arithmetic and copies ran while one was open for 18% -> 5% of each run, Pallas kernels for 10% -> 13%
where the time goes in v2:
time: 298 us; the launch traced here: 295 us
  Pallas kernels  105 us (35%)
  starting transfers between devices  104 us (35%)
  waiting for transfers between devices  60.5 us (20%)
  other arithmetic  13.6 us (5%)
  local copies, waits for them, and re-layouts  9.97 us (3%)
    pallas_call x14, Pallas kernels, call(): pl.pallas_call(kernel, out_shape=[jax.ShapeDtypeStruct(s, d) for s, d in...  105 us
    ppermute x49, starting transfers between devices, permute(): return lax.ppermute(value, ('pipe', 'dp', 'tensor'), pairs)  104 us
    ppermute x49, waiting for transfers between devices, permute(): return lax.ppermute(value, ('pipe', 'dp', 'tensor'), pairs)  60.5 us
    concatenate x6, other arithmetic, gather(): held = jnp.concatenate([held, permute(held, bit_pairs(b))], axis=0)  7.16 us
    unnamed x65, local copies, waits for them, and re-layouts  6.89 us
  transfers between devices with their start and end apart: 49, of which 26 were waited for; matrix products, arithmetic and copies ran while one was open for 5% of the time, Pallas kernels for 13%

profile of v2, /device:TPU:1, one launch (start us, length us, event | category | flops | bytes accessed | tf_op | source)
XLA Modules:
  0.0 295.5 jit_solution(2268000156662801016)
XLA Ops:
  0.6 5.6 %collective-permute-start.9 = (bf16[8,128,128]{2,1,0:T(8,128)(2,1)}, bf16[8,128,128]{2,1,0:T(8,128)(2,1)S(1)}, u32[]{:S(2)}, u32[]{:S(2)}) collective-permute-start(bf16[8,128,128]{2,1,0:T(8,128)(2,1)} %bitcast.116), channel_id=1, source_target_pairs={{0,0},{1,1},{2,2},{3,3},{4,4},{5,5},{6,6},{7,7},{8,16},{9,17},{10,... | collective-permute-start | bytes 786440 | tf_op jit(solution)/shard_map/ppermute | solution.py:545
  10.8 4.5 %collective-permute-start.18 = (bf16[256,512]{1,0:T(8,128)(2,1)S(1)}, bf16[256,512]{1,0:T(8,128)(2,1)S(1)}, u32[]{:S(2)}, u32[]{:S(2)}) collective-permute-start(bf16[256,512]{1,0:T(8,128)(2,1)S(1)} %bitcast.88), channel_id=1, source_target_pairs={{0,0},{1,1},{2,2},{3,3},{4,4},{5,5},{6,6},{7,7},{8,16},{9,17},{10,... | collective-permute-start | bytes 786440 | tf_op jit(solution)/shard_map/ppermute | solution.py:545
  34.4 4.3 %collective-permute-done.11 = bf16[2,8,128,128]{3,2,1,0:T(8,128)(2,1)} collective-permute-done((bf16[2,8,128,128]{3,2,1,0:T(8,128)(2,1)S(1)}, bf16[2,8,128,128]{3,2,1,0:T(8,128)(2,1)}, u32[]{:S(2)}, u32[]{:S(2)}) %collective-permute-start.11) | collective-permute-done | bytes 524320 | tf_op jit(solution)/shard_map/ppermute | solution.py:545
  50.3 4.9 %collective-permute-start = (bf16[48,512]{1,0:T(8,128)(2,1)S(1)}, bf16[48,512]{1,0:T(8,128)(2,1)S(1)}, u32[]{:S(2)}, u32[]{:S(2)}) collective-permute-start(bf16[48,512]{1,0:T(8,128)(2,1)S(1)} %get-tuple-element.182), channel_id=1, source_target_pairs={{0,0},{1,16},{2,2},{3,18},{4,4},{5,20},{6,6},{7,22},{8,17},{9,1},{... | collective-permute-start | bytes 147464 | tf_op jit(solution)/shard_map/ppermute | solution.py:545
  55.2 5.8 %collective-permute-done = bf16[48,512]{1,0:T(8,128)(2,1)S(1)} collective-permute-done((bf16[48,512]{1,0:T(8,128)(2,1)S(1)}, bf16[48,512]{1,0:T(8,128)(2,1)S(1)}, u32[]{:S(2)}, u32[]{:S(2)}) %collective-permute-start) | collective-permute-done | bytes 49184 | tf_op jit(solution)/shard_map/ppermute | solution.py:545
  74.2 10.4 %layer_front.2 = (f32[128,512]{1,0:T(8,128)}, f32[128,512]{1,0:T(8,128)}, f32[8,512]{1,0:T(8,128)}, f32[128,512]{1,0:T(8,128)}, f32[128,2048]{1,0:T(8,128)}, /*i...) custom-call(s32[4]{0:T(128)} %pad_add_fusion.meta, ...), custom_call_target="tpu_custom_call" | custom-call | flops 1006632960 | bytes 9355280 | tf_op jit(solution)/shard_map/layer_front/pallas_call | solution.py:532
  84.6 5.4 %collective-permute-start.17 = (f32[1,8,512]{2,1,0:T(8,128)}, f32[1,8,512]{2,1,0:T(8,128)S(1)}, u32[]{:S(2)}, u32[]{:S(2)}) collective-permute-start(f32[1,8,512]{2,1,0:T(8,128)} %bitcast.102), channel_id=1, source_target_pairs={{0,5},{1,4},{2,7},{3,6},{4,1},{5,0},{6,3},{7,2},{8,13},{9,12},{10,... | collective-permute-start | bytes 49160 | tf_op jit(solution)/shard_map/ppermute | solution.py:545
  93.4 5.6 %layer_rear.2 = (bf16[128,512]{1,0:T(8,128)(2,1)}, f32[128,512]{1,0:T(8,128)}, f32[128,2048]{1,0:T(8,128)}, f32[128,512]{1,0:T(8,128)}, f32[8,512]{1,0:T(8,128)}) custom-call(s32[4]{0:T(128)} %pad_add_fusion.meta, f32[128,512]{1,0:T(8,128)} %get-tuple-element.87.s2_ref, f32[128,512]{1,0:T(8,128)} %get-tuple-element.88.filt_ref, f32[1,8,512]{2,1,0:T(8,128)} %bitcast.105, ...), custom_call_target="tpu_custom_call" | custom-call | flops 603979776 | bytes 9158672 | tf_op jit(solution)/shard_map/layer_rear/pallas_call | solution.py:532
  104.2 10.4 %layer_front.3 = (f32[128,512]{1,0:T(8,128)}, f32[128,512]{1,0:T(8,128)}, f32[8,512]{1,0:T(8,128)}, f32[128,512]{1,0:T(8,128)}, f32[128,2048]{1,0:T(8,128)}, /*i...) custom-call(s32[4]{0:T(128)} %pad_add_fusion.meta, ...), custom_call_target="tpu_custom_call" | custom-call | flops 1006632960 | bytes 9355280 | tf_op jit(solution)/shard_map/layer_front/pallas_call | solution.py:532
  121.9 5.6 %layer_rear.3 = (bf16[128,512]{1,0:T(8,128)(2,1)}, f32[128,512]{1,0:T(8,128)}, f32[128,2048]{1,0:T(8,128)}, f32[128,512]{1,0:T(8,128)}, f32[8,512]{1,0:T(8,128)}) custom-call(s32[4]{0:T(128)} %pad_add_fusion.meta, f32[128,512]{1,0:T(8,128)} %get-tuple-element.91.s2_ref.refs_8_, f32[128,512]{1,0:T(8,128)} %get-tuple-element.92.filt_ref.refs_4_, ...), custom_call_target="tpu_custom_call" | custom-call | flops 603979776 | bytes 9158672 | tf_op jit(solution)/shard_map/layer_rear/pallas_call | solution.py:532
  127.6 6.6 %back_rear.2 = (f32[128,512]{1,0:T(8,128)}, f32[128,512]{1,0:T(8,128)}, f32[8,512]{1,0:T(8,128)}, bf16[128,512]{1,0:T(8,128)(2,1)}, bf16[128,2048]{1,0:T(8,128)(...) custom-call(s32[4]{0:T(128)} %pad_add_fusion.meta, ...), custom_call_target="tpu_custom_call" | custom-call | flops 603979776 | bytes 10616848 | tf_op jit(solution)/shard_map/back_rear/pallas_call | solution.py:532
  140.1 23.3 %back_front.2 = (f32[128,512]{1,0:T(8,128)}, bf16[128,512]{1,0:T(8,128)(2,1)}, bf16[128,512]{1,0:T(8,128)(2,1)}, bf16[128,512]{1,0:T(8,128)(2,1)}, bf16[128,512]...) custom-call(s32[4]{0:T(128)} %pad_add_fusion.meta, ...), custom_call_target="tpu_custom_call" | custom-call | flops 1073741824 | bytes 7569424 | tf_op jit(solution)/shard_map/back_front/pallas_call | solution.py:532
  163.4 5.6 %back_first.2 = (bf16[128,512]{1,0:T(8,128)(2,1)}, bf16[128,512]{1,0:T(8,128)(2,1)}, bf16[128,2048]{1,0:T(8,128)(2,1)}, bf16[128,512]{1,0:T(8,128)(2,1)}, bf16[1...) custom-call(s32[4]{0:T(128)} %pad_add_fusion.meta, f32[128,512]{1,0:T(8,128)} %get-tuple-element.113.ds1_ref, ...), custom_call_target="tpu_custom_call" | custom-call | flops 536870912 | bytes 6062096 | tf_op jit(solution)/shard_map/back_first/pallas_call | solution.py:532
  170.3 7.0 %collective-permute-done.31.gb_ref = bf16[128,512]{1,0:T(8,128)(2,1)S(1)} collective-permute-done((bf16[128,512]{1,0:T(8,128)(2,1)}, bf16[128,512]{1,0:T(8,128)(2,1)S(1)}, u32[]{:S(2)}, u32[]{:S(2)}) %collective-permute-start.31) | collective-permute-done | bytes 131104 | tf_op jit(solution)/shard_map/ppermute | solution.py:545
  178.0 6.6 %back_rear.3 = (f32[128,512]{1,0:T(8,128)}, f32[128,512]{1,0:T(8,128)}, f32[8,512]{1,0:T(8,128)}, bf16[128,512]{1,0:T(8,128)(2,1)}, bf16[128,2048]{1,0:T(8,128)(...) custom-call(s32[4]{0:T(128)} %pad_add_fusion.meta, ...), custom_call_target="tpu_custom_call" | custom-call | flops 603979776 | bytes 10616848 | tf_op jit(solution)/shard_map/back_rear/pallas_call | solution.py:532
  194.6 11.9 %back_front.3 = (f32[128,512]{1,0:T(8,128)}, bf16[128,512]{1,0:T(8,128)(2,1)}, bf16[128,512]{1,0:T(8,128)(2,1)}, bf16[128,512]{1,0:T(8,128)(2,1)}, bf16[128,512]...) custom-call(s32[4]{0:T(128)} %pad_add_fusion.meta, ...), custom_call_target="tpu_custom_call" | custom-call | flops 1073741824 | bytes 7569424 | tf_op jit(solution)/shard_map/back_front/pallas_call | solution.py:532
  206.5 4.0 %weight_grads.3 = (bf16[4,8,128,128]{3,2,1,0:T(8,128)(2,1)}, bf16[2,8,128,128]{3,2,1,0:T(8,128)(2,1)}, bf16[1,8,128,128]{3,2,1,0:T(8,128)(2,1)}, bf16[1,8,128,128]{3,2,1,0:T(8,128)(2,1)}) custom-call(s32[4]{0:T(128)} %pad_add_fusion.meta, bf16[128,512]{1,0:T(8,128)(2,1)} %get-tuple-element.122.refs_0_.refs_2_.refs_4_, ...), custom_call_target="tpu_custom_call" | custom-call | flops 268435456 | bytes 2359312 | tf_op jit(solution)/shard_map/weight_grads/pallas_call | solution.py:532
  211.6 5.8 %back_first.3 = (bf16[128,512]{1,0:T(8,128)(2,1)}, bf16[128,512]{1,0:T(8,128)(2,1)}, bf16[128,2048]{1,0:T(8,128)(2,1)}, bf16[128,512]{1,0:T(8,128)(2,1)}, bf16[1...) custom-call(s32[4]{0:T(128)} %pad_add_fusion.meta, f32[128,512]{1,0:T(8,128)} %get-tuple-element.135.ds1_ref, ...), custom_call_target="tpu_custom_call" | custom-call | flops 536870912 | bytes 6062096 | tf_op jit(solution)/shard_map/back_first/pallas_call | solution.py:532
  221.2 9.7 %collective-permute-start.35 = (bf16[32,512]{1,0:T(8,128)(2,1)S(1)}, bf16[32,512]{1,0:T(8,128)(2,1)S(1)}, u32[]{:S(2)}, u32[]{:S(2)}) collective-permute-start(bf16[32,512]{1,0:T(8,128)(2,1)S(1)} %get-tuple-element.178), channel_id=1, source_target_pairs={{0,0},{16,1},{2,2},{18,3},{4,4},{20,5},{6,6},{22,7},{17,8},{1,9},{... | collective-permute-start | bytes 98312 | tf_op jit(solution)/shard_map/ppermute | solution.py:545
  232.2 4.0 %collective-permute-done.36 = bf16[32,512]{1,0:T(8,128)(2,1)S(1)} collective-permute-done((bf16[32,512]{1,0:T(8,128)(2,1)S(1)}, bf16[32,512]{1,0:T(8,128)(2,1)S(1)}, u32[]{:S(2)}, u32[]{:S(2)}) %collective-permute-start.36) | collective-permute-done | bytes 32800 | tf_op jit(solution)/shard_map/ppermute | solution.py:545
  240.9 13.2 %collective-permute-start.38 = (bf16[2,8,128,128]{3,2,1,0:T(8,128)(2,1)S(1)}, bf16[2,8,128,128]{3,2,1,0:T(8,128)(2,1)S(1)}, u32[]{:S(2)}, u32[]{:S(2)}) collective-permute-start(bf16[2,8,128,128]{3,2,1,0:T(8,128)(2,1)S(1)} %add_convert_fusion.2), channel_id=1, source_target_pairs={{0,4},{1,5},{2,6},{3,7},{4,0},{5,1},{6,2},{7,3},{8,12},{9,13},{10,... | collective-permute-start | bytes 1572872 | tf_op jit(solution)/shard_map/ppermute | solution.py:545
  255.5 6.8 %collective-permute-start.47 = (bf16[1,256,512]{2,1,0:T(8,128)(2,1)S(1)}, bf16[1,256,512]{2,1,0:T(8,128)(2,1)S(1)}, u32[]{:S(2)}, u32[]{:S(2)}) collective-permute-start(bf16[1,256,512]{2,1,0:T(8,128)(2,1)S(1)} %add_convert_fusion.6), channel_id=1, source_target_pairs={{0,4},{1,5},{2,6},{3,7},{4,0},{5,1},{6,2},{7,3},{8,12},{9,13},{10,... | collective-permute-start | bytes 786440 | tf_op jit(solution)/shard_map/ppermute | solution.py:545
  262.3 4.3 %collective-permute-done.38 = bf16[2,8,128,128]{3,2,1,0:T(8,128)(2,1)S(1)} collective-permute-done((bf16[2,8,128,128]{3,2,1,0:T(8,128)(2,1)S(1)}, bf16[2,8,128,128]{3,2,1,0:T(8,128)(2,1)S(1)}, u32[]{:S(2)}, u32[]{:S(2)}) %collective-permute-start.38) | collective-permute-done | bytes 524320 | tf_op jit(solution)/shard_map/ppermute | solution.py:545
  279.6 6.8 %collective-permute-done.48 = bf16[256,512]{1,0:T(8,128)(2,1)S(1)} collective-permute-done((bf16[256,512]{1,0:T(8,128)(2,1)S(1)}, bf16[256,512]{1,0:T(8,128)(2,1)S(1)}, u32[]{:S(2)}, u32[]{:S(2)}) %collective-permute-start.48) | collective-permute-done | bytes 262176 | tf_op jit(solution)/shard_map/ppermute | solution.py:545
  (202 shorter events, 115.1 us)
Async XLA Ops:
  0.6 14.7 %collective-permute-start.9 = (bf16[8,128,128]{2,1,0:T(8,128)(2,1)}, bf16[8,128,128]{2,1,0:T(8,128)(2,1)S(1)}, u32[]{:S(2)}, u32[]{:S(2)}) collective-permute-start(bf16[8,128,128]{2,1,0:T(8,128)(2,1)} %bitcast.116), channel_id=1, source_target_pairs={{0,0},{1,1},{2,2},{3,3},{4,4},{5,5},{6,6},{7,7},{8,16},{9,17},{10,... | collective-permute-start | bytes 786440 | tf_op jit(solution)/shard_map/ppermute | solution.py:545
  8.9 10.8 %collective-permute-start.3 = (bf16[272,512]{1,0:T(8,128)(2,1)S(1)}, bf16[272,512]{1,0:T(8,128)(2,1)S(1)}, u32[]{:S(2)}, u32[]{:S(2)}) collective-permute-start(bf16[272,512]{1,0:T(8,128)(2,1)S(1)} %pad_maximum_fusion.6), channel_id=1, source_target_pairs={{0,0},{1,1},{2,2},{3,3},{4,4},{5,5},{6,6},{7,7},{8,16},{9,17},{10,... | collective-permute-start | bytes 835592 | tf_op jit(solution)/shard_map/ppermute | solution.py:545
  10.8 14.5 %collective-permute-start.18 = (bf16[256,512]{1,0:T(8,128)(2,1)S(1)}, bf16[256,512]{1,0:T(8,128)(2,1)S(1)}, u32[]{:S(2)}, u32[]{:S(2)}) collective-permute-start(bf16[256,512]{1,0:T(8,128)(2,1)S(1)} %bitcast.88), channel_id=1, source_target_pairs={{0,0},{1,1},{2,2},{3,3},{4,4},{5,5},{6,6},{7,7},{8,16},{9,17},{10,... | collective-permute-start | bytes 786440 | tf_op jit(solution)/shard_map/ppermute | solution.py:545
  15.3 12.2 %collective-permute-start.10 = (bf16[1,8,128,128]{3,2,1,0:T(8,128)(2,1)S(1)}, bf16[1,8,128,128]{3,2,1,0:T(8,128)(2,1)S(1)}, u32[]{:S(2)}, u32[]{:S(2)}) collective-permute-start(bf16[1,8,128,128]{3,2,1,0:T(8,128)(2,1)S(1)} %bitcast.83), channel_id=1, source_target_pairs={{0,2},{1,3},{2,0},{3,1},{4,6},{5,7},{6,4},{7,5},{8,10},{9,11},{10,... | collective-permute-start | bytes 786440 | tf_op jit(solution)/shard_map/ppermute | solution.py:545
  27.7 11.0 %collective-permute-start.11 = (bf16[2,8,128,128]{3,2,1,0:T(8,128)(2,1)S(1)}, bf16[2,8,128,128]{3,2,1,0:T(8,128)(2,1)}, u32[]{:S(2)}, u32[]{:S(2)}) collective-permute-start(bf16[2,8,128,128]{3,2,1,0:T(8,128)(2,1)S(1)} %pad_maximum_fusion.4), channel_id=1, source_target_pairs={{0,4},{1,5},{2,6},{3,7},{4,0},{5,1},{6,2},{7,3},{8,12},{9,13},{10,... | collective-permute-start | bytes 1572872 | tf_op jit(solution)/shard_map/ppermute | solution.py:545
  29.3 12.2 %collective-permute-start.5 = (bf16[2,272,512]{2,1,0:T(8,128)(2,1)}, bf16[2,272,512]{2,1,0:T(8,128)(2,1)}, u32[]{:S(2)}, u32[]{:S(2)}) collective-permute-start(bf16[2,272,512]{2,1,0:T(8,128)(2,1)} %pad_maximum_fusion.3), channel_id=1, source_target_pairs={{0,2},{1,3},{2,0},{3,1},{4,6},{5,7},{6,4},{7,5},{8,10},{9,11},{10,... | collective-permute-start | bytes 1671176 | tf_op jit(solution)/shard_map/ppermute | solution.py:545
  32.8 14.3 %collective-permute-start.20 = (bf16[2,256,512]{2,1,0:T(8,128)(2,1)}, bf16[2,256,512]{2,1,0:T(8,128)(2,1)}, u32[]{:S(2)}, u32[]{:S(2)}) collective-permute-start(bf16[2,256,512]{2,1,0:T(8,128)(2,1)} %pad_maximum_fusion.5), channel_id=1, source_target_pairs={{0,1},{1,0},{2,3},{3,2},{4,5},{5,4},{6,7},{7,6},{8,9},{9,8},{10,11... | collective-permute-start | bytes 1572872 | tf_op jit(solution)/shard_map/ppermute | solution.py:545
  39.9 27.0 %collective-permute-start.12 = (bf16[4,8,128,128]{3,2,1,0:T(8,128)(2,1)S(1)}, bf16[4,8,128,128]{3,2,1,0:T(8,128)(2,1)S(1)}, u32[]{:S(2)}, u32[]{:S(2)}) collective-permute-start(bf16[4,8,128,128]{3,2,1,0:T(8,128)(2,1)S(1)} %pad_maximum_fusion.1.b0.refs_7_.refs_20_), channel_id=1, source_target_pairs={{0,1},{1,0},{2,3},{3,2},{4,5},{5,4},{6,7},{7,6},{8,9},{9,8},{10,11... | collective-permute-start | bytes 3145736 | tf_op jit(solution)/shard_map/ppermute | solution.py:545
  43.6 21.8 %collective-permute-start.6 = (bf16[4,272,512]{2,1,0:T(8,128)(2,1)}, bf16[4,272,512]{2,1,0:T(8,128)(2,1)}, u32[]{:S(2)}, u32[]{:S(2)}) collective-permute-start(bf16[4,272,512]{2,1,0:T(8,128)(2,1)} %pad_maximum_fusion.refs_0_.a0), channel_id=1, source_target_pairs={{0,4},{1,5},{2,6},{3,7},{4,0},{5,1},{6,2},{7,3},{8,12},{9,13},{10,... | collective-permute-start | bytes 3342344 | tf_op jit(solution)/shard_map/ppermute | solution.py:545
  49.2 18.0 %collective-permute-start.21 = (bf16[4,256,512]{2,1,0:T(8,128)(2,1)}, bf16[4,256,512]{2,1,0:T(8,128)(2,1)}, u32[]{:S(2)}, u32[]{:S(2)}) collective-permute-start(bf16[4,256,512]{2,1,0:T(8,128)(2,1)} %pad_maximum_fusion.2.refs_11_.c0), channel_id=1, source_target_pairs={{0,2},{1,3},{2,0},{3,1},{4,6},{5,7},{6,4},{7,5},{8,10},{9,11},{10,... | collective-permute-start | bytes 3145736 | tf_op jit(solution)/shard_map/ppermute | solution.py:545
  50.1 17.3 %collective-permute-start.7 = (bf16[4,272,512]{2,1,0:T(8,128)(2,1)}, bf16[4,272,512]{2,1,0:T(8,128)(2,1)}, u32[]{:S(2)}, u32[]{:S(2)}) collective-permute-start(bf16[4,272,512]{2,1,0:T(8,128)(2,1)} %pad_maximum_fusion.refs_0_.a0), channel_id=1, source_target_pairs={{0,16},{1,17},{2,18},{3,19},{4,20},{5,21},{6,22},{7,23},{8,24},{9,... | collective-permute-start | bytes 3342344 | tf_op jit(solution)/shard_map/ppermute | solution.py:545
  67.2 23.1 %collective-permute-start.22 = (bf16[4,256,512]{2,1,0:T(8,128)(2,1)}, bf16[4,256,512]{2,1,0:T(8,128)(2,1)}, u32[]{:S(2)}, u32[]{:S(2)}) collective-permute-start(bf16[4,256,512]{2,1,0:T(8,128)(2,1)} %pad_maximum_fusion.2.refs_11_.c0), channel_id=1, source_target_pairs={{0,16},{1,17},{2,18},{3,19},{4,20},{5,21},{6,22},{7,23},{8,24},{9,... | collective-permute-start | bytes 3145736 | tf_op jit(solution)/shard_map/ppermute | solution.py:545
  67.4 23.0 %collective-permute-start.23 = (bf16[4,256,512]{2,1,0:T(8,128)(2,1)}, bf16[4,256,512]{2,1,0:T(8,128)(2,1)}, u32[]{:S(2)}, u32[]{:S(2)}) collective-permute-start(bf16[4,256,512]{2,1,0:T(8,128)(2,1)} %collective-permute-done.21.refs_12_.c1), channel_id=1, source_target_pairs={{0,16},{1,17},{2,18},{3,19},{4,20},{5,21},{6,22},{7,23},{8,24},{9,... | collective-permute-start | bytes 3145736 | tf_op jit(solution)/shard_map/ppermute | solution.py:545
  188.0 48.1 %collective-permute-start.45 = (bf16[4,256,512]{2,1,0:T(8,128)(2,1)}, bf16[4,256,512]{2,1,0:T(8,128)(2,1)S(1)}, u32[]{:S(2)}, u32[]{:S(2)}) collective-permute-start(bf16[4,256,512]{2,1,0:T(8,128)(2,1)} %get-tuple-element.159), channel_id=1, source_target_pairs={{0,2},{1,3},{2,0},{3,1},{4,6},{5,7},{6,4},{7,5},{8,10},{9,11},{10,... | collective-permute-start | bytes 3145736 | tf_op jit(solution)/shard_map/ppermute | solution.py:545
  210.5 30.2 %collective-permute-start.37 = (bf16[4,8,128,128]{3,2,1,0:T(8,128)(2,1)}, bf16[4,8,128,128]{3,2,1,0:T(8,128)(2,1)S(1)}, u32[]{:S(2)}, u32[]{:S(2)}) collective-permute-start(bf16[4,8,128,128]{3,2,1,0:T(8,128)(2,1)} %get-tuple-element.138), channel_id=1, source_target_pairs={{0,1},{1,0},{2,3},{3,2},{4,5},{5,4},{6,7},{7,6},{8,9},{9,8},{10,11... | collective-permute-start | bytes 3145736 | tf_op jit(solution)/shard_map/ppermute | solution.py:545
  221.0 33.1 %collective-permute-start.41 = (bf16[4,272,512]{2,1,0:T(8,128)(2,1)}, bf16[4,272,512]{2,1,0:T(8,128)(2,1)S(1)}, u32[]{:S(2)}, u32[]{:S(2)}) collective-permute-start(bf16[4,272,512]{2,1,0:T(8,128)(2,1)} %get-tuple-element.151), channel_id=1, source_target_pairs={{0,4},{1,5},{2,6},{3,7},{4,0},{5,1},{6,2},{7,3},{8,12},{9,13},{10,... | collective-permute-start | bytes 3342344 | tf_op jit(solution)/shard_map/ppermute | solution.py:545
  221.2 11.0 %collective-permute-start.35 = (bf16[32,512]{1,0:T(8,128)(2,1)S(1)}, bf16[32,512]{1,0:T(8,128)(2,1)S(1)}, u32[]{:S(2)}, u32[]{:S(2)}) collective-permute-start(bf16[32,512]{1,0:T(8,128)(2,1)S(1)} %get-tuple-element.178), channel_id=1, source_target_pairs={{0,0},{16,1},{2,2},{18,3},{4,4},{20,5},{6,6},{22,7},{17,8},{1,9},{... | collective-permute-start | bytes 98312 | tf_op jit(solution)/shard_map/ppermute | solution.py:545
  237.4 18.0 %collective-permute-start.46 = (bf16[2,256,512]{2,1,0:T(8,128)(2,1)S(1)}, bf16[2,256,512]{2,1,0:T(8,128)(2,1)S(1)}, u32[]{:S(2)}, u32[]{:S(2)}) collective-permute-start(bf16[2,256,512]{2,1,0:T(8,128)(2,1)S(1)} %add_convert_fusion.1), channel_id=1, source_target_pairs={{0,1},{1,0},{2,3},{3,2},{4,5},{5,4},{6,7},{7,6},{8,9},{9,8},{10,11... | collective-permute-start | bytes 1572872 | tf_op jit(solution)/shard_map/ppermute | solution.py:545
  240.9 25.8 %collective-permute-start.38 = (bf16[2,8,128,128]{3,2,1,0:T(8,128)(2,1)S(1)}, bf16[2,8,128,128]{3,2,1,0:T(8,128)(2,1)S(1)}, u32[]{:S(2)}, u32[]{:S(2)}) collective-permute-start(bf16[2,8,128,128]{3,2,1,0:T(8,128)(2,1)S(1)} %add_convert_fusion.2), channel_id=1, source_target_pairs={{0,4},{1,5},{2,6},{3,7},{4,0},{5,1},{6,2},{7,3},{8,12},{9,13},{10,... | collective-permute-start | bytes 1572872 | tf_op jit(solution)/shard_map/ppermute | solution.py:545
  254.2 12.7 %collective-permute-start.42 = (bf16[2,272,512]{2,1,0:T(8,128)(2,1)S(1)}, bf16[2,272,512]{2,1,0:T(8,128)(2,1)S(1)}, u32[]{:S(2)}, u32[]{:S(2)}) collective-permute-start(bf16[2,272,512]{2,1,0:T(8,128)(2,1)S(1)} %add_convert_fusion), channel_id=1, source_target_pairs={{0,2},{1,3},{2,0},{3,1},{4,6},{5,7},{6,4},{7,5},{8,10},{9,11},{10,... | collective-permute-start | bytes 1671176 | tf_op jit(solution)/shard_map/ppermute | solution.py:545
  255.5 13.7 %collective-permute-start.47 = (bf16[1,256,512]{2,1,0:T(8,128)(2,1)S(1)}, bf16[1,256,512]{2,1,0:T(8,128)(2,1)S(1)}, u32[]{:S(2)}, u32[]{:S(2)}) collective-permute-start(bf16[1,256,512]{2,1,0:T(8,128)(2,1)S(1)} %add_convert_fusion.6), channel_id=1, source_target_pairs={{0,4},{1,5},{2,6},{3,7},{4,0},{5,1},{6,2},{7,3},{8,12},{9,13},{10,... | collective-permute-start | bytes 786440 | tf_op jit(solution)/shard_map/ppermute | solution.py:545
  269.3 17.0 %collective-permute-start.48 = (bf16[256,512]{1,0:T(8,128)(2,1)S(1)}, bf16[256,512]{1,0:T(8,128)(2,1)S(1)}, u32[]{:S(2)}, u32[]{:S(2)}) collective-permute-start(bf16[256,512]{1,0:T(8,128)(2,1)S(1)} %fusion.2), channel_id=1, source_target_pairs={{0,0},{1,1},{2,2},{3,3},{4,4},{5,5},{6,6},{7,7},{8,16},{9,17},{10,... | collective-permute-start | bytes 786440 | tf_op jit(solution)/shard_map/ppermute | solution.py:545
  272.3 16.9 %collective-permute-start.40 = (bf16[8,128,128]{2,1,0:T(8,128)(2,1)S(1)}, bf16[8,128,128]{2,1,0:T(8,128)(2,1)S(1)}, u32[]{:S(2)}, u32[]{:S(2)}) collective-permute-start(bf16[8,128,128]{2,1,0:T(8,128)(2,1)S(1)} %fusion.1), channel_id=1, source_target_pairs={{0,0},{1,1},{2,2},{3,3},{4,4},{5,5},{6,6},{7,7},{8,16},{9,17},{10,... | collective-permute-start | bytes 786440 | tf_op jit(solution)/shard_map/ppermute | solution.py:545
  276.2 16.0 %collective-permute-start.44 = (bf16[272,512]{1,0:T(8,128)(2,1)S(1)}, bf16[272,512]{1,0:T(8,128)(2,1)S(1)}, u32[]{:S(2)}, u32[]{:S(2)}) collective-permute-start(bf16[272,512]{1,0:T(8,128)(2,1)S(1)} %fusion), channel_id=1, source_target_pairs={{0,0},{1,1},{2,2},{3,3},{4,4},{5,5},{6,6},{7,7},{8,16},{9,17},{10,... | collective-permute-start | bytes 835592 | tf_op jit(solution)/shard_map/ppermute | solution.py:545
  (56 other events, 304.1 us)

commit v3 on v2

--- a/solution.py
+++ b/solution.py
@@ -20,6 +20,9 @@
 ORDER_A = 0
 ORDER_B = 1
 ORDER_C = 2
+PARTS_A = 4
+PARTS_B = 4
+PARTS_C = 4
 
 
 def sinusoid(length, width):
@@ -87,38 +90,40 @@
     return out
 
 
-def owners(meta, order, dims):
+def owners(meta, srcs, order, dims):
     slots, tensor, half = dims
     bits = bit_order(order, slots.bit_length() - 1)
     me, core = meta[0], meta[1]
-    out = []
-    for slot in range(slots):
-        f = me ^ slot_mask(slot, bits)
-        plane, t = f // tensor, lax.rem(f, tensor)
-        hi, at = divmod(slot, slots // 2)
-        out.append((hi, at, core * half + plane, t))
-        out.append((2 + hi, at, (1 - core) * half + plane, t))
+    out, own = [], len(srcs) // 2
+    for side in range(2):
+        slot = 0
+        for src in srcs[side * own:(side + 1) * own]:
+            for at in range(src.shape[0]):
+                f = me ^ slot_mask(slot, bits)
+                plane, t = f // tensor, lax.rem(f, tensor)
+                out.append((src, at, (core if side == 0 else 1 - core) * half + plane, t))
+                slot += 1
     return out
 
 
 def start_a(meta, srcs, dst, sem, order, dims):
     cols = srcs[0].shape[-1]
     rows = dst.shape[1] // (2 * dims[2])
-    for which, at, d, t in owners(meta, order, dims):
+    for which, at, d, t in owners(meta, srcs, order, dims):
         col = pl.ds(pl.multiple_of(t * cols, cols), cols)
         row = pl.ds(pl.multiple_of(d * rows, rows), rows)
         for k in range(2):
             pltpu.make_async_copy(
-                srcs[which].at[at, pl.ds(k * rows, rows)], dst.at[k, row, col], sem).start()
+                which.at[at, pl.ds(k * rows, rows)], dst.at[k, row, col], sem).start()
 
 
 def start_b(meta, srcs, dst, sem, order, dims, which_mats):
     rows, cols = srcs[0].shape[-2:]
-    for which, at, d, t in owners(meta, order, dims):
+    for which, at, d, t in owners(meta, srcs, order, dims):
         col = pl.ds(pl.multiple_of(t * cols, cols), cols)
         row = pl.ds(pl.multiple_of(d * rows, rows), rows)
         pltpu.make_async_copy(
-            srcs[which].at[at, pl.ds(*which_mats)], dst.at[:, row, col], sem).start()
+            which.at[at, pl.ds(*which_mats)], dst.at[:, row, col], sem).start()
 
 
 def wait_weights(dst, sem):
@@ -145,10 +150,10 @@
 
 
 def prep_kernel(dims, rows, meta, *refs):
-    srcs, (vm_ref, vi_ref, vf_ref, held, sem) = refs[:4], refs[4:]
-    where = owners(meta, ORDER_A, dims)
+    srcs, (vm_ref, vi_ref, vf_ref, held, sem) = refs[:PARTS_A], refs[PARTS_A:]
+    where = owners(meta, srcs, ORDER_A, dims)
     for i, (which, at, d, t) in enumerate(where):
-        pltpu.make_async_copy(srcs[which].at[at, pl.ds(2 * rows, 16)], held.at[i], sem).start()
+        pltpu.make_async_copy(which.at[at, pl.ds(2 * rows, 16)], held.at[i], sem).start()
     wait_weights(held, sem)
     width, hidden = vm_ref.shape[1], vf_ref.shape[1]
     totals = None
@@ -165,12 +170,12 @@
     vm_ref[...], vi_ref[...], vf_ref[...] = totals
 
 
-def f1_kernel(dims, meta, xa_ref, xb_ref, vm_ref, vi_ref, vf_ref, pos_ref, a0, a1, a2, a3,
-              b0, b1, b2, b3, s2_ref, filt_ref, stat_ref, s1_ref, before_ref, qu_ref, qv_ref, k_ref, v_ref,
-              rel_ref, probs_ref, ctx_ref, gi_ref, gs_ref,
-              wa, wb, pad, sems):
-    start_a(meta, (a0, a1, a2, a3), wa, sems.at[0], ORDER_A, dims)
-    start_b(meta, (b0, b1, b2, b3), wb, sems.at[1], ORDER_B, dims, (0, 8))
+def f1_kernel(dims, meta, xa_ref, xb_ref, vm_ref, vi_ref, vf_ref, pos_ref, *refs):
+    part_a, part_b, refs = refs[:PARTS_A], refs[PARTS_A:PARTS_A + PARTS_B], refs[PARTS_A + PARTS_B:]
+    (s2_ref, filt_ref, stat_ref, s1_ref, before_ref, act_ref, qu_ref, qv_ref, k_ref, v_ref,
+     rel_ref, probs_ref, ctx_ref, gi_ref, gs_ref, wa, wb, pad, sems) = refs
+    start_a(meta, part_a, wa, sems.at[0], ORDER_A, dims)
+    start_b(meta, part_b, wb, sems.at[1], ORDER_B, dims, (0, 8))
     length = meta[2]
     n_tok = xa_ref.shape[0]
     vm = lambda r: vm_ref[r:r + 1, :]
@@ -181,6 +186,7 @@
     before = nn(n0, wa[0]) + vf_ref[0:1, :]
     before_ref[...] = before
     active = (before * sigmoid(before)).astype(BF16)
+    act_ref[...] = active
     s1 = x + 0.5 * (nt(active, wa[1]) + vm(2))
     s1_ref[...] = s1
     wait_weights(wb, sems.at[1])
@@ -272,10 +278,11 @@
 
 def f2_kernel(dims, groups, meta, s2_ref, filt_ref, *refs):
     stats, refs = refs[:groups], refs[groups:]
-    vm_ref, vi_ref, vf_ref, b0, b1, b2, b3, c0, c1, c2, c3 = refs[:11]
-    out_ref, s3_ref, before_ref, s4_ref, bn_ref, wct, wc, sems = refs[11:]
-    start_b(meta, (b0, b1, b2, b3), wct, sems.at[0], ORDER_B, dims, (7, 1))
-    start_a(meta, (c0, c1, c2, c3), wc, sems.at[1], ORDER_C, dims)
+    vm_ref, vi_ref, vf_ref = refs[:3]
+    part_b, part_c, refs = refs[3:3 + PARTS_B], refs[3 + PARTS_B:3 + PARTS_B + PARTS_C], refs[3 + PARTS_B + PARTS_C:]
+    out_ref, s3_ref, before_ref, s4_ref, bn_ref, wct, wc, sems = refs
+    start_b(meta, part_b, wct, sems.at[0], ORDER_B, dims, (7, 1))
+    start_a(meta, part_c, wc, sems.at[1], ORDER_C, dims)
     vm = lambda r: vm_ref[r:r + 1, :]
     vi = lambda r: vi_ref[r:r + 1, :]
     mean, inv, count = bn_combine(stats)
@@ -298,12 +305,14 @@
     out_ref[...] = ln(s4, vm(12), vm(13)).astype(BF16)
 
 
-def b1_kernel(dims, meta, ga_ref, gb_ref, s4_ref, s3_ref, before_ref, filt_ref, bn_ref, vm_ref,
-              vi_ref, b0, b1, b2, b3, c0, c1, c2, c3,
-              ds3_ref, dnorm_ref, sum_ref, n3_ref, db_ref, dl_ref, a_ref, dlc_ref, ac_ref,
-              gm_ref, gi_ref, gf_ref, wct, wc, sems):
-    start_a(meta, (c0, c1, c2, c3), wc, sems.at[1], ORDER_C, dims)
-    start_b(meta, (b0, b1, b2, b3), wct, sems.at[0], ORDER_B, dims, (7, 1))
+def b1_kernel(dims, fresh, meta, ga_ref, gb_ref, s4_ref, s3_ref, before_ref, filt_ref, bn_ref,
+              vm_ref, vi_ref, *refs):
+    part_b, part_c, refs = refs[:PARTS_B], refs[PARTS_B:PARTS_B + PARTS_C], refs[PARTS_B + PARTS_C:]
+    (ds3_ref, dnorm_ref, sum_ref, n3_ref, db_ref, dl_ref, a_ref, dlc_ref, ac_ref,
+     gm_ref, gi_ref, gf_ref, wct, wc, sems) = refs
+    if fresh:
+        start_a(meta, part_c, wc, sems.at[1], ORDER_C, dims)
+        start_b(meta, part_b, wct, sems.at[0], ORDER_B, dims, (7, 1))
     vm = lambda r: vm_ref[r:r + 1, :]
     vi = lambda r: vi_ref[r:r + 1, :]
     g = jnp.where(meta[3] == 1, ga_ref[...].astype(F32), gb_ref[...].astype(F32))
@@ -314,7 +323,8 @@
     n3_ref[...] = ln(s3, vm(9), vm(10)).astype(BF16)
     before = before_ref[...]
     a_ref[...] = (before * sigmoid(before)).astype(BF16)
-    wait_weights(wc, sems.at[1])
+    if fresh:
+        wait_weights(wc, sems.at[1])
     db = (nn(delta, wc[1]) * silu_slope(before)).astype(BF16)
     db_ref[...] = db
     dn = nt(db, wc[0])
@@ -326,7 +336,8 @@
     xhat = (filt_ref[...] - bn_ref[0:1, :]) * bn_ref[1:2, :]
     normal = xhat * (1.0 + vi(6)) + vi(7)
     ac_ref[...] = (normal * sigmoid(normal)).astype(BF16)
-    wait_weights(wct, sems.at[0])
+    if fresh:
+        wait_weights(wct, sems.at[0])
     dnorm = nn(dlc, wct[0]) * silu_slope(normal)
     dnorm_ref[...] = dnorm
     u6 = rows_sum(dnorm * xhat)
@@ -347,13 +358,27 @@
     gf_ref[...] = rows_sum(db.astype(F32))
 
 
+def turn_kernel(dims, groups, meta, ga_ref, s2_ref, filt_ref, *refs):
+    stats, refs = refs[:groups], refs[groups:]
+    n_in = 3 + PARTS_B + PARTS_C
+    vm_ref, vi_ref, vf_ref, *weights = refs[:n_in]
+    refs = refs[n_in:]
+    ahead, behind, (wct, wc, sems) = refs[:5], refs[5:17], refs[17:]
+    f2_kernel(dims, groups, meta, s2_ref, filt_ref, *stats, vm_ref, vi_ref, vf_ref, *weights,
+              *ahead, wct, wc, sems)
+    _, s3_ref, before_ref, s4_ref, bn_ref = ahead
+    b1_kernel(dims, False, meta, ga_ref, ga_ref, s4_ref, s3_ref, before_ref, filt_ref, bn_ref,
+              vm_ref, vi_ref, *weights, *behind, wct, wc, sems)
+
+
 def b2_kernel(dims, groups, meta, ds3_ref, dnorm_ref, *refs):
     sums, refs = refs[:groups], refs[groups:]
     (filt_ref, bn_ref, gin_ref, gsig_ref, s2_ref, s1_ref, qu_ref, qv_ref, k_ref, v_ref, rel_ref,
-     probs_ref, gm1_ref, gi1_ref, vm_ref, vi_ref, b0, b1, b2, b3) = refs[:20]
+     probs_ref, gm1_ref, gi1_ref, vm_ref, vi_ref) = refs[:16]
+    part_b, refs = refs[16:16 + PARTS_B], refs[16 + PARTS_B:]
     (ds1_ref, n2_ref, dgi_ref, dgs_ref, dla_ref, n1_ref, dq_ref, dk_ref, dv_ref, drel_ref,
-     gm_ref, gi_ref, wb, pad_m, pad_d, dmix, sem) = refs[20:]
-    start_b(meta, (b0, b1, b2, b3), wb, sem, ORDER_B, dims, (0, 8))
+     dl_ref, gm_ref, gi_ref, wb, pad_m, pad_d, dmix, sem) = refs
+    start_b(meta, part_b, wb, sem, ORDER_B, dims, (0, 8))
     length = meta[2]
     n_tok, width = ds3_ref.shape
     vm = lambda r: vm_ref[r:r + 1, :]
@@ -441,18 +466,19 @@
     gm_ref[3:4, :] = gain
     gm_ref[4:5, :] = shift
     gm_ref[5:6, :] = rows_sum(dla.astype(F32))
-    ds1_ref[...] = ds2 + dx
-
-
-def b3_kernel(dims, meta, ds1_ref, xa_ref, xb_ref, before_ref, vm_ref, a0, a1, a2, a3,
-              dx_ref, n0_ref, db_ref, dl_ref, a_ref, gm_ref, gf_ref, wa, sem):
-    start_a(meta, (a0, a1, a2, a3), wa, sem, ORDER_A, dims)
+    ds1 = ds2 + dx
+    ds1_ref[...] = ds1
+    dl_ref[...] = (0.5 * ds1).astype(BF16)
+
+
+def b3_kernel(dims, fresh, meta, ds1_ref, xa_ref, xb_ref, before_ref, vm_ref, *refs):
+    part_a, (dx_ref, n0_ref, db_ref, gm_ref, gf_ref, wa, sem) = refs[:PARTS_A], refs[PARTS_A:]
+    if fresh:
+        start_a(meta, part_a, wa, sem, ORDER_A, dims)
     vm = lambda r: vm_ref[r:r + 1, :]
     ds1 = ds1_ref[...]
     delta = (0.5 * ds1).astype(BF16)
-    dl_ref[...] = delta
     before = before_ref[...]
-    a_ref[...] = (before * sigmoid(before)).astype(BF16)
     slope = silu_slope(before)
     x = jnp.where(meta[3] == 1, xb_ref[...].astype(F32), xa_ref[...].astype(F32))
     n0_ref[...] = ln(x, vm(0), vm(1)).astype(BF16)
@@ -466,6 +492,17 @@
     gm_ref[3:8, :] = jnp.zeros((5, gain.shape[1]), F32)
     gf_ref[...] = rows_sum(db.astype(F32))
     dx_ref[...] = (ds1 + dx).astype(BF16)
+
+
+def back_kernel(dims, groups, meta, *refs):
+    n_in = 2 + groups + 16 + PARTS_B
+    ins, refs = refs[:n_in], refs[n_in:]
+    (xa_ref, xb_ref, before_ref), part_a, refs = refs[:3], refs[3:3 + PARTS_A], refs[3 + PARTS_A:]
+    mid, last, scratch, (wa, sem_a) = refs[:13], refs[13:18], refs[18:23], refs[23:]
+    start_a(meta, part_a, wa, sem_a, ORDER_A, dims)
+    b2_kernel(dims, groups, meta, *ins, *mid, *scratch)
+    b3_kernel(dims, False, meta, mid[0], xa_ref, xb_ref, before_ref, ins[groups + 16], *part_a,
+              *last, wa, sem_a)
 
 
 def pieces_of(slots):
@@ -526,7 +563,7 @@
 def call(kernel, ins, outs, scratch=(), any_from=None, flops=0, name=None):
     specs = [pl.BlockSpec(memory_space=pltpu.SMEM)]
     for i in range(1, len(ins)):
-        away = any_from is not None and i >= any_from
+        away = i in any_from if isinstance(any_from, list) else any_from is not None and i >= any_from
         specs.append(pl.BlockSpec(memory_space=pl.ANY if away else pltpu.VMEM))
     nbytes = sum(a.size * a.dtype.itemsize for a in ins)
     return pl.pallas_call(
@@ -577,14 +614,20 @@
             out.append((flat(c, dd, tt), flat(c, dd // half * half + f // tensor, f % tensor)))
         return out
 
+    def spread(held, bits):
+        for b in bits:
+            held = jnp.concatenate([held, permute(held, bit_pairs(b))], axis=0)
+        return held
+
+    def both_cores(pieces):
+        return pieces + [permute(p, core_pairs) for p in pieces]
+
     def gather(block, order):
-        held = permute(block, swap_pairs)[None]
-        order = bit_order(order, nbits)
-        for b in order[:-1]:
-            held = jnp.concatenate([held, permute(held, bit_pairs(b))], axis=0)
-        far = permute(held, bit_pairs(order[-1]))
-        return [held, far, permute(held, core_pairs), permute(far, core_pairs)]
-
+        bits = bit_order(order, nbits)
+        held = spread(permute(block, swap_pairs)[None], bits[:-1])
+        return both_cores([held, permute(held, bit_pairs(bits[-1]))])
+
+    rows, fcols, mcols = ffw.shape[2], ffw.shape[3], mats.shape[3]
     ends = boundary[0]
     rows_here, width = ends.shape[1], ends.shape[2]
     length_all = rows_here * tensor
@@ -603,6 +646,14 @@
         there.append(pairs)
         back.append([(b, a) for a, b in pairs])
 
+    def lanes(v):
+        return jnp.pad(v[0], ((0, 0), (0, LANES - v.shape[2])))
+
+    vec = jnp.concatenate([
+        jnp.pad(lanes(vec_model), ((0, VEC_INNER - vec_model.shape[1]), (0, 0))),
+        jnp.pad(lanes(vec_inner), ((0, VEC_FF - VEC_INNER - vec_inner.shape[1]), (0, 0))),
+        jnp.pad(lanes(vec_ff), ((0, VEC_ROWS - VEC_FF - vec_ff.shape[1]), (0, 0)))], axis=0)
+    vec = vec.reshape(4, 16, LANES).transpose(1, 0, 2).reshape(16, 4 * LANES)
     ordered = jnp.where(first_is, ends, ends[::-1])
     len_ordered = jnp.where(first_is, lengths, lengths[::-1]).astype(BF16)
     parcels = jnp.concatenate(
@@ -618,15 +669,6 @@
     meta = jnp.stack([me, core, my_length, upper]).astype(jnp.int32)
     pos = jnp.asarray(sinusoid(length_all, width)).astype(BF16)
 
-    def lanes(v):
-        return jnp.pad(v[0], ((0, 0), (0, LANES - v.shape[2])))
-
-    vec = jnp.concatenate([
-        jnp.pad(lanes(vec_model), ((0, VEC_INNER - vec_model.shape[1]), (0, 0))),
-        jnp.pad(lanes(vec_inner), ((0, VEC_FF - VEC_INNER - vec_inner.shape[1]), (0, 0))),
-        jnp.pad(lanes(vec_ff), ((0, VEC_ROWS - VEC_FF - vec_ff.shape[1]), (0, 0)))], axis=0)
-    vec = vec.reshape(4, 16, LANES).transpose(1, 0, 2).reshape(16, 4 * LANES)
-    rows, fcols, mcols = ffw.shape[2], ffw.shape[3], mats.shape[3]
     a_all = gather(jnp.concatenate([ffw[0, 0:2].reshape(2 * rows, fcols), vec], axis=0), ORDER_A)
     b_all = gather(mats[0], ORDER_B)
     c_all = gather(ffw[0, 2:4].reshape(2 * rows, fcols), ORDER_C)
@@ -652,47 +694,67 @@
         return call(
             functools.partial(f1_kernel, dims),
             [meta, xa, xb, vm, vi, vf, pos] + a_all + b_all,
-            [((L, D), F32), ((L, D), F32), ((8, D), F32), ((L, D), F32), ((L, H), F32)]
-            + [((L, D), BF16)] * 4
+            [((L, D), F32), ((L, D), F32), ((8, D), F32), ((L, D), F32), ((L, H), F32),
+             ((L, H), BF16)] + [((L, D), BF16)] * 4
             + [((2 * L, D), BF16), ((heads, L, L), F32), ((L, D), BF16), ((L, D), F32), ((L, D), F32)],
             [wa_s, wb_s, pad_s, sems], 7, 15 * mat_flops, "layer_front",
         )
 
+    rear_out = [((L, D), BF16), ((L, D), F32), ((L, H), F32), ((L, D), F32), ((8, D), F32)]
+    back_rear_out = [
+        ((L, D), F32), ((L, D), F32), ((8, D), F32), ((L, D), BF16), ((L, H), BF16),
+        ((L, D), BF16), ((L, H), BF16), ((L, D), BF16), ((L, D), BF16),
+        ((8, D), F32), ((8, D), F32), ((1, H), F32)]
+    back_front_out = ([((L, D), F32)] + [((L, D), BF16)] * 8
+                      + [((2 * L, D), BF16), ((L, D), BF16), ((16, D), F32), ((40, D), F32)])
+    back_first_out = [((L, D), BF16), ((L, D), BF16), ((L, H), BF16), ((8, D), F32), ((1, H), F32)]
+    front_scratch = [wb_s, pad_s, pad_s, pltpu.VMEM((L, D), F32), sem_s]
+
     def f2(s2, filt, stats):
+        ins = [meta, s2, filt] + stats + [vm, vi, vf]
         return call(
-            functools.partial(f2_kernel, dims, len(stats)),
-            [meta, s2, filt] + stats + [vm, vi, vf] + b_all + c_all,
-            [((L, D), BF16), ((L, D), F32), ((L, H), F32), ((L, D), F32), ((8, D), F32)],
-            [wct_s, wa_s, sems], 6 + len(stats), 9 * mat_flops, "layer_rear",
+            functools.partial(f2_kernel, dims, len(stats)), ins + b_all + c_all, rear_out,
+            [wct_s, wa_s, sems], len(ins), 9 * mat_flops, "layer_rear",
         )
+
+    def turn(ga, s2, filt, stats):
+        ins = [meta, ga, s2, filt] + stats + [vm, vi, vf]
+        out = call(
+            functools.partial(turn_kernel, dims, len(stats)), ins + b_all + c_all,
+            rear_out + back_rear_out, [wct_s, wa_s, sems], len(ins), 18 * mat_flops, "layer_turn",
+        )
+        return out[:5], out[5:]
 
     def b1(ga, gb, s4, s3, before, filt, bn):
         return call(
-            functools.partial(b1_kernel, dims),
-            [meta, ga, gb, s4, s3, before, filt, bn, vm, vi] + b_all + c_all,
-            [((L, D), F32), ((L, D), F32), ((8, D), F32), ((L, D), BF16), ((L, H), BF16),
-             ((L, D), BF16), ((L, H), BF16), ((L, D), BF16), ((L, D), BF16),
-             ((8, D), F32), ((8, D), F32), ((1, H), F32)],
+            functools.partial(b1_kernel, dims, True),
+            [meta, ga, gb, s4, s3, before, filt, bn, vm, vi] + b_all + c_all, back_rear_out,
             [wct_s, wa_s, sems], 10, 9 * mat_flops, "back_rear",
         )
 
     def b2(ds3, dnorm, sums, *rest):
         ins = [meta, ds3, dnorm] + sums + list(rest) + [vm, vi]
         return call(
-            functools.partial(b2_kernel, dims, len(sums)), ins + b_all,
-            [((L, D), F32)] + [((L, D), BF16)] * 8
-            + [((2 * L, D), BF16), ((16, D), F32), ((40, D), F32)],
-            [wb_s, pad_s, pad_s, pltpu.VMEM((L, D), F32), sem_s], len(ins), 16 * mat_flops,
-            "back_front",
+            functools.partial(b2_kernel, dims, len(sums)), ins + b_all, back_front_out,
+            front_scratch, len(ins), 16 * mat_flops, "back_front",
         )
 
     def b3(ds1, xa, xb, before):
         return call(
-            functools.partial(b3_kernel, dims), [meta, ds1, xa, xb, before, vm] + a_all,
-            [((L, D), BF16), ((L, D), BF16), ((L, H), BF16), ((L, D), BF16), ((L, H), BF16),
-             ((8, D), F32), ((1, H), F32)],
-            [wa_s, sem_s], 6, 8 * mat_flops, "back_first",
+            functools.partial(b3_kernel, dims, True), [meta, ds1, xa, xb, before, vm] + a_all,
+            back_first_out, [wa_s, sem_s], 6, 8 * mat_flops, "back_first",
         )
+
+    def back_whole(ds3, dnorm, sums, rest, xa, xb, before):
+        ins = [meta, ds3, dnorm] + sums + list(rest) + [vm, vi]
+        away = list(range(len(ins), len(ins) + PARTS_B))
+        whole = ins + b_all + [xa, xb, before] + a_all
+        away += list(range(len(whole) - PARTS_A, len(whole)))
+        return call(
+            functools.partial(back_kernel, dims, len(sums)), whole,
+            back_front_out + back_first_out, front_scratch + [wa_s, sem_s], away, 24 * mat_flops,
+            "back_whole",
+        )[len(back_front_out)]
 
     def w(order, pairs, cols, is_ff, vecs=()):
         count = len(pairs)
@@ -736,45 +798,60 @@
         stats = norm_group(front[2])
         return front, f2(front[0], front[1], stats)
 
-    front, rear = forward(x0, x0)
+    _, rear = forward(x0, x0)
     middle = permute(rear[0], up_pairs)
-    front, rear = forward(x0, middle)
-    (s2, filt, _, s1, before0, qu, qv, k, v, rel, probs, ctx, gin, gsig) = front
+    front = f1(x0, middle)
+    (s2, filt, stats, s1, before0, a0, qu, qv, k, v, rel, probs, ctx, gin, gsig) = front
+    rear, part1 = turn(x0, s2, filt, norm_group(stats))
     made, s3, before1, s4, bn = rear
 
-    def backward(gb):
-        part1 = b1(x0, gb, s4, s3, before1, filt, bn)
-        sums = norm_group(part1[2])
-        part2 = b2(part1[0], part1[1], sums, filt, bn, gin, gsig, s2, s1, qu, qv, k, v, rel, probs,
-                   part1[9], part1[10])
-        return part1, part2
-
-    part1, part2 = backward(x0)
-    d_middle = permute(b3(part2[0], x0, middle, before0)[0], down_pairs)
-    part1, part2 = backward(d_middle)
+    def rest(part):
+        return [filt, bn, gin, gsig, s2, s1, qu, qv, k, v, rel, probs, part[9], part[10]]
+
+    dx = back_whole(part1[0], part1[1], norm_group(part1[2]), rest(part1), x0, middle, before0)
+    d_middle = permute(dx, down_pairs)
+    part1 = b1(x0, d_middle, s4, s3, before1, filt, bn)
+    sums = norm_group(part1[2])
     (_, _, _, n3, db1, dl3, a1, dlc, ac, _, _, gf1) = part1
-    (ds1, n2, dgi, dgs, dla, n1, dq, dk, dv, drel, gm2, gi2) = part2
-
-    def scatter(sent, order):
-        got = []
-        for piece, b in zip(sent[:-1], reversed(bit_order(order, nbits))):
-            size = piece.shape[0]
-            for g in got:
-                piece = piece.astype(F32) + g[size:2 * size].astype(F32)
-            got.append(permute(piece.astype(BF16), bit_pairs(b)))
-        total = sent[-1][0].astype(F32)
+
+    def round_of(sent, got, order):
+        done = len(got)
+        total = sent[done].astype(F32)
+        size = total.shape[0]
+        last = done == nbits
         for g in got:
-            total = total + g[0].astype(F32)
-        return permute(total.astype(BF16), swap_pairs)
-
-    grad_c = scatter(w(ORDER_C, [(n3, db1), (dl3, a1)], fcols, True), ORDER_C)
-    pieces_b = list(w(ORDER_B, [(n1, dq), (n1, dk), (n1, dv), (dla, ctx), (pos, drel), (n2, dgi),
-                                (n2, dgs), (dlc, ac)], mcols, False))
-    ds1, pieces_b[0] = lax.optimization_barrier((ds1, pieces_b[0]))
-    dx, n0, db0, dl0, a0, gm0, gf0 = b3(ds1, x0, middle, before0)
-    grad_b = scatter(pieces_b, ORDER_B)
-    grad_a = scatter(w(ORDER_A, [(n0, db0), (dl0, a0)], fcols, True, (gm2, gm0, gi2, gf0, gf1)),
-                     ORDER_A)
+            total = total + (g[0:1] if last else g[size:2 * size]).astype(F32)
+        if last:
+            return permute(total[0].astype(BF16), swap_pairs)
+        bit = list(reversed(bit_order(order, nbits)))[done]
+        return got + [permute(total.astype(BF16), bit_pairs(bit))]
+
+    def scatter(sent, got, order):
+        while len(got) <= nbits:
+            more = round_of(sent, got, order)
+            if len(got) == nbits:
+                return more
+            got = more
+
+    pieces_c = w(2, [(n3, db1), (dl3, a1)], fcols, True)
+    got_c = round_of(pieces_c, [], 2)
+    part2 = b2(part1[0], part1[1], sums, *rest(part1))
+    (ds1, n2, dgi, dgs, dla, n1, dq, dk, dv, drel, dl0, gm2, gi2) = part2
+    got_c[0], n1 = lax.optimization_barrier((got_c[0], n1))
+    got_c = round_of(pieces_c, got_c, 2)
+    pieces_b = list(w(0, [(n1, dq), (n1, dk), (n1, dv), (dla, ctx), (pos, drel), (n2, dgi),
+                          (n2, dgs), (dlc, ac)], mcols, False))
+    got_b = round_of(pieces_b, [], 0)
+    ds1, pieces_b[1] = lax.optimization_barrier((ds1, pieces_b[1]))
+    dx, n0, db0, gm0, gf0 = b3(ds1, x0, middle, before0)
+    got_c[1], n0 = lax.optimization_barrier((got_c[1], n0))
+    got_c = round_of(pieces_c, got_c, 2)
+    pieces_a = w(1, [(n0, db0), (dl0, a0)], fcols, True, (gm2, gm0, gi2, gf0, gf1))
+    got_a = round_of(pieces_a, [], 1)
+    got_c[2], got_a[0] = lax.optimization_barrier((got_c[2], got_a[0]))
+    grad_c = scatter(pieces_c, got_c, 2)
+    grad_b = scatter(pieces_b, got_b, 0)
+    grad_a = scatter(pieces_a, got_a, 1)
 
     stream = jnp.where(is_upper, made, dx).reshape(tensor, rows_here, width)
     pair = jnp.stack([
@@ -790,9 +867,10 @@
                            gv[:8, 3 * LANES:3 * LANES + small]], axis=0)
     grad_f = jnp.concatenate([grad_a[:2 * rows].reshape(2, rows, fcols),
                               grad_c.astype(F32).reshape(2, rows, fcols)], axis=0)
+    grad_m = grad_b.astype(F32)
     return (
         ends_out,
-        grad_b.astype(F32)[None],
+        grad_m[None],
         grad_f[None],
         gv[:vec_model.shape[1], :small][None],
         gvi[:vec_inner.shape[1]][None],

time: 298 us -> 282 us (0.946)
  starting transfers between devices: 104 us -> 91.7 us
  Pallas kernels: 105 us -> 96.9 us
  waiting for transfers between devices: 60.5 us -> 64 us
    ppermute x49, starting transfers between devices: 104 us -> 91.7 us  [permute(): return lax.ppermute(value, ('pipe', 'dp', 'tensor'), pairs)]
    pallas_call x14 -> x12, Pallas kernels: 105 us -> 96.9 us  [call(): pl.pallas_call(kernel, out_shape=[jax.ShapeDtypeStruct(s, d) for s, d in...]
    ppermute x49, waiting for transfers between devices: 60.5 us -> 64 us  [permute(): return lax.ppermute(value, ('pipe', 'dp', 'tensor'), pairs)]
    unnamed x65 -> x67, local copies, waits for them, and re-layouts: 6.89 us -> 6.88 us
  transfers between devices with their start and end apart: 49 -> 49, of which waited for: 26 -> 24; matrix products, arithmetic and copies ran while one was open for 5% -> 6% of each run, Pallas kernels for 13% -> 14%
where the time goes in v3:
time: 282 us; the launch traced here: 279 us
  Pallas kernels  96.9 us (34%)
  starting transfers between devices  91.7 us (33%)
  waiting for transfers between devices  64 us (23%)
  other arithmetic  14.5 us (5%)
  local copies, waits for them, and re-layouts  9.96 us (4%)
    pallas_call x12, Pallas kernels, call(): pl.pallas_call(kernel, out_shape=[jax.ShapeDtypeStruct(s, d) for s, d in...  96.9 us
    ppermute x49, starting transfers between devices, permute(): return lax.ppermute(value, ('pipe', 'dp', 'tensor'), pairs)  91.7 us
    ppermute x49, waiting for transfers between devices, permute(): return lax.ppermute(value, ('pipe', 'dp', 'tensor'), pairs)  64 us
    concatenate x6, other arithmetic, spread(): held = jnp.concatenate([held, permute(held, bit_pairs(b))], axis=0)  7.15 us
    unnamed x67, local copies, waits for them, and re-layouts  6.88 us
  transfers between devices with their start and end apart: 49, of which 24 were waited for; matrix products, arithmetic and copies ran while one was open for 6% of the time, Pallas kernels for 14%

profile of v3, /device:TPU:1, one launch (start us, length us, event | category | flops | bytes accessed | tf_op | source)
XLA Modules:
  0.0 279.2 jit_solution(6932237659593198370)
XLA Ops:
  0.6 5.6 %collective-permute-start.9 = (bf16[8,128,128]{2,1,0:T(8,128)(2,1)}, bf16[8,128,128]{2,1,0:T(8,128)(2,1)S(1)}, u32[]{:S(2)}, u32[]{:S(2)}) collective-permute-start(bf16[8,128,128]{2,1,0:T(8,128)(2,1)} %bitcast.115), channel_id=1, source_target_pairs={{0,0},{1,1},{2,2},{3,3},{4,4},{5,5},{6,6},{7,7},{8,16},{9,17},{10,... | collective-permute-start | bytes 786440 | tf_op jit(solution)/shard_map/ppermute | solution.py:582
  10.8 4.5 %collective-permute-start.18 = (bf16[256,512]{1,0:T(8,128)(2,1)S(1)}, bf16[256,512]{1,0:T(8,128)(2,1)S(1)}, u32[]{:S(2)}, u32[]{:S(2)}) collective-permute-start(bf16[256,512]{1,0:T(8,128)(2,1)S(1)} %bitcast.87), channel_id=1, source_target_pairs={{0,0},{1,1},{2,2},{3,3},{4,4},{5,5},{6,6},{7,7},{8,16},{9,17},{10,... | collective-permute-start | bytes 786440 | tf_op jit(solution)/shard_map/ppermute | solution.py:582
  34.4 4.3 %collective-permute-done.11 = bf16[2,8,128,128]{3,2,1,0:T(8,128)(2,1)} collective-permute-done((bf16[2,8,128,128]{3,2,1,0:T(8,128)(2,1)S(1)}, bf16[2,8,128,128]{3,2,1,0:T(8,128)(2,1)}, u32[]{:S(2)}, u32[]{:S(2)}) %collective-permute-start.11) | collective-permute-done | bytes 524320 | tf_op jit(solution)/shard_map/ppermute | solution.py:582
  50.3 4.9 %collective-permute-start = (bf16[48,512]{1,0:T(8,128)(2,1)S(1)}, bf16[48,512]{1,0:T(8,128)(2,1)S(1)}, u32[]{:S(2)}, u32[]{:S(2)}) collective-permute-start(bf16[48,512]{1,0:T(8,128)(2,1)S(1)} %get-tuple-element.192), channel_id=1, source_target_pairs={{0,0},{1,16},{2,2},{3,18},{4,4},{5,20},{6,6},{7,22},{8,17},{9,1},{... | collective-permute-start | bytes 147464 | tf_op jit(solution)/shard_map/ppermute | solution.py:582
  55.2 5.8 %collective-permute-done = bf16[48,512]{1,0:T(8,128)(2,1)S(1)} collective-permute-done((bf16[48,512]{1,0:T(8,128)(2,1)S(1)}, bf16[48,512]{1,0:T(8,128)(2,1)S(1)}, u32[]{:S(2)}, u32[]{:S(2)}) %collective-permute-start) | collective-permute-done | bytes 49184 | tf_op jit(solution)/shard_map/ppermute | solution.py:582
  74.2 10.0 %layer_front.2 = (f32[128,512]{1,0:T(8,128)}, f32[128,512]{1,0:T(8,128)}, f32[8,512]{1,0:T(8,128)}, f32[128,512]{1,0:T(8,128)}, f32[128,2048]{1,0:T(8,128)}, /*i...) custom-call(s32[4]{0:T(128)} %pad_add_fusion.meta, ...), custom_call_target="tpu_custom_call" | custom-call | flops 1006632960 | bytes 9355280 | tf_op jit(solution)/shard_map/layer_front/pallas_call | solution.py:569
  84.2 5.5 %collective-permute-start.17 = (f32[1,8,512]{2,1,0:T(8,128)}, f32[1,8,512]{2,1,0:T(8,128)S(1)}, u32[]{:S(2)}, u32[]{:S(2)}) collective-permute-start(f32[1,8,512]{2,1,0:T(8,128)} %bitcast.105), channel_id=1, source_target_pairs={{0,5},{1,4},{2,7},{3,6},{4,1},{5,0},{6,3},{7,2},{8,13},{9,12},{10,... | collective-permute-start | bytes 49160 | tf_op jit(solution)/shard_map/ppermute | solution.py:582
  93.1 5.6 %layer_rear.1 = (bf16[128,512]{1,0:T(8,128)(2,1)}, f32[128,512]{1,0:T(8,128)}, f32[128,2048]{1,0:T(8,128)}, f32[128,512]{1,0:T(8,128)}, f32[8,512]{1,0:T(8,128)}) custom-call(s32[4]{0:T(128)} %pad_add_fusion.meta, f32[128,512]{1,0:T(8,128)} %get-tuple-element.92.s2_ref, f32[128,512]{1,0:T(8,128)} %get-tuple-element.93.filt_ref, f32[1,8,512]{2,1,0:T(8,128)} %bitcast.108, ...), custom_call_target="tpu_custom_call" | custom-call | flops 603979776 | bytes 9158672 | tf_op jit(solution)/shard_map/layer_rear/pallas_call | solution.py:569
  103.8 10.0 %layer_front.3 = (f32[128,512]{1,0:T(8,128)}, f32[128,512]{1,0:T(8,128)}, f32[8,512]{1,0:T(8,128)}, f32[128,512]{1,0:T(8,128)}, f32[128,2048]{1,0:T(8,128)}, /*i...) custom-call(s32[4]{0:T(128)} %pad_add_fusion.meta, ...), custom_call_target="tpu_custom_call" | custom-call | flops 1006632960 | bytes 9355280 | tf_op jit(solution)/shard_map/layer_front/pallas_call | solution.py:569
  121.2 7.4 %layer_turn.1 = (bf16[128,512]{1,0:T(8,128)(2,1)}, f32[128,512]{1,0:T(8,128)}, f32[128,2048]{1,0:T(8,128)}, f32[128,512]{1,0:T(8,128)}, f32[8,512]{1,0:T(8,128)}...) custom-call(s32[4]{0:T(128)} %pad_add_fusion.meta, ...), custom_call_target="tpu_custom_call" | custom-call | flops 1207959552 | bytes 9289744 | tf_op jit(solution)/shard_map/layer_turn/pallas_call | solution.py:569
  134.5 25.6 %back_whole.1 = (f32[128,512]{1,0:T(8,128)}, bf16[128,512]{1,0:T(8,128)(2,1)}, bf16[128,512]{1,0:T(8,128)(2,1)}, bf16[128,512]{1,0:T(8,128)(2,1)}, bf16[128,512]...) custom-call(s32[4]{0:T(128)} %pad_add_fusion.meta, ...), custom_call_target="tpu_custom_call" | custom-call | flops 1610612736 | bytes 13336592 | tf_op jit(solution)/shard_map/back_whole/pallas_call | solution.py:569
  161.4 7.1 %collective-permute-done.31.gb_ref = bf16[128,512]{1,0:T(8,128)(2,1)S(1)} collective-permute-done((bf16[128,512]{1,0:T(8,128)(2,1)}, bf16[128,512]{1,0:T(8,128)(2,1)S(1)}, u32[]{:S(2)}, u32[]{:S(2)}) %collective-permute-start.31) | collective-permute-done | bytes 131104 | tf_op jit(solution)/shard_map/ppermute | solution.py:582
  169.2 6.6 %back_rear.1 = (f32[128,512]{1,0:T(8,128)}, f32[128,512]{1,0:T(8,128)}, f32[8,512]{1,0:T(8,128)}, bf16[128,512]{1,0:T(8,128)(2,1)}, bf16[128,2048]{1,0:T(8,128)(...) custom-call(s32[4]{0:T(128)} %pad_add_fusion.meta, ...), custom_call_target="tpu_custom_call" | custom-call | flops 603979776 | bytes 10616848 | tf_op jit(solution)/shard_map/back_rear/pallas_call | solution.py:569
  175.8 3.4 %weight_grads.3 = (bf16[4,256,512]{2,1,0:T(8,128)(2,1)}, bf16[2,256,512]{2,1,0:T(8,128)(2,1)}, bf16[1,256,512]{2,1,0:T(8,128)(2,1)}, bf16[1,256,512]{2,1,0:T(8,128)(2,1)}) custom-call(s32[4]{0:T(128)} %pad_add_fusion.meta, bf16[128,512]{1,0:T(8,128)(2,1)} %get-tuple-element.126.refs_0_, bf16[128,2048]{1,0:T(8,128)(2,1)} %get-tuple-element.127.refs_1_, ...), custom_call_target="tpu_custom_call" | custom-call | flops 268435456 | bytes 1310736 | tf_op jit(solution)/shard_map/weight_grads/pallas_call | solution.py:569
  185.7 11.9 %back_front.1 = (f32[128,512]{1,0:T(8,128)}, bf16[128,512]{1,0:T(8,128)(2,1)}, bf16[128,512]{1,0:T(8,128)(2,1)}, bf16[128,512]{1,0:T(8,128)(2,1)}, bf16[128,512]...) custom-call(s32[4]{0:T(128)} %pad_add_fusion.meta, ...), custom_call_target="tpu_custom_call" | custom-call | flops 1073741824 | bytes 7569424 | tf_op jit(solution)/shard_map/back_front/pallas_call | solution.py:569
  200.7 4.0 %weight_grads.4 = (bf16[4,8,128,128]{3,2,1,0:T(8,128)(2,1)}, bf16[2,8,128,128]{3,2,1,0:T(8,128)(2,1)}, bf16[1,8,128,128]{3,2,1,0:T(8,128)(2,1)}, bf16[1,8,128,128]{3,2,1,0:T(8,128)(2,1)}) custom-call(s32[4]{0:T(128)} %pad_add_fusion.meta, bf16[128,512]{1,0:T(8,128)(2,1)} %get-tuple-element.132.refs_0_.refs_2_.refs_4_, ...), custom_call_target="tpu_custom_call" | custom-call | flops 268435456 | bytes 2359312 | tf_op jit(solution)/shard_map/weight_grads/pallas_call | solution.py:569
  204.7 5.8 %back_first.1 = (bf16[128,512]{1,0:T(8,128)(2,1)}, bf16[128,512]{1,0:T(8,128)(2,1)}, bf16[128,2048]{1,0:T(8,128)(2,1)}, f32[8,512]{1,0:T(8,128)}, f32[1,2048]{1,0:T(1,128)}) custom-call(s32[4]{0:T(128)} %pad_add_fusion.meta, f32[128,512]{1,0:T(8,128)} %get-tuple-element.145.ds1_ref, bf16[128,512]{1,0:T(8,128)(2,1)} %bitcast.73, bf16[128,512]{1,0:T(8,128)(2,1)} %copy-done.3, ...), custom_call_target="tpu_custom_call" | custom-call | flops 536870912 | bytes 6062096 | tf_op jit(solution)/shard_map/back_first/pallas_call | solution.py:569
  210.6 3.7 %weight_grads.5 = (bf16[4,272,512]{2,1,0:T(8,128)(2,1)}, bf16[2,272,512]{2,1,0:T(8,128)(2,1)}, bf16[1,272,512]{2,1,0:T(8,128)(2,1)}, bf16[1,272,512]{2,1,0:T(8,128)(2,1)}) custom-call(s32[4]{0:T(128)} %pad_add_fusion.meta, bf16[128,512]{1,0:T(8,128)(2,1)} %get-tuple-element.154.refs_0_, bf16[128,2048]{1,0:T(8,128)(2,1)} %get-tuple-element.155.refs_1_, ...), custom_call_target="tpu_custom_call" | custom-call | flops 268435456 | bytes 1458192 | tf_op jit(solution)/shard_map/weight_grads/pallas_call | solution.py:569
  216.7 8.1 %collective-permute-start.36 = (bf16[32,512]{1,0:T(8,128)(2,1)S(1)}, bf16[32,512]{1,0:T(8,128)(2,1)S(1)}, u32[]{:S(2)}, u32[]{:S(2)}) collective-permute-start(bf16[32,512]{1,0:T(8,128)(2,1)S(1)} %get-tuple-element.188), channel_id=1, source_target_pairs={{0,0},{16,1},{2,2},{18,3},{4,4},{20,5},{6,6},{22,7},{17,8},{1,9},{... | collective-permute-start | bytes 98312 | tf_op jit(solution)/shard_map/ppermute | solution.py:582
  229.0 7.1 %collective-permute-done.43 = bf16[1,256,512]{2,1,0:T(8,128)(2,1)S(1)} collective-permute-done((bf16[1,256,512]{2,1,0:T(8,128)(2,1)S(1)}, bf16[1,256,512]{2,1,0:T(8,128)(2,1)S(1)}, u32[]{:S(2)}, u32[]{:S(2)}) %collective-permute-start.43) | collective-permute-done | bytes 262176 | tf_op jit(solution)/shard_map/ppermute | solution.py:582
  239.3 5.4 %collective-permute-done.45 = bf16[2,272,512]{2,1,0:T(8,128)(2,1)S(1)} collective-permute-done((bf16[2,272,512]{2,1,0:T(8,128)(2,1)S(1)}, bf16[2,272,512]{2,1,0:T(8,128)(2,1)S(1)}, u32[]{:S(2)}, u32[]{:S(2)}) %collective-permute-start.45) | collective-permute-done | bytes 557088 | tf_op jit(solution)/shard_map/ppermute | solution.py:582
  246.7 10.8 %collective-permute-start.48 = (bf16[256,512]{1,0:T(8,128)(2,1)S(1)}, bf16[256,512]{1,0:T(8,128)(2,1)S(1)}, u32[]{:S(2)}, u32[]{:S(2)}) collective-permute-start(bf16[256,512]{1,0:T(8,128)(2,1)S(1)} %fusion.2), channel_id=1, source_target_pairs={{0,0},{1,1},{2,2},{3,3},{4,4},{5,5},{6,6},{7,7},{8,16},{9,17},{10,... | collective-permute-start | bytes 786440 | tf_op jit(solution)/shard_map/ppermute | solution.py:582
  259.8 4.5 %collective-permute-start.47 = (bf16[272,512]{1,0:T(8,128)(2,1)S(1)}, bf16[272,512]{1,0:T(8,128)(2,1)S(1)}, u32[]{:S(2)}, u32[]{:S(2)}) collective-permute-start(bf16[272,512]{1,0:T(8,128)(2,1)S(1)} %fusion), channel_id=1, source_target_pairs={{0,0},{1,1},{2,2},{3,3},{4,4},{5,5},{6,6},{7,7},{8,16},{9,17},{10,... | collective-permute-start | bytes 835592 | tf_op jit(solution)/shard_map/ppermute | solution.py:582
  265.0 7.9 %collective-permute-done.41 = bf16[8,128,128]{2,1,0:T(8,128)(2,1)S(1)} collective-permute-done((bf16[8,128,128]{2,1,0:T(8,128)(2,1)S(1)}, bf16[8,128,128]{2,1,0:T(8,128)(2,1)S(1)}, u32[]{:S(2)}, u32[]{:S(2)}) %collective-permute-start.41) | collective-permute-done | bytes 262176 | tf_op jit(solution)/shard_map/ppermute | solution.py:582
  (202 shorter events, 101.4 us)
Async XLA Ops:
  0.6 14.7 %collective-permute-start.9 = (bf16[8,128,128]{2,1,0:T(8,128)(2,1)}, bf16[8,128,128]{2,1,0:T(8,128)(2,1)S(1)}, u32[]{:S(2)}, u32[]{:S(2)}) collective-permute-start(bf16[8,128,128]{2,1,0:T(8,128)(2,1)} %bitcast.115), channel_id=1, source_target_pairs={{0,0},{1,1},{2,2},{3,3},{4,4},{5,5},{6,6},{7,7},{8,16},{9,17},{10,... | collective-permute-start | bytes 786440 | tf_op jit(solution)/shard_map/ppermute | solution.py:582
  8.9 10.8 %collective-permute-start.3 = (bf16[272,512]{1,0:T(8,128)(2,1)S(1)}, bf16[272,512]{1,0:T(8,128)(2,1)S(1)}, u32[]{:S(2)}, u32[]{:S(2)}) collective-permute-start(bf16[272,512]{1,0:T(8,128)(2,1)S(1)} %pad_maximum_fusion.6), channel_id=1, source_target_pairs={{0,0},{1,1},{2,2},{3,3},{4,4},{5,5},{6,6},{7,7},{8,16},{9,17},{10,... | collective-permute-start | bytes 835592 | tf_op jit(solution)/shard_map/ppermute | solution.py:582
  10.8 14.5 %collective-permute-start.18 = (bf16[256,512]{1,0:T(8,128)(2,1)S(1)}, bf16[256,512]{1,0:T(8,128)(2,1)S(1)}, u32[]{:S(2)}, u32[]{:S(2)}) collective-permute-start(bf16[256,512]{1,0:T(8,128)(2,1)S(1)} %bitcast.87), channel_id=1, source_target_pairs={{0,0},{1,1},{2,2},{3,3},{4,4},{5,5},{6,6},{7,7},{8,16},{9,17},{10,... | collective-permute-start | bytes 786440 | tf_op jit(solution)/shard_map/ppermute | solution.py:582
  15.3 12.2 %collective-permute-start.10 = (bf16[1,8,128,128]{3,2,1,0:T(8,128)(2,1)S(1)}, bf16[1,8,128,128]{3,2,1,0:T(8,128)(2,1)S(1)}, u32[]{:S(2)}, u32[]{:S(2)}) collective-permute-start(bf16[1,8,128,128]{3,2,1,0:T(8,128)(2,1)S(1)} %bitcast.82), channel_id=1, source_target_pairs={{0,2},{1,3},{2,0},{3,1},{4,6},{5,7},{6,4},{7,5},{8,10},{9,11},{10,... | collective-permute-start | bytes 786440 | tf_op jit(solution)/shard_map/ppermute | solution.py:582
  27.7 11.0 %collective-permute-start.11 = (bf16[2,8,128,128]{3,2,1,0:T(8,128)(2,1)S(1)}, bf16[2,8,128,128]{3,2,1,0:T(8,128)(2,1)}, u32[]{:S(2)}, u32[]{:S(2)}) collective-permute-start(bf16[2,8,128,128]{3,2,1,0:T(8,128)(2,1)S(1)} %pad_maximum_fusion.4), channel_id=1, source_target_pairs={{0,4},{1,5},{2,6},{3,7},{4,0},{5,1},{6,2},{7,3},{8,12},{9,13},{10,... | collective-permute-start | bytes 1572872 | tf_op jit(solution)/shard_map/ppermute | solution.py:582
  29.3 12.2 %collective-permute-start.5 = (bf16[2,272,512]{2,1,0:T(8,128)(2,1)}, bf16[2,272,512]{2,1,0:T(8,128)(2,1)}, u32[]{:S(2)}, u32[]{:S(2)}) collective-permute-start(bf16[2,272,512]{2,1,0:T(8,128)(2,1)} %pad_maximum_fusion.3), channel_id=1, source_target_pairs={{0,2},{1,3},{2,0},{3,1},{4,6},{5,7},{6,4},{7,5},{8,10},{9,11},{10,... | collective-permute-start | bytes 1671176 | tf_op jit(solution)/shard_map/ppermute | solution.py:582
  32.8 14.3 %collective-permute-start.20 = (bf16[2,256,512]{2,1,0:T(8,128)(2,1)}, bf16[2,256,512]{2,1,0:T(8,128)(2,1)}, u32[]{:S(2)}, u32[]{:S(2)}) collective-permute-start(bf16[2,256,512]{2,1,0:T(8,128)(2,1)} %pad_maximum_fusion.5), channel_id=1, source_target_pairs={{0,1},{1,0},{2,3},{3,2},{4,5},{5,4},{6,7},{7,6},{8,9},{9,8},{10,11... | collective-permute-start | bytes 1572872 | tf_op jit(solution)/shard_map/ppermute | solution.py:582
  39.9 27.0 %collective-permute-start.12 = (bf16[4,8,128,128]{3,2,1,0:T(8,128)(2,1)S(1)}, bf16[4,8,128,128]{3,2,1,0:T(8,128)(2,1)S(1)}, u32[]{:S(2)}, u32[]{:S(2)}) collective-permute-start(bf16[4,8,128,128]{3,2,1,0:T(8,128)(2,1)S(1)} %pad_maximum_fusion.1.refs_4_.refs_7_.refs_22_.refs_0_.refs_20_), channel_id=1, source_target_pairs={{0,1},{1,0},{2,3},{3,2},{4,5},{5,4},{6,7},{7,6},{8,9},{9,8},{10,11... | collective-permute-start | bytes 3145736 | tf_op jit(solution)/shard_map/ppermute | solution.py:582
  43.6 21.8 %collective-permute-start.6 = (bf16[4,272,512]{2,1,0:T(8,128)(2,1)}, bf16[4,272,512]{2,1,0:T(8,128)(2,1)}, u32[]{:S(2)}, u32[]{:S(2)}) collective-permute-start(bf16[4,272,512]{2,1,0:T(8,128)(2,1)} %pad_maximum_fusion.refs_0_.refs_29_), channel_id=1, source_target_pairs={{0,4},{1,5},{2,6},{3,7},{4,0},{5,1},{6,2},{7,3},{8,12},{9,13},{10,... | collective-permute-start | bytes 3342344 | tf_op jit(solution)/shard_map/ppermute | solution.py:582
  49.2 18.0 %collective-permute-start.21 = (bf16[4,256,512]{2,1,0:T(8,128)(2,1)}, bf16[4,256,512]{2,1,0:T(8,128)(2,1)}, u32[]{:S(2)}, u32[]{:S(2)}) collective-permute-start(bf16[4,256,512]{2,1,0:T(8,128)(2,1)} %pad_maximum_fusion.2.refs_11_.refs_4_), channel_id=1, source_target_pairs={{0,2},{1,3},{2,0},{3,1},{4,6},{5,7},{6,4},{7,5},{8,10},{9,11},{10,... | collective-permute-start | bytes 3145736 | tf_op jit(solution)/shard_map/ppermute | solution.py:582
  50.1 17.3 %collective-permute-start.7 = (bf16[4,272,512]{2,1,0:T(8,128)(2,1)}, bf16[4,272,512]{2,1,0:T(8,128)(2,1)}, u32[]{:S(2)}, u32[]{:S(2)}) collective-permute-start(bf16[4,272,512]{2,1,0:T(8,128)(2,1)} %pad_maximum_fusion.refs_0_.refs_29_), channel_id=1, source_target_pairs={{0,16},{1,17},{2,18},{3,19},{4,20},{5,21},{6,22},{7,23},{8,24},{9,... | collective-permute-start | bytes 3342344 | tf_op jit(solution)/shard_map/ppermute | solution.py:582
  50.3 10.7 %collective-permute-start = (bf16[48,512]{1,0:T(8,128)(2,1)S(1)}, bf16[48,512]{1,0:T(8,128)(2,1)S(1)}, u32[]{:S(2)}, u32[]{:S(2)}) collective-permute-start(bf16[48,512]{1,0:T(8,128)(2,1)S(1)} %get-tuple-element.192), channel_id=1, source_target_pairs={{0,0},{1,16},{2,2},{3,18},{4,4},{5,20},{6,6},{7,22},{8,17},{9,1},{... | collective-permute-start | bytes 147464 | tf_op jit(solution)/shard_map/ppermute | solution.py:582
  67.2 22.8 %collective-permute-start.22 = (bf16[4,256,512]{2,1,0:T(8,128)(2,1)}, bf16[4,256,512]{2,1,0:T(8,128)(2,1)}, u32[]{:S(2)}, u32[]{:S(2)}) collective-permute-start(bf16[4,256,512]{2,1,0:T(8,128)(2,1)} %pad_maximum_fusion.2.refs_11_.refs_4_), channel_id=1, source_target_pairs={{0,16},{1,17},{2,18},{3,19},{4,20},{5,21},{6,22},{7,23},{8,24},{9,... | collective-permute-start | bytes 3145736 | tf_op jit(solution)/shard_map/ppermute | solution.py:582
  67.4 22.7 %collective-permute-start.23 = (bf16[4,256,512]{2,1,0:T(8,128)(2,1)}, bf16[4,256,512]{2,1,0:T(8,128)(2,1)}, u32[]{:S(2)}, u32[]{:S(2)}) collective-permute-start(bf16[4,256,512]{2,1,0:T(8,128)(2,1)} %collective-permute-done.21.refs_12_.refs_5_), channel_id=1, source_target_pairs={{0,16},{1,17},{2,18},{3,19},{4,20},{5,21},{6,22},{7,23},{8,24},{9,... | collective-permute-start | bytes 3145736 | tf_op jit(solution)/shard_map/ppermute | solution.py:582
  179.2 21.3 %collective-permute-start.35 = (bf16[4,256,512]{2,1,0:T(8,128)(2,1)}, bf16[4,256,512]{2,1,0:T(8,128)(2,1)S(1)}, u32[]{:S(2)}, u32[]{:S(2)}) collective-permute-start(bf16[4,256,512]{2,1,0:T(8,128)(2,1)} %get-tuple-element.130), channel_id=1, source_target_pairs={{0,2},{1,3},{2,0},{3,1},{4,6},{5,7},{6,4},{7,5},{8,10},{9,11},{10,... | collective-permute-start | bytes 3145736 | tf_op jit(solution)/shard_map/ppermute | solution.py:582
  204.7 23.7 %collective-permute-start.38 = (bf16[4,8,128,128]{3,2,1,0:T(8,128)(2,1)}, bf16[4,8,128,128]{3,2,1,0:T(8,128)(2,1)S(1)}, u32[]{:S(2)}, u32[]{:S(2)}) collective-permute-start(bf16[4,8,128,128]{3,2,1,0:T(8,128)(2,1)} %get-tuple-element.148), channel_id=1, source_target_pairs={{0,4},{1,5},{2,6},{3,7},{4,0},{5,1},{6,2},{7,3},{8,12},{9,13},{10,... | collective-permute-start | bytes 3145736 | tf_op jit(solution)/shard_map/ppermute | solution.py:582
  214.3 21.8 %collective-permute-start.44 = (bf16[4,272,512]{2,1,0:T(8,128)(2,1)}, bf16[4,272,512]{2,1,0:T(8,128)(2,1)S(1)}, u32[]{:S(2)}, u32[]{:S(2)}) collective-permute-start(bf16[4,272,512]{2,1,0:T(8,128)(2,1)} %get-tuple-element.166), channel_id=1, source_target_pairs={{0,1},{1,0},{2,3},{3,2},{4,5},{5,4},{6,7},{7,6},{8,9},{9,8},{10,11... | collective-permute-start | bytes 3342344 | tf_op jit(solution)/shard_map/ppermute | solution.py:582
  216.7 20.2 %collective-permute-start.36 = (bf16[32,512]{1,0:T(8,128)(2,1)S(1)}, bf16[32,512]{1,0:T(8,128)(2,1)S(1)}, u32[]{:S(2)}, u32[]{:S(2)}) collective-permute-start(bf16[32,512]{1,0:T(8,128)(2,1)S(1)} %get-tuple-element.188), channel_id=1, source_target_pairs={{0,0},{16,1},{2,2},{18,3},{4,4},{20,5},{6,6},{22,7},{17,8},{1,9},{... | collective-permute-start | bytes 98312 | tf_op jit(solution)/shard_map/ppermute | solution.py:582
  224.9 12.1 %collective-permute-start.37 = (bf16[32,512]{1,0:T(8,128)(2,1)S(1)}, bf16[32,512]{1,0:T(8,128)(2,1)S(1)}, u32[]{:S(2)}, u32[]{:S(2)}) collective-permute-start(bf16[32,512]{1,0:T(8,128)(2,1)S(1)} %get-tuple-element.189), channel_id=1, source_target_pairs={{2,0},{18,1},{0,2},{16,3},{6,4},{22,5},{4,6},{20,7},{19,8},{3,9},{... | collective-permute-start | bytes 98312 | tf_op jit(solution)/shard_map/ppermute | solution.py:582
  237.2 20.3 %collective-permute-start.40 = (bf16[1,8,128,128]{3,2,1,0:T(8,128)(2,1)S(1)}, bf16[1,8,128,128]{3,2,1,0:T(8,128)(2,1)S(1)}, u32[]{:S(2)}, u32[]{:S(2)}) collective-permute-start(bf16[1,8,128,128]{3,2,1,0:T(8,128)(2,1)S(1)} %add_convert_fusion.8), channel_id=1, source_target_pairs={{0,1},{1,0},{2,3},{3,2},{4,5},{5,4},{6,7},{7,6},{8,9},{9,8},{10,11... | collective-permute-start | bytes 786440 | tf_op jit(solution)/shard_map/ppermute | solution.py:582
  244.8 14.8 %collective-permute-start.46 = (bf16[1,272,512]{2,1,0:T(8,128)(2,1)S(1)}, bf16[1,272,512]{2,1,0:T(8,128)(2,1)S(1)}, u32[]{:S(2)}, u32[]{:S(2)}) collective-permute-start(bf16[1,272,512]{2,1,0:T(8,128)(2,1)S(1)} %add_convert_fusion.4), channel_id=1, source_target_pairs={{0,2},{1,3},{2,0},{3,1},{4,6},{5,7},{6,4},{7,5},{8,10},{9,11},{10,... | collective-permute-start | bytes 835592 | tf_op jit(solution)/shard_map/ppermute | solution.py:582
  246.7 18.3 %collective-permute-start.48 = (bf16[256,512]{1,0:T(8,128)(2,1)S(1)}, bf16[256,512]{1,0:T(8,128)(2,1)S(1)}, u32[]{:S(2)}, u32[]{:S(2)}) collective-permute-start(bf16[256,512]{1,0:T(8,128)(2,1)S(1)} %fusion.2), channel_id=1, source_target_pairs={{0,0},{1,1},{2,2},{3,3},{4,4},{5,5},{6,6},{7,7},{8,16},{9,17},{10,... | collective-permute-start | bytes 786440 | tf_op jit(solution)/shard_map/ppermute | solution.py:582
  257.7 15.3 %collective-permute-start.41 = (bf16[8,128,128]{2,1,0:T(8,128)(2,1)S(1)}, bf16[8,128,128]{2,1,0:T(8,128)(2,1)S(1)}, u32[]{:S(2)}, u32[]{:S(2)}) collective-permute-start(bf16[8,128,128]{2,1,0:T(8,128)(2,1)S(1)} %fusion.1), channel_id=1, source_target_pairs={{0,0},{1,1},{2,2},{3,3},{4,4},{5,5},{6,6},{7,7},{8,16},{9,17},{10,... | collective-permute-start | bytes 786440 | tf_op jit(solution)/shard_map/ppermute | solution.py:582
  259.8 16.2 %collective-permute-start.47 = (bf16[272,512]{1,0:T(8,128)(2,1)S(1)}, bf16[272,512]{1,0:T(8,128)(2,1)S(1)}, u32[]{:S(2)}, u32[]{:S(2)}) collective-permute-start(bf16[272,512]{1,0:T(8,128)(2,1)S(1)} %fusion), channel_id=1, source_target_pairs={{0,0},{1,1},{2,2},{3,3},{4,4},{5,5},{6,6},{7,7},{8,16},{9,17},{10,... | collective-permute-start | bytes 835592 | tf_op jit(solution)/shard_map/ppermute | solution.py:582
  (57 other events, 319.4 us)

commit v4 on v3

--- a/solution.py
+++ b/solution.py
@@ -15,7 +15,7 @@
 F32 = jnp.float32
 BF16 = jnp.bfloat16
 LANES = 128
-VMEM_LIMIT = 56 * 1024 * 1024
+VMEM_LIMIT = 28 * 1024 * 1024
 
 ORDER_A = 0
 ORDER_B = 1
@@ -848,8 +848,9 @@
     got_c = round_of(pieces_c, got_c, 2)
     pieces_a = w(1, [(n0, db0), (dl0, a0)], fcols, True, (gm2, gm0, gi2, gf0, gf1))
     got_a = round_of(pieces_a, [], 1)
-    got_c[2], got_a[0] = lax.optimization_barrier((got_c[2], got_a[0]))
     grad_c = scatter(pieces_c, got_c, 2)
+    got_a = round_of(pieces_a, got_a, 1)
+    got_a[1], grad_c = lax.optimization_barrier((got_a[1], grad_c))
     grad_b = scatter(pieces_b, got_b, 0)
     grad_a = scatter(pieces_a, got_a, 1)
 

time: 282 us -> 265 us (0.940)
  Pallas kernels: 96.9 us -> 82.2 us
  local copies, waits for them, and re-layouts: 9.96 us -> 4.55 us
  other arithmetic: 14.5 us -> 19.9 us
    pallas_call x12, Pallas kernels: 96.9 us -> 82.2 us  [call(): pl.pallas_call(kernel, out_shape=[jax.ShapeDtypeStruct(s, d) for s, d in...]
    unnamed x67 -> x21, local copies, waits for them, and re-layouts: 6.88 us -> 2.12 us
    convert_element_type x6, other arithmetic: 1.75 us -> 5.77 us  [round_of(): return got + [permute(total.astype(BF16), bit_pairs(bit))]]
    convert_element_type x3, other arithmetic: 0.43 us -> 3.28 us  [round_of(): return permute(total[0].astype(BF16), swap_pairs)]
  transfers between devices with their start and end apart: 49 -> 49, of which waited for: 24 -> 29; matrix products, arithmetic and copies ran while one was open for 6% -> 8% of each run, Pallas kernels for 14% -> 12%
where the time goes in v4:
time: 265 us; the launch traced here: 263 us
  starting transfers between devices  91 us (34%)
  Pallas kernels  82.2 us (31%)
  waiting for transfers between devices  63.4 us (24%)
  other arithmetic  19.9 us (8%)
  local copies, waits for them, and re-layouts  4.55 us (2%)
    ppermute x49, starting transfers between devices, permute(): return lax.ppermute(value, ('pipe', 'dp', 'tensor'), pairs)  91 us
    pallas_call x12, Pallas kernels, call(): pl.pallas_call(kernel, out_shape=[jax.ShapeDtypeStruct(s, d) for s, d in...  82.2 us
    ppermute x49, waiting for transfers between devices, permute(): return lax.ppermute(value, ('pipe', 'dp', 'tensor'), pairs)  63.4 us
    concatenate x6, other arithmetic, spread(): held = jnp.concatenate([held, permute(held, bit_pairs(b))], axis=0)  7.19 us
    convert_element_type x6, other arithmetic, round_of(): return got + [permute(total.astype(BF16), bit_pairs(bit))]  5.77 us
  transfers between devices with their start and end apart: 49, of which 29 were waited for; matrix products, arithmetic and copies ran while one was open for 8% of the time, Pallas kernels for 12%

profile of v4, /device:TPU:1, one launch (start us, length us, event | category | flops | bytes accessed | tf_op | source)
XLA Modules:
  0.0 263.1 jit_solution(3558495986472430172)
XLA Ops:
  0.6 5.6 %collective-permute-start.9 = (bf16[8,128,128]{2,1,0:T(8,128)(2,1)}, bf16[8,128,128]{2,1,0:T(8,128)(2,1)S(1)}, u32[]{:S(2)}, u32[]{:S(2)}) collective-permute-start(bf16[8,128,128]{2,1,0:T(8,128)(2,1)} %bitcast.115), channel_id=1, source_target_pairs={{0,0},{1,1},{2,2},{3,3},{4,4},{5,5},{6,6},{7,7},{8,16},{9,17},{10,... | collective-permute-start | bytes 786440 | tf_op jit(solution)/shard_map/ppermute | solution.py:582
  10.8 4.5 %collective-permute-start.18 = (bf16[256,512]{1,0:T(8,128)(2,1)S(1)}, bf16[256,512]{1,0:T(8,128)(2,1)S(1)}, u32[]{:S(2)}, u32[]{:S(2)}) collective-permute-start(bf16[256,512]{1,0:T(8,128)(2,1)S(1)} %bitcast.103), channel_id=1, source_target_pairs={{0,0},{1,1},{2,2},{3,3},{4,4},{5,5},{6,6},{7,7},{8,16},{9,17},{10,... | collective-permute-start | bytes 786440 | tf_op jit(solution)/shard_map/ppermute | solution.py:582
  22.0 3.2 %collective-permute-done.18 = bf16[256,512]{1,0:T(8,128)(2,1)S(1)} collective-permute-done((bf16[256,512]{1,0:T(8,128)(2,1)S(1)}, bf16[256,512]{1,0:T(8,128)(2,1)S(1)}, u32[]{:S(2)}, u32[]{:S(2)}) %collective-permute-start.18) | collective-permute-done | bytes 262176 | tf_op jit(solution)/shard_map/ppermute | solution.py:582
  34.4 4.3 %collective-permute-done.11 = bf16[2,8,128,128]{3,2,1,0:T(8,128)(2,1)} collective-permute-done((bf16[2,8,128,128]{3,2,1,0:T(8,128)(2,1)S(1)}, bf16[2,8,128,128]{3,2,1,0:T(8,128)(2,1)}, u32[]{:S(2)}, u32[]{:S(2)}) %collective-permute-start.11) | collective-permute-done | bytes 524320 | tf_op jit(solution)/shard_map/ppermute | solution.py:582
  50.3 4.9 %collective-permute-start = (bf16[48,512]{1,0:T(8,128)(2,1)S(1)}, bf16[48,512]{1,0:T(8,128)(2,1)S(1)}, u32[]{:S(2)}, u32[]{:S(2)}) collective-permute-start(bf16[48,512]{1,0:T(8,128)(2,1)S(1)} %get-tuple-element.192), channel_id=1, source_target_pairs={{0,0},{1,16},{2,2},{3,18},{4,4},{5,20},{6,6},{7,22},{8,17},{9,1},{... | collective-permute-start | bytes 147464 | tf_op jit(solution)/shard_map/ppermute | solution.py:582
  55.2 5.8 %collective-permute-done = bf16[48,512]{1,0:T(8,128)(2,1)S(1)} collective-permute-done((bf16[48,512]{1,0:T(8,128)(2,1)S(1)}, bf16[48,512]{1,0:T(8,128)(2,1)S(1)}, u32[]{:S(2)}, u32[]{:S(2)}) %collective-permute-start) | collective-permute-done | bytes 49184 | tf_op jit(solution)/shard_map/ppermute | solution.py:582
  73.0 9.6 %layer_front.2 = (f32[128,512]{1,0:T(8,128)S(1)}, f32[128,512]{1,0:T(8,128)S(1)}, f32[8,512]{1,0:T(8,128)S(1)}, f32[128,512]{1,0:T(8,128)}, f32[128,2048]{1,0:T(...) custom-call(s32[4]{0:T(128)S(1)} %pad_add_fusion.meta, ...), custom_call_target="tpu_custom_call" | custom-call | flops 1006632960 | bytes 9355280 | tf_op jit(solution)/shard_map/layer_front/pallas_call | solution.py:569
  82.6 5.7 %collective-permute-start.17 = (f32[1,8,512]{2,1,0:T(8,128)S(1)}, f32[1,8,512]{2,1,0:T(8,128)S(1)}, u32[]{:S(2)}, u32[]{:S(2)}) collective-permute-start(f32[1,8,512]{2,1,0:T(8,128)S(1)} %bitcast.82), channel_id=1, source_target_pairs={{0,5},{1,4},{2,7},{3,6},{4,1},{5,0},{6,3},{7,2},{8,13},{9,12},{10,... | collective-permute-start | bytes 49160 | tf_op jit(solution)/shard_map/ppermute | solution.py:582
  90.9 4.9 %layer_rear.1 = (bf16[128,512]{1,0:T(8,128)(2,1)S(1)}, f32[128,512]{1,0:T(8,128)}, f32[128,2048]{1,0:T(8,128)}, f32[128,512]{1,0:T(8,128)}, f32[8,512]{1,0:T(8,128)}) custom-call(s32[4]{0:T(128)S(1)} %pad_add_fusion.meta, f32[128,512]{1,0:T(8,128)S(1)} %get-tuple-element.92.s2_ref, f32[128,512]{1,0:T(8,128)S(1)} %get-tuple-element.93.filt_ref, ...), custom_call_target="tpu_custom_call" | custom-call | flops 603979776 | bytes 9158672 | tf_op jit(solution)/shard_map/layer_rear/pallas_call | solution.py:569
  100.2 8.8 %layer_front.3 = (f32[128,512]{1,0:T(8,128)S(1)}, f32[128,512]{1,0:T(8,128)S(1)}, f32[8,512]{1,0:T(8,128)S(1)}, f32[128,512]{1,0:T(8,128)S(1)}, f32[128,2048]{1,...) custom-call(s32[4]{0:T(128)S(1)} %pad_add_fusion.meta, ...), custom_call_target="tpu_custom_call" | custom-call | flops 1006632960 | bytes 9355280 | tf_op jit(solution)/shard_map/layer_front/pallas_call | solution.py:569
  116.1 6.9 %layer_turn.1 = (bf16[128,512]{1,0:T(8,128)(2,1)S(1)}, f32[128,512]{1,0:T(8,128)S(1)}, f32[128,2048]{1,0:T(8,128)S(1)}, f32[128,512]{1,0:T(8,128)S(1)}, f32[8,51...) custom-call(s32[4]{0:T(128)S(1)} %pad_add_fusion.meta, ...), custom_call_target="tpu_custom_call" | custom-call | flops 1207959552 | bytes 9289744 | tf_op jit(solution)/shard_map/layer_turn/pallas_call | solution.py:569
  127.9 24.3 %back_whole.1 = (f32[128,512]{1,0:T(8,128)}, bf16[128,512]{1,0:T(8,128)(2,1)}, bf16[128,512]{1,0:T(8,128)(2,1)}, bf16[128,512]{1,0:T(8,128)(2,1)}, bf16[128,512]...) custom-call(s32[4]{0:T(128)S(1)} %pad_add_fusion.meta, ...), custom_call_target="tpu_custom_call" | custom-call | flops 1610612736 | bytes 13336592 | tf_op jit(solution)/shard_map/back_whole/pallas_call | solution.py:569
  153.5 6.8 %collective-permute-done.31.gb_ref = bf16[128,512]{1,0:T(8,128)(2,1)S(1)} collective-permute-done((bf16[128,512]{1,0:T(8,128)(2,1)S(1)}, bf16[128,512]{1,0:T(8,128)(2,1)S(1)}, u32[]{:S(2)}, u32[]{:S(2)}) %collective-permute-start.31) | collective-permute-done | bytes 131104 | tf_op jit(solution)/shard_map/ppermute | solution.py:582
  160.3 4.6 %back_rear.1 = (f32[128,512]{1,0:T(8,128)S(1)}, f32[128,512]{1,0:T(8,128)S(1)}, f32[8,512]{1,0:T(8,128)S(1)}, bf16[128,512]{1,0:T(8,128)(2,1)S(1)}, bf16[128,204...) custom-call(s32[4]{0:T(128)S(1)} %pad_add_fusion.meta, ...), custom_call_target="tpu_custom_call" | custom-call | flops 603979776 | bytes 10616848 | tf_op jit(solution)/shard_map/back_rear/pallas_call | solution.py:569
  171.9 10.3 %back_front.1 = (f32[128,512]{1,0:T(8,128)S(1)}, bf16[128,512]{1,0:T(8,128)(2,1)S(1)}, bf16[128,512]{1,0:T(8,128)(2,1)S(1)}, bf16[128,512]{1,0:T(8,128)(2,1)S(1)...) custom-call(s32[4]{0:T(128)S(1)} %pad_add_fusion.meta, ...), custom_call_target="tpu_custom_call" | custom-call | flops 1073741824 | bytes 7569424 | tf_op jit(solution)/shard_map/back_front/pallas_call | solution.py:569
  182.1 5.2 %collective-permute-done.35 = bf16[4,256,512]{2,1,0:T(8,128)(2,1)S(1)} collective-permute-done((bf16[4,256,512]{2,1,0:T(8,128)(2,1)S(1)}, bf16[4,256,512]{2,1,0:T(8,128)(2,1)S(1)}, u32[]{:S(2)}, u32[]{:S(2)}) %collective-permute-start.35) | collective-permute-done | bytes 1048608 | tf_op jit(solution)/shard_map/ppermute | solution.py:582
  190.5 4.1 %back_first.1 = (bf16[128,512]{1,0:T(8,128)(2,1)S(1)}, bf16[128,512]{1,0:T(8,128)(2,1)S(1)}, bf16[128,2048]{1,0:T(8,128)(2,1)S(1)}, f32[8,512]{1,0:T(8,128)S(1)}, f32[1,2048]{1,0:T(1,128)S(1)}) custom-call(s32[4]{0:T(128)S(1)} %pad_add_fusion.meta, f32[128,512]{1,0:T(8,128)S(1)} %get-tuple-element.145.ds1_ref, bf16[128,512]{1,0:T(8,128)(2,1)S(1)} %bitcast.73, ...), custom_call_target="tpu_custom_call" | custom-call | flops 536870912 | bytes 6062096 | tf_op jit(solution)/shard_map/back_first/pallas_call | solution.py:569
  198.9 9.1 %collective-permute-start.36 = (bf16[32,512]{1,0:T(8,128)(2,1)S(1)}, bf16[32,512]{1,0:T(8,128)(2,1)S(1)}, u32[]{:S(2)}, u32[]{:S(2)}) collective-permute-start(bf16[32,512]{1,0:T(8,128)(2,1)S(1)} %get-tuple-element.188), channel_id=1, source_target_pairs={{0,0},{16,1},{2,2},{18,3},{4,4},{20,5},{6,6},{22,7},{17,8},{1,9},{... | collective-permute-start | bytes 98312 | tf_op jit(solution)/shard_map/ppermute | solution.py:582
  214.7 4.9 %collective-permute-done.43 = bf16[4,272,512]{2,1,0:T(8,128)(2,1)} collective-permute-done((bf16[4,272,512]{2,1,0:T(8,128)(2,1)}, bf16[4,272,512]{2,1,0:T(8,128)(2,1)}, u32[]{:S(2)}, u32[]{:S(2)}) %collective-permute-start.43) | collective-permute-done | bytes 1114144 | tf_op jit(solution)/shard_map/ppermute | solution.py:582
  222.0 9.8 %collective-permute-start.46 = (bf16[256,512]{1,0:T(8,128)(2,1)S(1)}, bf16[256,512]{1,0:T(8,128)(2,1)S(1)}, u32[]{:S(2)}, u32[]{:S(2)}) collective-permute-start(bf16[256,512]{1,0:T(8,128)(2,1)S(1)} %fusion.2), channel_id=1, source_target_pairs={{0,0},{1,1},{2,2},{3,3},{4,4},{5,5},{6,6},{7,7},{8,16},{9,17},{10,... | collective-permute-start | bytes 786440 | tf_op jit(solution)/shard_map/ppermute | solution.py:582
  233.0 4.5 %collective-permute-done.46 = bf16[256,512]{1,0:T(8,128)(2,1)S(1)} collective-permute-done((bf16[256,512]{1,0:T(8,128)(2,1)S(1)}, bf16[256,512]{1,0:T(8,128)(2,1)S(1)}, u32[]{:S(2)}, u32[]{:S(2)}) %collective-permute-start.46) | collective-permute-done | bytes 262176 | tf_op jit(solution)/shard_map/ppermute | solution.py:582
  241.8 5.2 %collective-permute-start.41 = (bf16[8,128,128]{2,1,0:T(8,128)(2,1)S(1)}, bf16[8,128,128]{2,1,0:T(8,128)(2,1)S(1)}, u32[]{:S(2)}, u32[]{:S(2)}) collective-permute-start(bf16[8,128,128]{2,1,0:T(8,128)(2,1)S(1)} %fusion.1), channel_id=1, source_target_pairs={{0,0},{1,1},{2,2},{3,3},{4,4},{5,5},{6,6},{7,7},{8,16},{9,17},{10,... | collective-permute-start | bytes 786440 | tf_op jit(solution)/shard_map/ppermute | solution.py:582
  248.1 3.6 %collective-permute-start.48 = (bf16[272,512]{1,0:T(8,128)(2,1)S(1)}, bf16[272,512]{1,0:T(8,128)(2,1)S(1)}, u32[]{:S(2)}, u32[]{:S(2)}) collective-permute-start(bf16[272,512]{1,0:T(8,128)(2,1)S(1)} %fusion), channel_id=1, source_target_pairs={{0,0},{1,1},{2,2},{3,3},{4,4},{5,5},{6,6},{7,7},{8,16},{9,17},{10,... | collective-permute-start | bytes 835592 | tf_op jit(solution)/shard_map/ppermute | solution.py:582
  254.7 5.1 %collective-permute-done.48 = bf16[272,512]{1,0:T(8,128)(2,1)S(1)} collective-permute-done((bf16[272,512]{1,0:T(8,128)(2,1)S(1)}, bf16[272,512]{1,0:T(8,128)(2,1)S(1)}, u32[]{:S(2)}, u32[]{:S(2)}) %collective-permute-start.48) | collective-permute-done | bytes 278560 | tf_op jit(solution)/shard_map/ppermute | solution.py:582
  (156 shorter events, 99.4 us)
Async XLA Ops:
  0.6 14.7 %collective-permute-start.9 = (bf16[8,128,128]{2,1,0:T(8,128)(2,1)}, bf16[8,128,128]{2,1,0:T(8,128)(2,1)S(1)}, u32[]{:S(2)}, u32[]{:S(2)}) collective-permute-start(bf16[8,128,128]{2,1,0:T(8,128)(2,1)} %bitcast.115), channel_id=1, source_target_pairs={{0,0},{1,1},{2,2},{3,3},{4,4},{5,5},{6,6},{7,7},{8,16},{9,17},{10,... | collective-permute-start | bytes 786440 | tf_op jit(solution)/shard_map/ppermute | solution.py:582
  8.9 10.8 %collective-permute-start.3 = (bf16[272,512]{1,0:T(8,128)(2,1)S(1)}, bf16[272,512]{1,0:T(8,128)(2,1)S(1)}, u32[]{:S(2)}, u32[]{:S(2)}) collective-permute-start(bf16[272,512]{1,0:T(8,128)(2,1)S(1)} %pad_maximum_fusion.6), channel_id=1, source_target_pairs={{0,0},{1,1},{2,2},{3,3},{4,4},{5,5},{6,6},{7,7},{8,16},{9,17},{10,... | collective-permute-start | bytes 835592 | tf_op jit(solution)/shard_map/ppermute | solution.py:582
  10.8 14.5 %collective-permute-start.18 = (bf16[256,512]{1,0:T(8,128)(2,1)S(1)}, bf16[256,512]{1,0:T(8,128)(2,1)S(1)}, u32[]{:S(2)}, u32[]{:S(2)}) collective-permute-start(bf16[256,512]{1,0:T(8,128)(2,1)S(1)} %bitcast.103), channel_id=1, source_target_pairs={{0,0},{1,1},{2,2},{3,3},{4,4},{5,5},{6,6},{7,7},{8,16},{9,17},{10,... | collective-permute-start | bytes 786440 | tf_op jit(solution)/shard_map/ppermute | solution.py:582
  15.3 12.2 %collective-permute-start.10 = (bf16[1,8,128,128]{3,2,1,0:T(8,128)(2,1)S(1)}, bf16[1,8,128,128]{3,2,1,0:T(8,128)(2,1)S(1)}, u32[]{:S(2)}, u32[]{:S(2)}) collective-permute-start(bf16[1,8,128,128]{3,2,1,0:T(8,128)(2,1)S(1)} %bitcast.98), channel_id=1, source_target_pairs={{0,2},{1,3},{2,0},{3,1},{4,6},{5,7},{6,4},{7,5},{8,10},{9,11},{10,... | collective-permute-start | bytes 786440 | tf_op jit(solution)/shard_map/ppermute | solution.py:582
  27.7 11.0 %collective-permute-start.11 = (bf16[2,8,128,128]{3,2,1,0:T(8,128)(2,1)S(1)}, bf16[2,8,128,128]{3,2,1,0:T(8,128)(2,1)}, u32[]{:S(2)}, u32[]{:S(2)}) collective-permute-start(bf16[2,8,128,128]{3,2,1,0:T(8,128)(2,1)S(1)} %pad_maximum_fusion.4), channel_id=1, source_target_pairs={{0,4},{1,5},{2,6},{3,7},{4,0},{5,1},{6,2},{7,3},{8,12},{9,13},{10,... | collective-permute-start | bytes 1572872 | tf_op jit(solution)/shard_map/ppermute | solution.py:582
  29.3 12.1 %collective-permute-start.5 = (bf16[2,272,512]{2,1,0:T(8,128)(2,1)}, bf16[2,272,512]{2,1,0:T(8,128)(2,1)}, u32[]{:S(2)}, u32[]{:S(2)}) collective-permute-start(bf16[2,272,512]{2,1,0:T(8,128)(2,1)} %pad_maximum_fusion.3), channel_id=1, source_target_pairs={{0,2},{1,3},{2,0},{3,1},{4,6},{5,7},{6,4},{7,5},{8,10},{9,11},{10,... | collective-permute-start | bytes 1671176 | tf_op jit(solution)/shard_map/ppermute | solution.py:582
  32.8 14.3 %collective-permute-start.20 = (bf16[2,256,512]{2,1,0:T(8,128)(2,1)}, bf16[2,256,512]{2,1,0:T(8,128)(2,1)}, u32[]{:S(2)}, u32[]{:S(2)}) collective-permute-start(bf16[2,256,512]{2,1,0:T(8,128)(2,1)} %pad_maximum_fusion.5), channel_id=1, source_target_pairs={{0,1},{1,0},{2,3},{3,2},{4,5},{5,4},{6,7},{7,6},{8,9},{9,8},{10,11... | collective-permute-start | bytes 1572872 | tf_op jit(solution)/shard_map/ppermute | solution.py:582
  39.8 27.0 %collective-permute-start.12 = (bf16[4,8,128,128]{3,2,1,0:T(8,128)(2,1)S(1)}, bf16[4,8,128,128]{3,2,1,0:T(8,128)(2,1)S(1)}, u32[]{:S(2)}, u32[]{:S(2)}) collective-permute-start(bf16[4,8,128,128]{3,2,1,0:T(8,128)(2,1)S(1)} %pad_maximum_fusion.1.refs_4_.refs_7_.refs_22_.refs_0_.refs_20_), channel_id=1, source_target_pairs={{0,1},{1,0},{2,3},{3,2},{4,5},{5,4},{6,7},{7,6},{8,9},{9,8},{10,11... | collective-permute-start | bytes 3145736 | tf_op jit(solution)/shard_map/ppermute | solution.py:582
  43.6 21.8 %collective-permute-start.6 = (bf16[4,272,512]{2,1,0:T(8,128)(2,1)}, bf16[4,272,512]{2,1,0:T(8,128)(2,1)}, u32[]{:S(2)}, u32[]{:S(2)}) collective-permute-start(bf16[4,272,512]{2,1,0:T(8,128)(2,1)} %pad_maximum_fusion.refs_0_.refs_29_), channel_id=1, source_target_pairs={{0,4},{1,5},{2,6},{3,7},{4,0},{5,1},{6,2},{7,3},{8,12},{9,13},{10,... | collective-permute-start | bytes 3342344 | tf_op jit(solution)/shard_map/ppermute | solution.py:582
  49.2 18.0 %collective-permute-start.21 = (bf16[4,256,512]{2,1,0:T(8,128)(2,1)}, bf16[4,256,512]{2,1,0:T(8,128)(2,1)}, u32[]{:S(2)}, u32[]{:S(2)}) collective-permute-start(bf16[4,256,512]{2,1,0:T(8,128)(2,1)} %pad_maximum_fusion.2.refs_11_.refs_4_), channel_id=1, source_target_pairs={{0,2},{1,3},{2,0},{3,1},{4,6},{5,7},{6,4},{7,5},{8,10},{9,11},{10,... | collective-permute-start | bytes 3145736 | tf_op jit(solution)/shard_map/ppermute | solution.py:582
  50.1 17.3 %collective-permute-start.7 = (bf16[4,272,512]{2,1,0:T(8,128)(2,1)}, bf16[4,272,512]{2,1,0:T(8,128)(2,1)}, u32[]{:S(2)}, u32[]{:S(2)}) collective-permute-start(bf16[4,272,512]{2,1,0:T(8,128)(2,1)} %pad_maximum_fusion.refs_0_.refs_29_), channel_id=1, source_target_pairs={{0,16},{1,17},{2,18},{3,19},{4,20},{5,21},{6,22},{7,23},{8,24},{9,... | collective-permute-start | bytes 3342344 | tf_op jit(solution)/shard_map/ppermute | solution.py:582
  50.3 10.7 %collective-permute-start = (bf16[48,512]{1,0:T(8,128)(2,1)S(1)}, bf16[48,512]{1,0:T(8,128)(2,1)S(1)}, u32[]{:S(2)}, u32[]{:S(2)}) collective-permute-start(bf16[48,512]{1,0:T(8,128)(2,1)S(1)} %get-tuple-element.192), channel_id=1, source_target_pairs={{0,0},{1,16},{2,2},{3,18},{4,4},{5,20},{6,6},{7,22},{8,17},{9,1},{... | collective-permute-start | bytes 147464 | tf_op jit(solution)/shard_map/ppermute | solution.py:582
  67.2 21.4 %collective-permute-start.22 = (bf16[4,256,512]{2,1,0:T(8,128)(2,1)}, bf16[4,256,512]{2,1,0:T(8,128)(2,1)}, u32[]{:S(2)}, u32[]{:S(2)}) collective-permute-start(bf16[4,256,512]{2,1,0:T(8,128)(2,1)} %pad_maximum_fusion.2.refs_11_.refs_4_), channel_id=1, source_target_pairs={{0,16},{1,17},{2,18},{3,19},{4,20},{5,21},{6,22},{7,23},{8,24},{9,... | collective-permute-start | bytes 3145736 | tf_op jit(solution)/shard_map/ppermute | solution.py:582
  67.4 21.3 %collective-permute-start.23 = (bf16[4,256,512]{2,1,0:T(8,128)(2,1)}, bf16[4,256,512]{2,1,0:T(8,128)(2,1)}, u32[]{:S(2)}, u32[]{:S(2)}) collective-permute-start(bf16[4,256,512]{2,1,0:T(8,128)(2,1)} %collective-permute-done.21.refs_12_.refs_5_), channel_id=1, source_target_pairs={{0,16},{1,17},{2,18},{3,19},{4,20},{5,21},{6,22},{7,23},{8,24},{9,... | collective-permute-start | bytes 3145736 | tf_op jit(solution)/shard_map/ppermute | solution.py:582
  166.4 21.0 %collective-permute-start.35 = (bf16[4,256,512]{2,1,0:T(8,128)(2,1)S(1)}, bf16[4,256,512]{2,1,0:T(8,128)(2,1)S(1)}, u32[]{:S(2)}, u32[]{:S(2)}) collective-permute-start(bf16[4,256,512]{2,1,0:T(8,128)(2,1)S(1)} %get-tuple-element.130), channel_id=1, source_target_pairs={{0,2},{1,3},{2,0},{3,1},{4,6},{5,7},{6,4},{7,5},{8,10},{9,11},{10,... | collective-permute-start | bytes 3145736 | tf_op jit(solution)/shard_map/ppermute | solution.py:582
  190.5 20.5 %collective-permute-start.38 = (bf16[4,8,128,128]{3,2,1,0:T(8,128)(2,1)}, bf16[4,8,128,128]{3,2,1,0:T(8,128)(2,1)}, u32[]{:S(2)}, u32[]{:S(2)}) collective-permute-start(bf16[4,8,128,128]{3,2,1,0:T(8,128)(2,1)} %get-tuple-element.148), channel_id=1, source_target_pairs={{0,4},{1,5},{2,6},{3,7},{4,0},{5,1},{6,2},{7,3},{8,12},{9,13},{10,... | collective-permute-start | bytes 3145736 | tf_op jit(solution)/shard_map/ppermute | solution.py:582
  198.8 20.8 %collective-permute-start.43 = (bf16[4,272,512]{2,1,0:T(8,128)(2,1)}, bf16[4,272,512]{2,1,0:T(8,128)(2,1)}, u32[]{:S(2)}, u32[]{:S(2)}) collective-permute-start(bf16[4,272,512]{2,1,0:T(8,128)(2,1)} %get-tuple-element.164), channel_id=1, source_target_pairs={{0,1},{1,0},{2,3},{3,2},{4,5},{5,4},{6,7},{7,6},{8,9},{9,8},{10,11... | collective-permute-start | bytes 3342344 | tf_op jit(solution)/shard_map/ppermute | solution.py:582
  198.9 32.9 %collective-permute-start.36 = (bf16[32,512]{1,0:T(8,128)(2,1)S(1)}, bf16[32,512]{1,0:T(8,128)(2,1)S(1)}, u32[]{:S(2)}, u32[]{:S(2)}) collective-permute-start(bf16[32,512]{1,0:T(8,128)(2,1)S(1)} %get-tuple-element.188), channel_id=1, source_target_pairs={{0,0},{16,1},{2,2},{18,3},{4,4},{20,5},{6,6},{22,7},{17,8},{1,9},{... | collective-permute-start | bytes 98312 | tf_op jit(solution)/shard_map/ppermute | solution.py:582
  208.0 23.8 %collective-permute-start.37 = (bf16[32,512]{1,0:T(8,128)(2,1)S(1)}, bf16[32,512]{1,0:T(8,128)(2,1)S(1)}, u32[]{:S(2)}, u32[]{:S(2)}) collective-permute-start(bf16[32,512]{1,0:T(8,128)(2,1)S(1)} %get-tuple-element.189), channel_id=1, source_target_pairs={{2,0},{18,1},{0,2},{16,3},{6,4},{22,5},{4,6},{20,7},{19,8},{3,9},{... | collective-permute-start | bytes 98312 | tf_op jit(solution)/shard_map/ppermute | solution.py:582
  212.2 19.7 %collective-permute-start.39 = (bf16[2,8,128,128]{3,2,1,0:T(8,128)(2,1)S(1)}, bf16[2,8,128,128]{3,2,1,0:T(8,128)(2,1)S(1)}, u32[]{:S(2)}, u32[]{:S(2)}) collective-permute-start(bf16[2,8,128,128]{3,2,1,0:T(8,128)(2,1)S(1)} %add_convert_fusion.2), channel_id=1, source_target_pairs={{0,2},{1,3},{2,0},{3,1},{4,6},{5,7},{6,4},{7,5},{8,10},{9,11},{10,... | collective-permute-start | bytes 1572872 | tf_op jit(solution)/shard_map/ppermute | solution.py:582
  220.8 16.6 %collective-permute-start.44 = (bf16[2,272,512]{2,1,0:T(8,128)(2,1)S(1)}, bf16[2,272,512]{2,1,0:T(8,128)(2,1)S(1)}, u32[]{:S(2)}, u32[]{:S(2)}) collective-permute-start(bf16[2,272,512]{2,1,0:T(8,128)(2,1)S(1)} %add_convert_fusion), channel_id=1, source_target_pairs={{0,4},{1,5},{2,6},{3,7},{4,0},{5,1},{6,2},{7,3},{8,12},{9,13},{10,... | collective-permute-start | bytes 1671176 | tf_op jit(solution)/shard_map/ppermute | solution.py:582
  222.0 15.5 %collective-permute-start.46 = (bf16[256,512]{1,0:T(8,128)(2,1)S(1)}, bf16[256,512]{1,0:T(8,128)(2,1)S(1)}, u32[]{:S(2)}, u32[]{:S(2)}) collective-permute-start(bf16[256,512]{1,0:T(8,128)(2,1)S(1)} %fusion.2), channel_id=1, source_target_pairs={{0,0},{1,1},{2,2},{3,3},{4,4},{5,5},{6,6},{7,7},{8,16},{9,17},{10,... | collective-permute-start | bytes 786440 | tf_op jit(solution)/shard_map/ppermute | solution.py:582
  241.8 12.0 %collective-permute-start.41 = (bf16[8,128,128]{2,1,0:T(8,128)(2,1)S(1)}, bf16[8,128,128]{2,1,0:T(8,128)(2,1)S(1)}, u32[]{:S(2)}, u32[]{:S(2)}) collective-permute-start(bf16[8,128,128]{2,1,0:T(8,128)(2,1)S(1)} %fusion.1), channel_id=1, source_target_pairs={{0,0},{1,1},{2,2},{3,3},{4,4},{5,5},{6,6},{7,7},{8,16},{9,17},{10,... | collective-permute-start | bytes 786440 | tf_op jit(solution)/shard_map/ppermute | solution.py:582
  248.1 11.8 %collective-permute-start.48 = (bf16[272,512]{1,0:T(8,128)(2,1)S(1)}, bf16[272,512]{1,0:T(8,128)(2,1)S(1)}, u32[]{:S(2)}, u32[]{:S(2)}) collective-permute-start(bf16[272,512]{1,0:T(8,128)(2,1)S(1)} %fusion), channel_id=1, source_target_pairs={{0,0},{1,1},{2,2},{3,3},{4,4},{5,5},{6,6},{7,7},{8,16},{9,17},{10,... | collective-permute-start | bytes 835592 | tf_op jit(solution)/shard_map/ppermute | solution.py:582
  (34 other events, 195.0 us)

commit v5 on v4

--- a/solution.py
+++ b/solution.py
@@ -170,7 +170,7 @@
     vm_ref[...], vi_ref[...], vf_ref[...] = totals
 
 
-def f1_kernel(dims, meta, xa_ref, xb_ref, vm_ref, vi_ref, vf_ref, pos_ref, *refs):
+def f1_kernel(dims, ready, meta, xa_ref, xb_ref, vm_ref, vi_ref, vf_ref, pos_ref, *refs):
     part_a, part_b, refs = refs[:PARTS_A], refs[PARTS_A:PARTS_A + PARTS_B], refs[PARTS_A + PARTS_B:]
     (s2_ref, filt_ref, stat_ref, s1_ref, before_ref, act_ref, qu_ref, qv_ref, k_ref, v_ref,
      rel_ref, probs_ref, ctx_ref, gi_ref, gs_ref, wa, wb, pad, sems) = refs
@@ -190,7 +190,7 @@
     s1 = x + 0.5 * (nt(active, wa[1]) + vm(2))
     s1_ref[...] = s1
     wait_weights(wb, sems.at[1])
-    rel_ref[...] = nn(pos_ref[...], wb[4]).astype(BF16)
+    rel_ref[...] = pos_ref[...] if ready else nn(pos_ref[...], wb[4]).astype(BF16)
     n1 = ln(s1, vm(3), vm(4)).astype(BF16)
     q = nn(n1, wb[0]) + vi(0)
     qu_ref[...] = (q + vi(2)).astype(BF16)
@@ -690,10 +690,10 @@
         [pltpu.VMEM((2 * slots, 16, 4 * LANES), BF16), sem_s], 1, 0, "vectors",
     )
 
-    def f1(xa, xb):
+    def f1(xa, xb, place, ready):
         return call(
-            functools.partial(f1_kernel, dims),
-            [meta, xa, xb, vm, vi, vf, pos] + a_all + b_all,
+            functools.partial(f1_kernel, dims, ready),
+            [meta, xa, xb, vm, vi, vf, place] + a_all + b_all,
             [((L, D), F32), ((L, D), F32), ((8, D), F32), ((L, D), F32), ((L, H), F32),
              ((L, H), BF16)] + [((L, D), BF16)] * 4
             + [((2 * L, D), BF16), ((heads, L, L), F32), ((L, D), BF16), ((L, D), F32), ((L, D), F32)],
@@ -794,13 +794,13 @@
     down_pairs = [(b, a) for a, b in up_pairs]
 
     def forward(xa, xb):
-        front = f1(xa, xb)
+        front = f1(xa, xb, pos, False)
         stats = norm_group(front[2])
         return front, f2(front[0], front[1], stats)
 
-    _, rear = forward(x0, x0)
+    front, rear = forward(x0, x0)
     middle = permute(rear[0], up_pairs)
-    front = f1(x0, middle)
+    front = f1(x0, middle, front[10], True)
     (s2, filt, stats, s1, before0, a0, qu, qv, k, v, rel, probs, ctx, gin, gsig) = front
     rear, part1 = turn(x0, s2, filt, norm_group(stats))
     made, s3, before1, s4, bn = rear

time: 265 us -> 266 us (level)
  no operation moved by 1% of the time
where the time goes in v5:
time: 266 us; the launch traced here: 263 us
  starting transfers between devices  90.7 us (34%)
  Pallas kernels  82.1 us (31%)
  waiting for transfers between devices  63.6 us (24%)
  other arithmetic  19.9 us (7%)
  local copies, waits for them, and re-layouts  4.55 us (2%)
    ppermute x49, starting transfers between devices, permute(): return lax.ppermute(value, ('pipe', 'dp', 'tensor'), pairs)  90.7 us
    pallas_call x12, Pallas kernels, call(): pl.pallas_call(kernel, out_shape=[jax.ShapeDtypeStruct(s, d) for s, d in...  82.1 us
    ppermute x49, waiting for transfers between devices, permute(): return lax.ppermute(value, ('pipe', 'dp', 'tensor'), pairs)  63.6 us
    concatenate x6, other arithmetic, spread(): held = jnp.concatenate([held, permute(held, bit_pairs(b))], axis=0)  7.19 us
    convert_element_type x6, other arithmetic, round_of(): return got + [permute(total.astype(BF16), bit_pairs(bit))]  5.77 us
  transfers between devices with their start and end apart: 49, of which 29 were waited for; matrix products, arithmetic and copies ran while one was open for 8% of the time, Pallas kernels for 12%

profile of v5, /device:TPU:1, one launch (start us, length us, event | category | flops | bytes accessed | tf_op | source)
XLA Modules:
  0.0 263.0 jit_solution(14793900341887805086)
XLA Ops:
  0.6 5.6 %collective-permute-start.9 = (bf16[8,128,128]{2,1,0:T(8,128)(2,1)}, bf16[8,128,128]{2,1,0:T(8,128)(2,1)S(1)}, u32[]{:S(2)}, u32[]{:S(2)}) collective-permute-start(bf16[8,128,128]{2,1,0:T(8,128)(2,1)} %bitcast.115), channel_id=1, source_target_pairs={{0,0},{1,1},{2,2},{3,3},{4,4},{5,5},{6,6},{7,7},{8,16},{9,17},{10,... | collective-permute-start | bytes 786440 | tf_op jit(solution)/shard_map/ppermute | solution.py:582
  10.8 4.5 %collective-permute-start.18 = (bf16[256,512]{1,0:T(8,128)(2,1)S(1)}, bf16[256,512]{1,0:T(8,128)(2,1)S(1)}, u32[]{:S(2)}, u32[]{:S(2)}) collective-permute-start(bf16[256,512]{1,0:T(8,128)(2,1)S(1)} %bitcast.103), channel_id=1, source_target_pairs={{0,0},{1,1},{2,2},{3,3},{4,4},{5,5},{6,6},{7,7},{8,16},{9,17},{10,... | collective-permute-start | bytes 786440 | tf_op jit(solution)/shard_map/ppermute | solution.py:582
  22.0 3.2 %collective-permute-done.18 = bf16[256,512]{1,0:T(8,128)(2,1)S(1)} collective-permute-done((bf16[256,512]{1,0:T(8,128)(2,1)S(1)}, bf16[256,512]{1,0:T(8,128)(2,1)S(1)}, u32[]{:S(2)}, u32[]{:S(2)}) %collective-permute-start.18) | collective-permute-done | bytes 262176 | tf_op jit(solution)/shard_map/ppermute | solution.py:582
  34.4 4.3 %collective-permute-done.11 = bf16[2,8,128,128]{3,2,1,0:T(8,128)(2,1)} collective-permute-done((bf16[2,8,128,128]{3,2,1,0:T(8,128)(2,1)S(1)}, bf16[2,8,128,128]{3,2,1,0:T(8,128)(2,1)}, u32[]{:S(2)}, u32[]{:S(2)}) %collective-permute-start.11) | collective-permute-done | bytes 524320 | tf_op jit(solution)/shard_map/ppermute | solution.py:582
  50.3 4.9 %collective-permute-start = (bf16[48,512]{1,0:T(8,128)(2,1)S(1)}, bf16[48,512]{1,0:T(8,128)(2,1)S(1)}, u32[]{:S(2)}, u32[]{:S(2)}) collective-permute-start(bf16[48,512]{1,0:T(8,128)(2,1)S(1)} %get-tuple-element.194), channel_id=1, source_target_pairs={{0,0},{1,16},{2,2},{3,18},{4,4},{5,20},{6,6},{7,22},{8,17},{9,1},{... | collective-permute-start | bytes 147464 | tf_op jit(solution)/shard_map/ppermute | solution.py:582
  55.2 5.8 %collective-permute-done = bf16[48,512]{1,0:T(8,128)(2,1)S(1)} collective-permute-done((bf16[48,512]{1,0:T(8,128)(2,1)S(1)}, bf16[48,512]{1,0:T(8,128)(2,1)S(1)}, u32[]{:S(2)}, u32[]{:S(2)}) %collective-permute-start) | collective-permute-done | bytes 49184 | tf_op jit(solution)/shard_map/ppermute | solution.py:582
  73.0 9.6 %layer_front.2 = (f32[128,512]{1,0:T(8,128)S(1)}, f32[128,512]{1,0:T(8,128)S(1)}, f32[8,512]{1,0:T(8,128)S(1)}, f32[128,512]{1,0:T(8,128)}, f32[128,2048]{1,0:T(...) custom-call(s32[4]{0:T(128)S(1)} %pad_add_fusion.meta, ...), custom_call_target="tpu_custom_call" | custom-call | flops 1006632960 | bytes 9355280 | tf_op jit(solution)/shard_map/layer_front/pallas_call | solution.py:569
  82.5 5.7 %collective-permute-start.17 = (f32[1,8,512]{2,1,0:T(8,128)S(1)}, f32[1,8,512]{2,1,0:T(8,128)S(1)}, u32[]{:S(2)}, u32[]{:S(2)}) collective-permute-start(f32[1,8,512]{2,1,0:T(8,128)S(1)} %bitcast.82), channel_id=1, source_target_pairs={{0,5},{1,4},{2,7},{3,6},{4,1},{5,0},{6,3},{7,2},{8,13},{9,12},{10,... | collective-permute-start | bytes 49160 | tf_op jit(solution)/shard_map/ppermute | solution.py:582
  90.9 4.9 %layer_rear.1 = (bf16[128,512]{1,0:T(8,128)(2,1)S(1)}, f32[128,512]{1,0:T(8,128)}, f32[128,2048]{1,0:T(8,128)}, f32[128,512]{1,0:T(8,128)}, f32[8,512]{1,0:T(8,128)}) custom-call(s32[4]{0:T(128)S(1)} %pad_add_fusion.meta, f32[128,512]{1,0:T(8,128)S(1)} %get-tuple-element.93.s2_ref, f32[128,512]{1,0:T(8,128)S(1)} %get-tuple-element.94.filt_ref, ...), custom_call_target="tpu_custom_call" | custom-call | flops 603979776 | bytes 9158672 | tf_op jit(solution)/shard_map/layer_rear/pallas_call | solution.py:569
  100.1 8.8 %layer_front.3 = (f32[128,512]{1,0:T(8,128)S(1)}, f32[128,512]{1,0:T(8,128)S(1)}, f32[8,512]{1,0:T(8,128)S(1)}, f32[128,512]{1,0:T(8,128)S(1)}, f32[128,2048]{1,...) custom-call(s32[4]{0:T(128)S(1)} %pad_add_fusion.meta, ...), custom_call_target="tpu_custom_call" | custom-call | flops 1006632960 | bytes 9355280 | tf_op jit(solution)/shard_map/layer_front/pallas_call | solution.py:569
  116.0 6.9 %layer_turn.1 = (bf16[128,512]{1,0:T(8,128)(2,1)S(1)}, f32[128,512]{1,0:T(8,128)S(1)}, f32[128,2048]{1,0:T(8,128)S(1)}, f32[128,512]{1,0:T(8,128)S(1)}, f32[8,51...) custom-call(s32[4]{0:T(128)S(1)} %pad_add_fusion.meta, ...), custom_call_target="tpu_custom_call" | custom-call | flops 1207959552 | bytes 9289744 | tf_op jit(solution)/shard_map/layer_turn/pallas_call | solution.py:569
  127.9 24.2 %back_whole.1 = (f32[128,512]{1,0:T(8,128)}, bf16[128,512]{1,0:T(8,128)(2,1)}, bf16[128,512]{1,0:T(8,128)(2,1)}, bf16[128,512]{1,0:T(8,128)(2,1)}, bf16[128,512]...) custom-call(s32[4]{0:T(128)S(1)} %pad_add_fusion.meta, ...), custom_call_target="tpu_custom_call" | custom-call | flops 1610612736 | bytes 13336592 | tf_op jit(solution)/shard_map/back_whole/pallas_call | solution.py:569
  153.4 6.8 %collective-permute-done.31.gb_ref = bf16[128,512]{1,0:T(8,128)(2,1)S(1)} collective-permute-done((bf16[128,512]{1,0:T(8,128)(2,1)S(1)}, bf16[128,512]{1,0:T(8,128)(2,1)S(1)}, u32[]{:S(2)}, u32[]{:S(2)}) %collective-permute-start.31) | collective-permute-done | bytes 131104 | tf_op jit(solution)/shard_map/ppermute | solution.py:582
  160.2 4.6 %back_rear.1 = (f32[128,512]{1,0:T(8,128)S(1)}, f32[128,512]{1,0:T(8,128)S(1)}, f32[8,512]{1,0:T(8,128)S(1)}, bf16[128,512]{1,0:T(8,128)(2,1)S(1)}, bf16[128,204...) custom-call(s32[4]{0:T(128)S(1)} %pad_add_fusion.meta, ...), custom_call_target="tpu_custom_call" | custom-call | flops 603979776 | bytes 10616848 | tf_op jit(solution)/shard_map/back_rear/pallas_call | solution.py:569
  171.7 10.3 %back_front.1 = (f32[128,512]{1,0:T(8,128)S(1)}, bf16[128,512]{1,0:T(8,128)(2,1)S(1)}, bf16[128,512]{1,0:T(8,128)(2,1)S(1)}, bf16[128,512]{1,0:T(8,128)(2,1)S(1)...) custom-call(s32[4]{0:T(128)S(1)} %pad_add_fusion.meta, ...), custom_call_target="tpu_custom_call" | custom-call | flops 1073741824 | bytes 7569424 | tf_op jit(solution)/shard_map/back_front/pallas_call | solution.py:569
  182.0 5.3 %collective-permute-done.35 = bf16[4,256,512]{2,1,0:T(8,128)(2,1)S(1)} collective-permute-done((bf16[4,256,512]{2,1,0:T(8,128)(2,1)S(1)}, bf16[4,256,512]{2,1,0:T(8,128)(2,1)S(1)}, u32[]{:S(2)}, u32[]{:S(2)}) %collective-permute-start.35) | collective-permute-done | bytes 1048608 | tf_op jit(solution)/shard_map/ppermute | solution.py:582
  190.4 4.1 %back_first.1 = (bf16[128,512]{1,0:T(8,128)(2,1)S(1)}, bf16[128,512]{1,0:T(8,128)(2,1)S(1)}, bf16[128,2048]{1,0:T(8,128)(2,1)S(1)}, f32[8,512]{1,0:T(8,128)S(1)}, f32[1,2048]{1,0:T(1,128)S(1)}) custom-call(s32[4]{0:T(128)S(1)} %pad_add_fusion.meta, f32[128,512]{1,0:T(8,128)S(1)} %get-tuple-element.147.ds1_ref, bf16[128,512]{1,0:T(8,128)(2,1)S(1)} %bitcast.73, ...), custom_call_target="tpu_custom_call" | custom-call | flops 536870912 | bytes 6062096 | tf_op jit(solution)/shard_map/back_first/pallas_call | solution.py:569
  198.8 9.1 %collective-permute-start.36 = (bf16[32,512]{1,0:T(8,128)(2,1)S(1)}, bf16[32,512]{1,0:T(8,128)(2,1)S(1)}, u32[]{:S(2)}, u32[]{:S(2)}) collective-permute-start(bf16[32,512]{1,0:T(8,128)(2,1)S(1)} %get-tuple-element.190), channel_id=1, source_target_pairs={{0,0},{16,1},{2,2},{18,3},{4,4},{20,5},{6,6},{22,7},{17,8},{1,9},{... | collective-permute-start | bytes 98312 | tf_op jit(solution)/shard_map/ppermute | solution.py:582
  214.6 5.0 %collective-permute-done.43 = bf16[4,272,512]{2,1,0:T(8,128)(2,1)} collective-permute-done((bf16[4,272,512]{2,1,0:T(8,128)(2,1)}, bf16[4,272,512]{2,1,0:T(8,128)(2,1)}, u32[]{:S(2)}, u32[]{:S(2)}) %collective-permute-start.43) | collective-permute-done | bytes 1114144 | tf_op jit(solution)/shard_map/ppermute | solution.py:582
  221.9 9.8 %collective-permute-start.46 = (bf16[256,512]{1,0:T(8,128)(2,1)S(1)}, bf16[256,512]{1,0:T(8,128)(2,1)S(1)}, u32[]{:S(2)}, u32[]{:S(2)}) collective-permute-start(bf16[256,512]{1,0:T(8,128)(2,1)S(1)} %fusion.2), channel_id=1, source_target_pairs={{0,0},{1,1},{2,2},{3,3},{4,4},{5,5},{6,6},{7,7},{8,16},{9,17},{10,... | collective-permute-start | bytes 786440 | tf_op jit(solution)/shard_map/ppermute | solution.py:582
  232.9 4.5 %collective-permute-done.46 = bf16[256,512]{1,0:T(8,128)(2,1)S(1)} collective-permute-done((bf16[256,512]{1,0:T(8,128)(2,1)S(1)}, bf16[256,512]{1,0:T(8,128)(2,1)S(1)}, u32[]{:S(2)}, u32[]{:S(2)}) %collective-permute-start.46) | collective-permute-done | bytes 262176 | tf_op jit(solution)/shard_map/ppermute | solution.py:582
  241.7 5.1 %collective-permute-start.41 = (bf16[8,128,128]{2,1,0:T(8,128)(2,1)S(1)}, bf16[8,128,128]{2,1,0:T(8,128)(2,1)S(1)}, u32[]{:S(2)}, u32[]{:S(2)}) collective-permute-start(bf16[8,128,128]{2,1,0:T(8,128)(2,1)S(1)} %fusion.1), channel_id=1, source_target_pairs={{0,0},{1,1},{2,2},{3,3},{4,4},{5,5},{6,6},{7,7},{8,16},{9,17},{10,... | collective-permute-start | bytes 786440 | tf_op jit(solution)/shard_map/ppermute | solution.py:582
  247.9 3.6 %collective-permute-start.48 = (bf16[272,512]{1,0:T(8,128)(2,1)S(1)}, bf16[272,512]{1,0:T(8,128)(2,1)S(1)}, u32[]{:S(2)}, u32[]{:S(2)}) collective-permute-start(bf16[272,512]{1,0:T(8,128)(2,1)S(1)} %fusion), channel_id=1, source_target_pairs={{0,0},{1,1},{2,2},{3,3},{4,4},{5,5},{6,6},{7,7},{8,16},{9,17},{10,... | collective-permute-start | bytes 835592 | tf_op jit(solution)/shard_map/ppermute | solution.py:582
  254.6 5.1 %collective-permute-done.48 = bf16[272,512]{1,0:T(8,128)(2,1)S(1)} collective-permute-done((bf16[272,512]{1,0:T(8,128)(2,1)S(1)}, bf16[272,512]{1,0:T(8,128)(2,1)S(1)}, u32[]{:S(2)}, u32[]{:S(2)}) %collective-permute-start.48) | collective-permute-done | bytes 278560 | tf_op jit(solution)/shard_map/ppermute | solution.py:582
  (156 shorter events, 99.2 us)
Async XLA Ops:
  0.6 14.7 %collective-permute-start.9 = (bf16[8,128,128]{2,1,0:T(8,128)(2,1)}, bf16[8,128,128]{2,1,0:T(8,128)(2,1)S(1)}, u32[]{:S(2)}, u32[]{:S(2)}) collective-permute-start(bf16[8,128,128]{2,1,0:T(8,128)(2,1)} %bitcast.115), channel_id=1, source_target_pairs={{0,0},{1,1},{2,2},{3,3},{4,4},{5,5},{6,6},{7,7},{8,16},{9,17},{10,... | collective-permute-start | bytes 786440 | tf_op jit(solution)/shard_map/ppermute | solution.py:582
  8.9 10.8 %collective-permute-start.3 = (bf16[272,512]{1,0:T(8,128)(2,1)S(1)}, bf16[272,512]{1,0:T(8,128)(2,1)S(1)}, u32[]{:S(2)}, u32[]{:S(2)}) collective-permute-start(bf16[272,512]{1,0:T(8,128)(2,1)S(1)} %pad_maximum_fusion.6), channel_id=1, source_target_pairs={{0,0},{1,1},{2,2},{3,3},{4,4},{5,5},{6,6},{7,7},{8,16},{9,17},{10,... | collective-permute-start | bytes 835592 | tf_op jit(solution)/shard_map/ppermute | solution.py:582
  10.8 14.5 %collective-permute-start.18 = (bf16[256,512]{1,0:T(8,128)(2,1)S(1)}, bf16[256,512]{1,0:T(8,128)(2,1)S(1)}, u32[]{:S(2)}, u32[]{:S(2)}) collective-permute-start(bf16[256,512]{1,0:T(8,128)(2,1)S(1)} %bitcast.103), channel_id=1, source_target_pairs={{0,0},{1,1},{2,2},{3,3},{4,4},{5,5},{6,6},{7,7},{8,16},{9,17},{10,... | collective-permute-start | bytes 786440 | tf_op jit(solution)/shard_map/ppermute | solution.py:582
  15.3 12.2 %collective-permute-start.10 = (bf16[1,8,128,128]{3,2,1,0:T(8,128)(2,1)S(1)}, bf16[1,8,128,128]{3,2,1,0:T(8,128)(2,1)S(1)}, u32[]{:S(2)}, u32[]{:S(2)}) collective-permute-start(bf16[1,8,128,128]{3,2,1,0:T(8,128)(2,1)S(1)} %bitcast.98), channel_id=1, source_target_pairs={{0,2},{1,3},{2,0},{3,1},{4,6},{5,7},{6,4},{7,5},{8,10},{9,11},{10,... | collective-permute-start | bytes 786440 | tf_op jit(solution)/shard_map/ppermute | solution.py:582
  27.7 11.0 %collective-permute-start.11 = (bf16[2,8,128,128]{3,2,1,0:T(8,128)(2,1)S(1)}, bf16[2,8,128,128]{3,2,1,0:T(8,128)(2,1)}, u32[]{:S(2)}, u32[]{:S(2)}) collective-permute-start(bf16[2,8,128,128]{3,2,1,0:T(8,128)(2,1)S(1)} %pad_maximum_fusion.4), channel_id=1, source_target_pairs={{0,4},{1,5},{2,6},{3,7},{4,0},{5,1},{6,2},{7,3},{8,12},{9,13},{10,... | collective-permute-start | bytes 1572872 | tf_op jit(solution)/shard_map/ppermute | solution.py:582
  29.3 12.1 %collective-permute-start.5 = (bf16[2,272,512]{2,1,0:T(8,128)(2,1)}, bf16[2,272,512]{2,1,0:T(8,128)(2,1)}, u32[]{:S(2)}, u32[]{:S(2)}) collective-permute-start(bf16[2,272,512]{2,1,0:T(8,128)(2,1)} %pad_maximum_fusion.3), channel_id=1, source_target_pairs={{0,2},{1,3},{2,0},{3,1},{4,6},{5,7},{6,4},{7,5},{8,10},{9,11},{10,... | collective-permute-start | bytes 1671176 | tf_op jit(solution)/shard_map/ppermute | solution.py:582
  32.8 14.3 %collective-permute-start.20 = (bf16[2,256,512]{2,1,0:T(8,128)(2,1)}, bf16[2,256,512]{2,1,0:T(8,128)(2,1)}, u32[]{:S(2)}, u32[]{:S(2)}) collective-permute-start(bf16[2,256,512]{2,1,0:T(8,128)(2,1)} %pad_maximum_fusion.5), channel_id=1, source_target_pairs={{0,1},{1,0},{2,3},{3,2},{4,5},{5,4},{6,7},{7,6},{8,9},{9,8},{10,11... | collective-permute-start | bytes 1572872 | tf_op jit(solution)/shard_map/ppermute | solution.py:582
  39.8 27.0 %collective-permute-start.12 = (bf16[4,8,128,128]{3,2,1,0:T(8,128)(2,1)S(1)}, bf16[4,8,128,128]{3,2,1,0:T(8,128)(2,1)S(1)}, u32[]{:S(2)}, u32[]{:S(2)}) collective-permute-start(bf16[4,8,128,128]{3,2,1,0:T(8,128)(2,1)S(1)} %pad_maximum_fusion.1.refs_4_.refs_7_.refs_22_.refs_0_.refs_20_), channel_id=1, source_target_pairs={{0,1},{1,0},{2,3},{3,2},{4,5},{5,4},{6,7},{7,6},{8,9},{9,8},{10,11... | collective-permute-start | bytes 3145736 | tf_op jit(solution)/shard_map/ppermute | solution.py:582
  43.6 21.8 %collective-permute-start.6 = (bf16[4,272,512]{2,1,0:T(8,128)(2,1)}, bf16[4,272,512]{2,1,0:T(8,128)(2,1)}, u32[]{:S(2)}, u32[]{:S(2)}) collective-permute-start(bf16[4,272,512]{2,1,0:T(8,128)(2,1)} %pad_maximum_fusion.refs_0_.refs_29_), channel_id=1, source_target_pairs={{0,4},{1,5},{2,6},{3,7},{4,0},{5,1},{6,2},{7,3},{8,12},{9,13},{10,... | collective-permute-start | bytes 3342344 | tf_op jit(solution)/shard_map/ppermute | solution.py:582
  49.2 18.0 %collective-permute-start.21 = (bf16[4,256,512]{2,1,0:T(8,128)(2,1)}, bf16[4,256,512]{2,1,0:T(8,128)(2,1)}, u32[]{:S(2)}, u32[]{:S(2)}) collective-permute-start(bf16[4,256,512]{2,1,0:T(8,128)(2,1)} %pad_maximum_fusion.2.refs_11_.refs_4_), channel_id=1, source_target_pairs={{0,2},{1,3},{2,0},{3,1},{4,6},{5,7},{6,4},{7,5},{8,10},{9,11},{10,... | collective-permute-start | bytes 3145736 | tf_op jit(solution)/shard_map/ppermute | solution.py:582
  50.1 17.3 %collective-permute-start.7 = (bf16[4,272,512]{2,1,0:T(8,128)(2,1)}, bf16[4,272,512]{2,1,0:T(8,128)(2,1)}, u32[]{:S(2)}, u32[]{:S(2)}) collective-permute-start(bf16[4,272,512]{2,1,0:T(8,128)(2,1)} %pad_maximum_fusion.refs_0_.refs_29_), channel_id=1, source_target_pairs={{0,16},{1,17},{2,18},{3,19},{4,20},{5,21},{6,22},{7,23},{8,24},{9,... | collective-permute-start | bytes 3342344 | tf_op jit(solution)/shard_map/ppermute | solution.py:582
  50.3 10.7 %collective-permute-start = (bf16[48,512]{1,0:T(8,128)(2,1)S(1)}, bf16[48,512]{1,0:T(8,128)(2,1)S(1)}, u32[]{:S(2)}, u32[]{:S(2)}) collective-permute-start(bf16[48,512]{1,0:T(8,128)(2,1)S(1)} %get-tuple-element.194), channel_id=1, source_target_pairs={{0,0},{1,16},{2,2},{3,18},{4,4},{5,20},{6,6},{7,22},{8,17},{9,1},{... | collective-permute-start | bytes 147464 | tf_op jit(solution)/shard_map/ppermute | solution.py:582
  67.2 21.4 %collective-permute-start.22 = (bf16[4,256,512]{2,1,0:T(8,128)(2,1)}, bf16[4,256,512]{2,1,0:T(8,128)(2,1)}, u32[]{:S(2)}, u32[]{:S(2)}) collective-permute-start(bf16[4,256,512]{2,1,0:T(8,128)(2,1)} %pad_maximum_fusion.2.refs_11_.refs_4_), channel_id=1, source_target_pairs={{0,16},{1,17},{2,18},{3,19},{4,20},{5,21},{6,22},{7,23},{8,24},{9,... | collective-permute-start | bytes 3145736 | tf_op jit(solution)/shard_map/ppermute | solution.py:582
  67.4 21.2 %collective-permute-start.23 = (bf16[4,256,512]{2,1,0:T(8,128)(2,1)}, bf16[4,256,512]{2,1,0:T(8,128)(2,1)}, u32[]{:S(2)}, u32[]{:S(2)}) collective-permute-start(bf16[4,256,512]{2,1,0:T(8,128)(2,1)} %collective-permute-done.21.refs_12_.refs_5_), channel_id=1, source_target_pairs={{0,16},{1,17},{2,18},{3,19},{4,20},{5,21},{6,22},{7,23},{8,24},{9,... | collective-permute-start | bytes 3145736 | tf_op jit(solution)/shard_map/ppermute | solution.py:582
  166.3 21.0 %collective-permute-start.35 = (bf16[4,256,512]{2,1,0:T(8,128)(2,1)S(1)}, bf16[4,256,512]{2,1,0:T(8,128)(2,1)S(1)}, u32[]{:S(2)}, u32[]{:S(2)}) collective-permute-start(bf16[4,256,512]{2,1,0:T(8,128)(2,1)S(1)} %get-tuple-element.132), channel_id=1, source_target_pairs={{0,2},{1,3},{2,0},{3,1},{4,6},{5,7},{6,4},{7,5},{8,10},{9,11},{10,... | collective-permute-start | bytes 3145736 | tf_op jit(solution)/shard_map/ppermute | solution.py:582
  190.4 20.5 %collective-permute-start.38 = (bf16[4,8,128,128]{3,2,1,0:T(8,128)(2,1)}, bf16[4,8,128,128]{3,2,1,0:T(8,128)(2,1)}, u32[]{:S(2)}, u32[]{:S(2)}) collective-permute-start(bf16[4,8,128,128]{3,2,1,0:T(8,128)(2,1)} %get-tuple-element.150), channel_id=1, source_target_pairs={{0,4},{1,5},{2,6},{3,7},{4,0},{5,1},{6,2},{7,3},{8,12},{9,13},{10,... | collective-permute-start | bytes 3145736 | tf_op jit(solution)/shard_map/ppermute | solution.py:582
  198.8 20.8 %collective-permute-start.43 = (bf16[4,272,512]{2,1,0:T(8,128)(2,1)}, bf16[4,272,512]{2,1,0:T(8,128)(2,1)}, u32[]{:S(2)}, u32[]{:S(2)}) collective-permute-start(bf16[4,272,512]{2,1,0:T(8,128)(2,1)} %get-tuple-element.166), channel_id=1, source_target_pairs={{0,1},{1,0},{2,3},{3,2},{4,5},{5,4},{6,7},{7,6},{8,9},{9,8},{10,11... | collective-permute-start | bytes 3342344 | tf_op jit(solution)/shard_map/ppermute | solution.py:582
  198.8 32.9 %collective-permute-start.36 = (bf16[32,512]{1,0:T(8,128)(2,1)S(1)}, bf16[32,512]{1,0:T(8,128)(2,1)S(1)}, u32[]{:S(2)}, u32[]{:S(2)}) collective-permute-start(bf16[32,512]{1,0:T(8,128)(2,1)S(1)} %get-tuple-element.190), channel_id=1, source_target_pairs={{0,0},{16,1},{2,2},{18,3},{4,4},{20,5},{6,6},{22,7},{17,8},{1,9},{... | collective-permute-start | bytes 98312 | tf_op jit(solution)/shard_map/ppermute | solution.py:582
  207.9 23.8 %collective-permute-start.37 = (bf16[32,512]{1,0:T(8,128)(2,1)S(1)}, bf16[32,512]{1,0:T(8,128)(2,1)S(1)}, u32[]{:S(2)}, u32[]{:S(2)}) collective-permute-start(bf16[32,512]{1,0:T(8,128)(2,1)S(1)} %get-tuple-element.191), channel_id=1, source_target_pairs={{2,0},{18,1},{0,2},{16,3},{6,4},{22,5},{4,6},{20,7},{19,8},{3,9},{... | collective-permute-start | bytes 98312 | tf_op jit(solution)/shard_map/ppermute | solution.py:582
  212.1 19.7 %collective-permute-start.39 = (bf16[2,8,128,128]{3,2,1,0:T(8,128)(2,1)S(1)}, bf16[2,8,128,128]{3,2,1,0:T(8,128)(2,1)S(1)}, u32[]{:S(2)}, u32[]{:S(2)}) collective-permute-start(bf16[2,8,128,128]{3,2,1,0:T(8,128)(2,1)S(1)} %add_convert_fusion.2), channel_id=1, source_target_pairs={{0,2},{1,3},{2,0},{3,1},{4,6},{5,7},{6,4},{7,5},{8,10},{9,11},{10,... | collective-permute-start | bytes 1572872 | tf_op jit(solution)/shard_map/ppermute | solution.py:582
  220.8 16.6 %collective-permute-start.44 = (bf16[2,272,512]{2,1,0:T(8,128)(2,1)S(1)}, bf16[2,272,512]{2,1,0:T(8,128)(2,1)S(1)}, u32[]{:S(2)}, u32[]{:S(2)}) collective-permute-start(bf16[2,272,512]{2,1,0:T(8,128)(2,1)S(1)} %add_convert_fusion), channel_id=1, source_target_pairs={{0,4},{1,5},{2,6},{3,7},{4,0},{5,1},{6,2},{7,3},{8,12},{9,13},{10,... | collective-permute-start | bytes 1671176 | tf_op jit(solution)/shard_map/ppermute | solution.py:582
  221.9 15.5 %collective-permute-start.46 = (bf16[256,512]{1,0:T(8,128)(2,1)S(1)}, bf16[256,512]{1,0:T(8,128)(2,1)S(1)}, u32[]{:S(2)}, u32[]{:S(2)}) collective-permute-start(bf16[256,512]{1,0:T(8,128)(2,1)S(1)} %fusion.2), channel_id=1, source_target_pairs={{0,0},{1,1},{2,2},{3,3},{4,4},{5,5},{6,6},{7,7},{8,16},{9,17},{10,... | collective-permute-start | bytes 786440 | tf_op jit(solution)/shard_map/ppermute | solution.py:582
  241.7 12.0 %collective-permute-start.41 = (bf16[8,128,128]{2,1,0:T(8,128)(2,1)S(1)}, bf16[8,128,128]{2,1,0:T(8,128)(2,1)S(1)}, u32[]{:S(2)}, u32[]{:S(2)}) collective-permute-start(bf16[8,128,128]{2,1,0:T(8,128)(2,1)S(1)} %fusion.1), channel_id=1, source_target_pairs={{0,0},{1,1},{2,2},{3,3},{4,4},{5,5},{6,6},{7,7},{8,16},{9,17},{10,... | collective-permute-start | bytes 786440 | tf_op jit(solution)/shard_map/ppermute | solution.py:582
  247.9 11.8 %collective-permute-start.48 = (bf16[272,512]{1,0:T(8,128)(2,1)S(1)}, bf16[272,512]{1,0:T(8,128)(2,1)S(1)}, u32[]{:S(2)}, u32[]{:S(2)}) collective-permute-start(bf16[272,512]{1,0:T(8,128)(2,1)S(1)} %fusion), channel_id=1, source_target_pairs={{0,0},{1,1},{2,2},{3,3},{4,4},{5,5},{6,6},{7,7},{8,16},{9,17},{10,... | collective-permute-start | bytes 835592 | tf_op jit(solution)/shard_map/ppermute | solution.py:582
  (34 other events, 195.0 us)
